TPU v7x, 128 devices: a whole 4x4x4 slice. The times are simulated.
128 devices in a mesh: row: 16 (over z, x), col: 8 (over y, core).
Axes of the slice: x: 4, y: 4, z: 4, core: 2. Of those that a mesh axis runs over, the one named last changes fastest.
Arguments:
- iterate: float32 [16, 2048, 2048], P(None, 'row', 'col'), may hold values from -6 to 6
- direction: float32 [16, 2048, 2048], P(None, 'row', 'col'), may hold values from -6 to 6
- conductance: float32 [2048, 2048], P('row', 'col'), may hold values from 0.1 to 10
- ground: int32 [2048, 2048], P('row', 'col'), may hold values 0 or 1
- local_patch: int32 [2048, 2048], P('row', 'col'), may hold values from 0 to 2047, as said below
- tile_patches: int32 [16, 8, 2048], P('row', 'col'), may hold values from 0 to 65535, as said below
- sources: int32 [16], replicated, may hold values from 0 to 65535, as said below
Outputs:
- new_iterate: float32 [16, 2048, 2048], P(None, 'row', 'col')
- new_direction: float32 [16, 2048, 2048], P(None, 'row', 'col')
- migration: float32 [16, 65536], P(None, ('row', 'col'))
Inputs may be any that keep to these rules, and one draw needn't show every extreme that they name: `local_patch`: each aligned 4 x 4 block of cells holds one value, and the blocks of one tile take each value once. `tile_patches`: in every tile's list, entries o * 16 to (o + 1) * 16 - 1 are ids from o * 512 to (o + 1) * 512 - 1, where o runs over the devices in row-major order of (row, col); some list holds 0 and some holds the largest id. Each source patch appears in some tile's list; 0 and the largest id are among the sources.
All inputs are finite; a program needn't handle non-finite values. No bound on the sum of `ground` on one device may be relied on, other than what follows from the above.
Results may differ from a plain program's by a relative error of at most 0.0003.
Values sent between devices are 32-bit elements; how exact they have to be, the bound alone decides.
No kernel may reach another device: no remote copies, remote signals or barrier semaphores. Data moves between devices by JAX's collectives and lax.ppermute only.
A program may use at most 128 MiB of HBM per device.

v0:
```python
import jax
import jax.numpy as jnp
from jax import lax
from jax.sharding import PartitionSpec as P

PB = 4
PATCH_DEV = 512


SOURCE_AMPS = 4.0
GROUND_LEAK = 2.0
NEIGHBOURS = ((2, 1), (0, 1), (1, 2), (1, 0))


def with_halo(cells, sides, width):
    for axis, dim in sides:
        count = lax.axis_size(axis)
        ends = count - 1
        head = lax.slice_in_dim(cells, 0, width, axis=dim)
        tail = lax.slice_in_dim(cells, cells.shape[dim] - width, cells.shape[dim], axis=dim)
        cells = jnp.concatenate(
            [
                lax.ppermute(tail, axis, [(i, (i + 1) % count) for i in range(ends)]),
                cells,
                lax.ppermute(head, axis, [((i + 1) % count, i) for i in range(ends)]),
            ],
            axis=dim,
        )
    return cells


def edge_terms(field_pad, cond_pad, magnitude):
    height = field_pad.shape[1] - 2
    breadth = field_pad.shape[2] - 2
    centre = field_pad[:, 1:-1, 1:-1]
    middle = cond_pad[1:-1, 1:-1]
    summed = jnp.zeros(centre.shape, jnp.float32)
    for row_start, col_start in NEIGHBOURS:
        other = field_pad[:, row_start : row_start + height, col_start : col_start + breadth]
        cond_other = cond_pad[row_start : row_start + height, col_start : col_start + breadth]
        edges = jnp.where(cond_other > 0, 0.5 * (middle + cond_other), 0.0)
        change = centre - other
        if magnitude:
            change = jnp.abs(change)
        summed = summed + edges * change
    return summed


def operate(field_pad, cond_pad, grounded):
    centre = field_pad[:, 1:-1, 1:-1]
    return edge_terms(field_pad, cond_pad, False) + GROUND_LEAK * grounded * centre


def products(left, right):
    return jnp.einsum("kab,lab->kl", left, right, precision=lax.Precision.HIGHEST)


def combine(fields, matrix):
    return jnp.einsum("kab,kl->lab", fields, matrix, precision=lax.Precision.HIGHEST)


def on_device(iterate, direction, conductance, ground, local_patch, tile_patches, sources):
    fields = iterate.shape[0]
    height = iterate.shape[1]
    breadth = iterate.shape[2]
    block_rows = height // PB
    block_cols = breadth // PB
    owned_list = tile_patches.reshape(-1)
    local_count = owned_list.shape[0]
    block_ids = local_patch[::PB, ::PB]
    block_patch = owned_list[block_ids]
    patch_of_cell = jnp.broadcast_to(
        block_patch[:, None, :, None], (block_rows, PB, block_cols, PB)
    ).reshape(height, breadth)
    source = SOURCE_AMPS * (patch_of_cell[None] == sources[:, None, None]).astype(jnp.float32)
    stacked = jnp.concatenate([iterate, direction, conductance[None]], axis=0)
    padded = with_halo(stacked, (("row", 1), ("col", 2)), 1)
    iter_pad = padded[:fields]
    dir_pad = padded[fields : 2 * fields]
    cond_pad = padded[2 * fields]
    grounded = ground.astype(jnp.float32)
    residual = source - operate(iter_pad, cond_pad, grounded)
    image = operate(dir_pad, cond_pad, grounded)
    curvature, projection = lax.psum(
        (products(direction, image), products(direction, residual)), ("row", "col")
    )
    factor = jnp.linalg.cholesky(curvature)
    alpha = jax.scipy.linalg.cho_solve((factor, True), projection)
    new_residual = residual - combine(image, alpha)
    cross = lax.psum(products(image, new_residual), ("row", "col"))
    beta = -jax.scipy.linalg.cho_solve((factor, True), cross)
    new_iterate = iterate + combine(direction, alpha)
    new_direction = new_residual + combine(direction, beta)
    new_pad = with_halo(new_iterate, (("row", 1), ("col", 2)), 1)
    current = 0.5 * edge_terms(new_pad, cond_pad, True)
    block_sums = (
        current.reshape(fields, block_rows, PB, block_cols, PB).sum(axis=(2, 4)).reshape(fields, -1)
    )
    inverse = (
        jnp.zeros((local_count,), jnp.int32)
        .at[block_ids.reshape(-1)]
        .set(jnp.arange(local_count, dtype=jnp.int32))
    )
    tile_sums = block_sums[:, inverse].T
    devices = lax.axis_size("row") * lax.axis_size("col")
    spread = jax.ops.segment_sum(tile_sums, owned_list, num_segments=PATCH_DEV * devices).T
    migration = lax.psum_scatter(spread, ("row", "col"), scatter_dimension=1, tiled=True)
    return (new_iterate, new_direction, migration)


def solution(mesh):
    in_specs = (
        P(None, "row", "col"),
        P(None, "row", "col"),
        P("row", "col"),
        P("row", "col"),
        P("row", "col"),
        P("row", "col", None),
        P(),
    )
    out_specs = (P(None, "row", "col"), P(None, "row", "col"), P(None, ("row", "col")))
    return jax.shard_map(
        on_device, mesh=mesh, in_specs=in_specs, out_specs=out_specs, check_vma=False
    )
```

profile of v0, /device:TPU:1, one launch (start us, length us, event | category | flops | bytes accessed | tf_op | source)
XLA Modules:
  0.0 967.7 jit_solution(5025161376271603551)
XLA Ops:
  8.2 4.3 copy_dynamic-update-slice_fusion
  15.1 4.1 dynamic-update-slice.5
  20.0 3.9 collective-permute-start
  31.5 3.2 fusion.64
  40.8 5.2 collective-permute-start.2
  48.2 11.8 %gather_fusion = s32[2048]{0:T(1024)S(1)} fusion(s32[2048]{0:T(1024)S(1)} %bitcast.55, s32[2048]{0:T(1024)S(1)} %broadcast_clamp_fusion), kind=kCustom, calls=%fused_computation | custom fusion | bytes 24576 | tf_op jit(solution)/shard_map/gather | solution.py:71
  62.7 4.9 eq.15
  67.6 3.1 copy.59
  76.9 8.2 fusion.33
  85.1 3.5 fusion.48
  88.7 9.5 fusion.22
  99.6 3.5 fusion.45
  103.1 68.2 %all-reduce = (f32[16,16]{0,1:T(8,128)S(1)}, f32[16,16]{0,1:T(8,128)S(1)}) all-reduce(f32[16,16]{0,1:T(8,128)S(1)} %fusion.45, f32[16,16]{0,1:T(8,128)S(1)} %fusion.48), channel_id=1, replica_groups=mesh['row'=16,'col'=8] {'row','col'}, use_global_device_ids=true, to_apply=%region_3.4 | all-reduce | flops 512 | bytes 4096 | tf_op jit(solution)/shard_map/psum | solution.py:84
  175.8 5.5 copy_add_fusion
  186.1 8.2 scatter_custom_fusion
  200.0 3.2 collective-permute-start.7
  210.7 9.6 fusion.6
  220.4 9.7 copy.85
  230.1 10.1 %reduce_sum.9 = f32[16,32,64]{0,2,1:T(8,128)S(1)} reduce(f32[16,32,4,64,4]{0,4,3,2,1:T(4,128)} %bitcast.58, f32[]{:T(128)} %constant.54.clone.1), dimensions={2,4}, to_apply=%region_5.7 | reduce | flops 491520 | bytes 2228228 | tf_op jit(solution)/shard_map/reduce_sum | solution.py:97
  240.2 30.9 %scatter_custom_fusion.1 = f32[65536,16]{1,0:T(8,128)} fusion(s32[2048]{0:T(1024)S(1)} %bitcast.56, f32[]{:T(128)} %constant.54.clone.1, f32[16,2048]{0,1:T(8,128)S(1)} %bitcast.60, s32[2048]{0:T(1024)} %fusion.54), kind=kCustom, calls=%fused_computation.4 | custom fusion | flops 32768 | bytes 4194816 | tf_op jit(solution)/shard_map/scatter-add | solution.py:106
  271.1 4.3 copy.86
  281.4 69.0 %psum.23 = f32[16,16]{1,0:T(8,128)S(1)} all-reduce(f32[16,16]{1,0:T(8,128)S(1)} %convolution_bitcast_fusion), channel_id=1, replica_groups=mesh['row'=16,'col'=8] {'row','col'}, use_global_device_ids=true, to_apply=%region_4.6 | all-reduce | flops 256 | bytes 2048 | tf_op jit(solution)/shard_map/psum | solution.py:90
  350.7 4.5 convolution_add_fusion
  357.7 601.3 %reduce-scatter.2.cloned.1.call-done = f32[16,512]{0,1:T(8,128)} async-done(((f32[16,65536]{0,1:T(8,128)}), f32[16,512]{0,1:T(8,128)}) %reduce-scatter.2.cloned.1.call-update) | async-done | bytes 32784 | tf_op jit(solution)/shard_map/reduce_scatter | solution.py:107
  (88 shorter events, 63.3 us)
Async XLA Ops:
  7.2 951.8 %reduce-scatter.2.cloned.1.call-start = ((), (), s32[]{:S(2)}) async-start(), calls=%async_computation.1 | async-start | bytes 33816576 | tf_op jit(solution)/shard_map/reduce_scatter | solution.py:107
  8.2 4.3 copy-start.1
  12.5 13.9 %copy-start.13 = (s32[128,256]{1,0:T(8,128)S(1)}, s32[128,256]{1,0:T(8,128)}, u32[]{:S(2)}) copy-start(s32[128,256]{1,0:T(8,128)} %param.12) | copy-start | bytes 393220
  20.0 6.6 collective-permute-start
  23.9 4.7 collective-permute-start.1
  34.7 13.5 %copy-start = (s32[1,1,2048]{2,1,0:T(1,128)S(1)}, s32[1,1,2048]{2,1,0:T(1,128)}, u32[]{:S(2)}) copy-start(s32[1,1,2048]{2,1,0:T(1,128)} %param.14) | copy-start | bytes 24580
  40.8 29.9 %collective-permute-start.2 = (f32[33,130,1]{1,2,0:T(1,128)S(1)}, f32[33,130,1]{1,2,0:T(1,128)S(1)}, u32[]{:S(2)}, u32[]{:S(2)}) collective-permute-start(f32[33,130,1]{1,2,0:T(1,128)S(1)} %copy.56), channel_id=1, source_target_pairs={{0,1},{1,2},{2,3},{3,4},{4,5},{5,6},{6,7},{8,9},{9,10},{10,11},{11... | collective-permute-start | bytes 51488 | tf_op jit(solution)/shard_map/ppermute | solution.py:23
  46.0 21.6 %collective-permute-start.3 = (f32[33,130,1]{1,2,0:T(1,128)S(1)}, f32[33,130,1]{1,2,0:T(1,128)S(1)}, u32[]{:S(2)}, u32[]{:S(2)}) collective-permute-start(f32[33,130,1]{1,2,0:T(1,128)S(1)} %copy.57), channel_id=1, source_target_pairs={{1,0},{2,1},{3,2},{4,3},{5,4},{6,5},{7,6},{9,8},{10,9},{11,10},{12... | collective-permute-start | bytes 51488 | tf_op jit(solution)/shard_map/ppermute | solution.py:25
  73.7 2.6 copy-start.2
  73.7 3.2 copy-start.3
  76.2 12.4 %copy-start.11 = (f32[128,256]{1,0:T(8,128)}, f32[128,256]{1,0:T(8,128)S(1)}, u32[]{:S(2)}) copy-start(f32[128,256]{1,0:T(8,128)S(1)} %get-tuple-element.25) | copy-start | bytes 393220
  76.2 12.4 %copy-start.12 = (f32[128,256]{1,0:T(8,128)}, f32[128,256]{1,0:T(8,128)S(1)}, u32[]{:S(2)}) copy-start(f32[128,256]{1,0:T(8,128)S(1)} %get-tuple-element.26) | copy-start | bytes 393220
  85.1 3.6 copy-start.5
  85.1 3.6 copy-start.7
  85.1 3.6 copy-start.14
  98.3 1.4 copy-start.8
  181.3 1.3 copy-start.4
  182.7 11.7 %collective-permute-start.5 = (f32[16,1,256]{2,0,1:T(8,128)S(1)}, f32[16,1,256]{2,0,1:T(8,128)S(1)}, u32[]{:S(2)}, u32[]{:S(2)}) collective-permute-start(f32[16,1,256]{2,0,1:T(8,128)S(1)} %get-tuple-element.21), channel_id=1, source_target_pairs={{0,8},{8,16},{16,24},{24,32},{32,40},{40,48},{48,56},{56,64},{64,7... | collective-permute-start | bytes 49160 | tf_op jit(solution)/shard_map/ppermute | solution.py:23
  184.8 9.6 collective-permute-start.4
  200.0 9.1 collective-permute-start.7
  203.2 5.1 collective-permute-start.6
  271.1 4.3 copy-start.6
  271.1 4.3 copy-start.9
  277.3 1.3 copy-start.10
Sparse Core Ops, SparseCore 0:
  271.2 687.7 reduce-scatter.1
where the time goes:
time: 979 us; the launch traced here: 968 us
  waiting for transfers between devices  606 us (62%)
  blocking collectives  137 us (14%)
  local copies, waits for them, and re-layouts  86.3 us (9%)
  other arithmetic  80.2 us (8%)
  matrix products  22.4 us (2%)
  starting transfers between devices  21.1 us (2%)
  between operations  14.7 us (2%)
    reduce_scatter x1, waiting for transfers between devices, on_device(): lax.psum_scatter(spread, ('row', 'col'), scatter_dimension=1, tiled=True)  601 us
    psum x1, blocking collectives, on_device(): cross = lax.psum(products(image, new_residual), ('row', 'col'))  69 us
    psum x1, blocking collectives, on_device(): lax.psum((products(direction, image), products(direction, residual)), ('r...  68.2 us
    scatter-add x1, other arithmetic, on_device(): jax.ops.segment_sum(tile_sums, owned_list, num_segments=PATCH_DEV * devices)  30.9 us
    unnamed x36, local copies, waits for them, and re-layouts  20 us
  transfers between devices with their start and end apart: 9, of which 3 were waited for; matrix products, arithmetic and copies ran while one was open for 5% of the time, Pallas kernels for 0%

commit v1 on v0

v1 whole, which is shorter than its diff:
```python
import jax
import jax.numpy as jnp
from jax import lax
from jax.experimental import pallas as pl
from jax.experimental.pallas import tpu as pltpu
from jax.sharding import PartitionSpec as P

K = 16
CR = 128
CC = 256
PATCH_DEV = 512
DEVICES = 128
SLOTS = 16
SOURCE_AMPS = 4.0
GROUND_LEAK = 2.0
AXES = ("row", "col")
F32 = jnp.float32
BF16 = jnp.bfloat16
VMEM_BYTES = 30 * 1024 * 1024


def iota(shape, dim):
    return lax.broadcasted_iota(jnp.int32, shape, dim)


def dot(a, b, ca=1, cb=0, precision=None):
    return lax.dot_general(
        a, b, (((ca,), (cb,)), ((), ())), precision=precision, preferred_element_type=F32
    )


def dot_full(a, b, ca=1, cb=0):
    return dot(a, b, ca, cb, lax.Precision.HIGHEST)


def split(a):
    high = a.astype(BF16)
    return high, (a - high.astype(F32)).astype(BF16)


def one_hot(mask):
    return jnp.where(mask, 1.0, 0.0).astype(BF16)


def call(body, outs, scratch=(), specs=None, flops=0, moved=0):
    return pl.pallas_call(
        body,
        out_shape=outs,
        in_specs=specs,
        scratch_shapes=list(scratch),
        compiler_params=pltpu.CompilerParams(vmem_limit_bytes=VMEM_BYTES),
        cost_estimate=pl.CostEstimate(flops=flops, bytes_accessed=moved, transcendentals=0),
    )


def f32(*shape):
    return jax.ShapeDtypeStruct(shape, F32)


def i32(*shape):
    return jax.ShapeDtypeStruct(shape, jnp.int32)


def strips_body(x_ref, d_ref, c_ref, top_ref, bottom_ref, left_ref, right_ref):
    for row, out in ((0, top_ref), (CR - 1, bottom_ref)):
        out[0:16, :] = x_ref[:, row, :]
        out[16:32, :] = d_ref[:, row, :]
        out[32:40, :] = jnp.broadcast_to(c_ref[row : row + 1, :], (8, CC))
    lane = iota((CR, 128), 1)
    left = jnp.zeros((CR, 128), F32)
    right = jnp.zeros((CR, 128), F32)
    for f in range(33):
        ref = x_ref.at[f] if f < 16 else (d_ref.at[f - 16] if f < 32 else c_ref)
        west = ref[:, 0:128]
        east = ref[:, 128:256]
        left = jnp.where(lane == f, pltpu.roll(west, f, 1) if f else west, left)
        right = jnp.where(lane == f, pltpu.roll(east, f + 1, 1), right)
    left_ref[...] = left
    right_ref[...] = right


def patches_body(lp_ref, tp_ref, poc_ref, slot_ref, lp_s):
    lp_s[0] = lp_ref[:, 0:128]
    lp_s[1] = lp_ref[:, 128:256]
    cell = iota((CC, CC), 0)
    spot = iota((CC, CC), 1)
    acc = jnp.zeros((16, CC), F32)
    for q in range(4):
        every = pl.ds(4 * q, 8, stride=16)
        rows = jnp.concatenate([lp_s[0, every, :], lp_s[1, every, :]], axis=1)
        parts = jnp.concatenate([rows >> 4, rows & 15], axis=0).astype(F32).astype(BF16)
        pick = one_hot(((spot >> 6) == q) & (cell == 4 * (spot & 63)))
        acc = acc + dot(parts, pick)
    slots = (acc[8:16] * 128.0 + acc[0:8]).astype(jnp.int32)
    slot_ref[...] = slots
    listed = jnp.concatenate([tp_ref[e : e + 1, :] for e in range(SLOTS)], axis=1)
    table = jnp.concatenate(
        [jnp.broadcast_to(listed >> 8, (8, 2048)), jnp.broadcast_to(listed & 255, (8, 2048))], axis=0
    )
    table = table.astype(F32).astype(BF16)
    entry = iota((2048, CC), 0)
    highs = []
    lows = []
    for i in range(8):
        found = dot(table, one_hot(entry == slots[i : i + 1, :]))
        highs.append(found[0:1])
        lows.append(found[8:9])
    found = jnp.concatenate(highs + lows, axis=0).astype(BF16)
    for q in range(4):
        spread = dot(found, one_hot(spot == q * 64 + (cell >> 2)), 1, 1)
        ids = (spread[0:8] * 256.0 + spread[8:16]).astype(jnp.int32)
        for r in range(4):
            poc_ref[0, pl.ds(4 * q + r, 8, stride=16), :] = ids[:, 0:128]
            poc_ref[1, pl.ds(4 * q + r, 8, stride=16), :] = ids[:, 128:256]


def edges(c, east_ref, south_ref):
    east = 0.5 * (c + pltpu.roll(c, CC - 1, 1))
    east_ref[...] = jnp.where(iota((CR, CC), 1) == CC - 1, 0.0, east)
    south = 0.5 * (c + pltpu.roll(c, CR - 1, 0))
    south_ref[...] = jnp.where(iota((CR, CC), 0) == CR - 1, 0.0, south)


def products_body(
    src_ref, x_ref, d_ref, c_ref, gr_ref, poc_ref,
    top_ref, bottom_ref, left_ref, right_ref,
    north_ref, south_ref, west_ref, east_ref,
    gram_ref, nf_ref, sf_ref, wf_ref, ef_ref,
    q_s, r_s, ee_s, es_s, leak_s, acc_s,
):
    edges(c_ref[...], ee_s, es_s)
    leak_s[...] = GROUND_LEAK * gr_ref[...].astype(F32)
    for own, far, out in ((top_ref, north_ref, nf_ref), (bottom_ref, south_ref, sf_ref)):
        edge = jnp.where(far[32:33, :] > 0, 0.5 * (own[32:33, :] + far[32:33, :]), 0.0)
        out[...] = edge * (own[0:32, :] - far[0:32, :])
    for own, far, out in ((left_ref, west_ref, wf_ref), (right_ref, east_ref, ef_ref)):
        edge = jnp.where(far[:, 32:33] > 0, 0.5 * (own[:, 32:33] + far[:, 32:33]), 0.0)
        out[...] = edge * (own[...] - far[...])
    lane = iota((CR, 128), 1)

    def operate(v, field):
        flow = ee_s[...] * (v - pltpu.roll(v, CC - 1, 1))
        total = flow - pltpu.roll(flow, 1, 1) + leak_s[...] * v
        flow = es_s[...] * (v - pltpu.roll(v, CR - 1, 0))
        total = total + flow - pltpu.roll(flow, 1, 0)
        west = pltpu.roll(wf_ref[...], lax.rem(128 - field, 128), 1)
        east = pltpu.roll(ef_ref[...], 127 - field, 1)
        return (
            total[:, 0:128] + jnp.where(lane == 0, west, 0.0),
            total[:, 128:256] + jnp.where(lane == 127, east, 0.0),
        )

    def field_step(k, carry):
        first, second = operate(d_ref[k], k + 16)
        q_s[k, :, 0:128] = first
        q_s[k, :, 128:256] = second
        q_s[k, 0:1, :] += nf_ref[pl.ds(k + 16, 1), :]
        q_s[k, CR - 1 : CR, :] += sf_ref[pl.ds(k + 16, 1), :]
        first, second = operate(x_ref[k], k)
        patch = src_ref[k]
        r_s[k, :, 0:128] = jnp.where(poc_ref[0] == patch, SOURCE_AMPS, 0.0) - first
        r_s[k, :, 128:256] = jnp.where(poc_ref[1] == patch, SOURCE_AMPS, 0.0) - second
        r_s[k, 0:1, :] -= nf_ref[pl.ds(k, 1), :]
        r_s[k, CR - 1 : CR, :] -= sf_ref[pl.ds(k, 1), :]
        return carry

    lax.fori_loop(0, K, field_step, 0)
    acc_s[...] = jnp.zeros((256, 256), F32)

    def gram_step(b, carry):
        rows = pl.ds(pl.multiple_of(b * 8, 8), 8)
        dh, dl = split(d_ref[:, rows, :].reshape(128, CC))
        qh, ql = split(q_s[:, rows, :].reshape(128, CC))
        rh, rl = split(r_s[:, rows, :].reshape(128, CC))
        lh = jnp.concatenate([dh, qh], axis=0)
        ll = jnp.concatenate([dl, ql], axis=0)
        gh = jnp.concatenate([qh, rh], axis=0)
        gl = jnp.concatenate([ql, rl], axis=0)
        acc_s[...] += dot(lh, gh, 1, 1) + (dot(lh, gl, 1, 1) + dot(ll, gh, 1, 1))
        return carry

    lax.fori_loop(0, CR // 8, gram_step, 0)
    i = iota((256, 256), 0)
    j = iota((256, 256), 1)
    kept = jnp.where((i & 7) == (j & 7), acc_s[...], 0.0)
    fold_rows = jnp.where(iota((32, 256), 0) == (iota((32, 256), 1) >> 3), 1.0, 0.0)
    fold_lanes = jnp.where((iota((256, 128), 0) >> 3) == iota((256, 128), 1), 1.0, 0.0)
    small = dot_full(dot_full(fold_rows, kept), fold_lanes)
    packed = small[0:8]
    for q in range(1, 4):
        packed = packed + pltpu.roll(small[8 * q : 8 * q + 8], 32 * q, 1)
    gram_ref[...] = packed


def update_body(
    src_ref, gram_ref, x_ref, d_ref, c_ref, gr_ref, poc_ref, slot_ref, ids_ref,
    nf_ref, sf_ref, wf_ref, ef_ref,
    xo_ref, do_ref, msg_ref,
    db_s, cur_s, ee_s, es_s, leak_s, bs_s, wn_s, en_s, nn_s, sn_s,
):
    packed = gram_ref[...]
    small = jnp.concatenate(
        [packed] + [pltpu.roll(packed, 128 - 32 * q, 1) for q in range(1, 4)], axis=0
    )
    lane = iota((16, 128), 1)
    row = iota((16, 128), 0)
    system = jnp.where(lane < 32, small[0:16], pltpu.roll(small[16:32], 32, 1))
    system = jnp.where(lane < 64, system, 0.0)
    for j in range(K):
        pivot = system[j : j + 1, :]
        pivot = pivot / pivot[:, j : j + 1]
        system = jnp.where(row == j, pivot, system - system[:, j : j + 1] * pivot)

    def part(p):
        return jnp.where(lane < 16, pltpu.roll(system, 128 - 16 * p, 1), 0.0)

    alpha = part(1)
    blank = jnp.zeros((112, 128), F32)
    alpha_pad = jnp.concatenate([alpha, blank], axis=0)
    beta = dot_full(part(2), alpha_pad) - part(3)
    beta_pad = jnp.concatenate([beta, blank], axis=0)
    i = iota((128, 128), 0)
    j = iota((128, 128), 1)
    same = (i & 7) == (j & 7)
    repeat_rows = jnp.where((i >> 3) == j, 1.0, 0.0)
    repeat_lanes = jnp.where(i == (j >> 3), 1.0, 0.0)
    mix = []
    for coef in (alpha_pad, beta_pad):
        wide = dot_full(dot_full(repeat_rows, coef, 1, 1), repeat_lanes)
        mix.append(jnp.where(same, wide, 0.0))
    mh, ml = split(jnp.concatenate(mix, axis=0))
    carry_over = jnp.concatenate(
        [jnp.where(row == lane, 1.0, 0.0), alpha, jnp.zeros((96, 128), F32)], axis=0
    )
    wn_s[...] = dot_full(wf_ref[...], carry_over)
    en_s[...] = dot_full(ef_ref[...], carry_over)
    turned = carry_over.T[0:16, 0:32]
    nn_s[...] = dot_full(turned, nf_ref[...])
    sn_s[...] = dot_full(turned, sf_ref[...])
    edges(c_ref[...], ee_s, es_s)
    leak_s[...] = GROUND_LEAK * gr_ref[...].astype(F32)

    def combine_step(b, carry):
        rows = pl.ds(pl.multiple_of(b * 8, 8), 8)
        dh, dl = split(d_ref[:, rows, :].reshape(128, CC))
        mixed = dot(mh, dh) + (dot(mh, dl) + dot(ml, dh))
        xo_ref[:, rows, :] = x_ref[:, rows, :] + mixed[0:128].reshape(16, 8, CC)
        db_s[:, rows, :] = mixed[128:256].reshape(16, 8, CC)
        return carry

    lax.fori_loop(0, CR // 8, combine_step, 0)
    lane2 = iota((CR, 128), 1)

    def field_step(k, carry):
        v = xo_ref[k]
        flow = ee_s[...] * (v - pltpu.roll(v, CC - 1, 1))
        total = flow - pltpu.roll(flow, 1, 1) + leak_s[...] * v
        flow = jnp.abs(flow)
        current = flow + pltpu.roll(flow, 1, 1)
        flow = es_s[...] * (v - pltpu.roll(v, CR - 1, 0))
        total = total + flow - pltpu.roll(flow, 1, 0)
        flow = jnp.abs(flow)
        current = current + flow + pltpu.roll(flow, 1, 0)
        west = jnp.where(lane2 == 0, pltpu.roll(wn_s[...], lax.rem(128 - k, 128), 1), 0.0)
        east = jnp.where(lane2 == 127, pltpu.roll(en_s[...], 127 - k, 1), 0.0)
        north = nn_s[pl.ds(k, 1), :]
        south = sn_s[pl.ds(k, 1), :]
        patch = src_ref[k]
        for half, outer in ((0, west), (1, east)):
            at = slice(128 * half, 128 * half + 128)
            source = jnp.where(poc_ref[half] == patch, SOURCE_AMPS, 0.0)
            do_ref[k, :, at] = (source - (total[:, at] + outer)) + db_s[k, :, at]
            cur_s[half, k] = current[:, at] + jnp.abs(outer)
            cur_s[half, k, 0:1, :] += jnp.abs(north[:, at])
            cur_s[half, k, CR - 1 : CR, :] += jnp.abs(south[:, at])
        do_ref[k, 0:1, :] -= north
        do_ref[k, CR - 1 : CR, :] -= south
        return carry

    lax.fori_loop(0, K, field_step, 0)
    cell = iota((CC, CC), 0)
    spot = iota((CC, CC), 1)
    blocks = jnp.zeros((128, CC), F32)
    for q in range(4):
        halves = []
        for half in range(2):
            rows = [cur_s[half, :, pl.ds(4 * q + r, 8, stride=16), :] for r in range(4)]
            halves.append(((rows[0] + rows[1]) + (rows[2] + rows[3])).reshape(128, 128))
        pooled = jnp.concatenate(halves, axis=1)
        high, low = split(0.5 * pooled)
        spread = one_hot(spot == q * 64 + (cell >> 2))
        blocks = blocks + (dot(high, spread) + dot(low, spread))
    bs_s[0] = blocks[:, 0:128]
    bs_s[1] = blocks[:, 128:256]
    entry = iota((2048, CC), 0)
    sums = jnp.zeros((32, 2048), F32)
    for b in range(8):
        every = pl.ds(b, 16, stride=8)
        high, low = split(jnp.concatenate([bs_s[0, every, :], bs_s[1, every, :]], axis=1))
        place = one_hot(entry == slot_ref[b : b + 1, :])
        sums = sums + dot(jnp.concatenate([high, low], axis=0), place, 1, 1)
    sums = sums[0:16] + sums[16:32]
    stacked = jnp.concatenate([sums[:, 128 * e : 128 * e + 128] for e in range(SLOTS)], axis=0)
    msg_ref[:, 0:256] = stacked.T
    msg_ref[:, 256:384] = ids_ref[...]


def owner_body(msg_ref, out_ref):
    values = msg_ref[:, 0:256].T
    ids = msg_ref[:, 256:384].T
    patch = iota((PATCH_DEV, 256), 0).astype(F32)
    total = jnp.zeros((32, PATCH_DEV), F32)
    for e in range(0, SLOTS, 2):
        pair = jnp.concatenate(
            [values[16 * e : 16 * e + 16], values[16 * e + 16 : 16 * e + 32]], axis=1
        )
        high, low = split(pair)
        at = jnp.concatenate([ids[e : e + 1], ids[e + 1 : e + 2]], axis=1)
        total = total + dot(jnp.concatenate([high, low], axis=0), one_hot(patch == at), 1, 1)
    out_ref[...] = total[0:16] + total[16:32]


def exchange(value, axis, partner):
    return lax.ppermute(value, axis, [(i, partner(i)) for i in range(lax.axis_size(axis))])


def ring_partner(stride, step):
    table = ((1, 0, 3, 2), (3, 2, 1, 0))[step]

    def partner(i):
        at = (i // stride) % 4
        return i + (table[at] - at) * stride

    return partner


def add_up(value):
    value = value + exchange(value, "col", lambda i: i ^ 1)
    for axis, stride in (("col", 2), ("row", 1), ("row", 4)):
        for step in range(2):
            value = value + exchange(value, axis, ring_partner(stride, step))
    return value


def on_device(iterate, direction, conductance, ground, local_patch, tile_patches, sources):
    vmem = pl.BlockSpec(memory_space=pltpu.VMEM)
    smem = pl.BlockSpec(memory_space=pltpu.SMEM)
    listed = tile_patches.reshape(DEVICES, SLOTS)
    owners = jnp.arange(DEVICES, dtype=jnp.int32)[:, None]
    ids = jnp.pad((listed - owners * PATCH_DEV).astype(F32), ((0, 0), (0, 128 - SLOTS)))

    top, bottom, left, right = call(
        strips_body,
        (f32(40, CC), f32(40, CC), f32(CR, 128), f32(CR, 128)),
        specs=[vmem] * 3,
        moved=4_500_000,
    )(iterate, direction, conductance)
    rows = lax.axis_size("row")
    cols = lax.axis_size("col")
    north = lax.ppermute(bottom, "row", [(i, i + 1) for i in range(rows - 1)])
    south = lax.ppermute(top, "row", [(i + 1, i) for i in range(rows - 1)])
    west = lax.ppermute(right, "col", [(i, i + 1) for i in range(cols - 1)])
    east = lax.ppermute(left, "col", [(i + 1, i) for i in range(cols - 1)])

    patch_of_cell, slots = call(
        patches_body,
        (i32(2, CR, 128), i32(8, CC)),
        scratch=[pltpu.VMEM((2, CR, 128), jnp.int32)],
        specs=[vmem] * 2,
        moved=10_000_000,
    )(local_patch, listed.T)

    gram, nf, sf, wf, ef = call(
        products_body,
        (f32(8, 128), f32(32, CC), f32(32, CC), f32(CR, 128), f32(CR, 128)),
        scratch=[
            pltpu.VMEM((K, CR, CC), F32),
            pltpu.VMEM((K, CR, CC), F32),
            pltpu.VMEM((CR, CC), F32),
            pltpu.VMEM((CR, CC), F32),
            pltpu.VMEM((CR, CC), F32),
            pltpu.VMEM((256, 256), F32),
        ],
        specs=[smem] + [vmem] * 13,
        moved=20_000_000,
    )(
        sources, iterate, direction, conductance, ground, patch_of_cell,
        top, bottom, left, right, north, south, west, east,
    )
    gram = add_up(gram)

    new_iterate, new_direction, message = call(
        update_body,
        (f32(K, CR, CC), f32(K, CR, CC), f32(DEVICES, 384)),
        scratch=[
            pltpu.VMEM((K, CR, CC), F32),
            pltpu.VMEM((2, K, CR, 128), F32),
            pltpu.VMEM((CR, CC), F32),
            pltpu.VMEM((CR, CC), F32),
            pltpu.VMEM((CR, CC), F32),
            pltpu.VMEM((2, 128, 128), F32),
            pltpu.VMEM((CR, 128), F32),
            pltpu.VMEM((CR, 128), F32),
            pltpu.VMEM((16, CC), F32),
            pltpu.VMEM((16, CC), F32),
        ],
        specs=[smem] + [vmem] * 12,
        moved=20_000_000,
    )(
        sources, gram, iterate, direction, conductance, ground, patch_of_cell, slots, ids,
        nf, sf, wf, ef,
    )
    received = lax.all_to_all(message, AXES, 0, 0, tiled=True)
    migration = call(owner_body, f32(K, PATCH_DEV), specs=[vmem], moved=1_000_000)(received)
    return new_iterate, new_direction, migration


def solution(mesh):
    in_specs = (
        P(None, "row", "col"),
        P(None, "row", "col"),
        P("row", "col"),
        P("row", "col"),
        P("row", "col"),
        P("row", "col", None),
        P(),
    )
    out_specs = (P(None, "row", "col"), P(None, "row", "col"), P(None, ("row", "col")))
    return jax.shard_map(
        on_device, mesh=mesh, in_specs=in_specs, out_specs=out_specs, check_vma=False
    )
```

time: 979 us -> 99.6 us (0.10); the launches traced: 968 us -> 99.3 us
  waiting for transfers between devices: 606 us -> 8.06 us
  blocking collectives: 137 us -> 23.5 us
  local copies, waits for them, and re-layouts: 86.3 us -> 6.56 us
  other arithmetic: 80.2 us -> 0.77 us
  Pallas kernels: 0 us -> 31.9 us
  matrix products: 22.4 us -> 0 us
  between operations: 14.7 us -> 0.85 us
    reduce_scatter x1 -> x0, waiting for transfers between devices: 601 us -> none  [on_device(): lax.psum_scatter(spread, ('row', 'col'), scatter_dimension=1, tiled=True)]
    psum x2 -> x0, blocking collectives: 137 us -> none  [the longest x1 69 us: on_device(): cross = lax.psum(products(image, new_residual), ('row', 'col'))]
    pallas_call x0 -> x5, Pallas kernels: none -> 31.9 us  [the longest x1 15 us: on_device(): call(update_body, (f32(K, CR, CC), f32(K, CR, CC), f32(DEVICES, 384)), sc...]
    scatter-add x1 -> x0, other arithmetic: 30.9 us -> none  [on_device(): jax.ops.segment_sum(tile_sums, owned_list, num_segments=PATCH_DEV * devices)]
    all_to_all x0 -> x1, blocking collectives: none -> 23.5 us  [on_device(): received = lax.all_to_all(message, AXES, 0, 0, tiled=True)]
    dot_general x6 -> x0, matrix products: 21.6 us -> none  [the longest x3 11.9 us: combine(): jnp.einsum('kab,kl->lab', fields, matrix, precision=lax.Precision.HIGHEST)]
    slice x9 -> x0, local copies, waits for them, and re-layouts: 15.2 us -> none  [the longest x4 9.41 us: with_halo(): head = lax.slice_in_dim(cells, 0, width, axis=dim)]
    unnamed x36 -> x24, local copies, waits for them, and re-layouts: 20 us -> 6.22 us
  transfers between devices with their start and end apart: 9 -> 11, of which waited for: 3 -> 7; matrix products, arithmetic and copies ran while one was open for 5% -> 1% of each run, Pallas kernels for 0% -> 2%
where the time goes in v1:
time: 99.6 us; the launch traced here: 99.3 us
  Pallas kernels  31.9 us (32%)
  starting transfers between devices  27.7 us (28%)
  blocking collectives  23.5 us (24%)
  waiting for transfers between devices  8.06 us (8%)
  local copies, waits for them, and re-layouts  6.56 us (7%)
    all_to_all x1, blocking collectives, on_device(): received = lax.all_to_all(message, AXES, 0, 0, tiled=True)  23.5 us
    ppermute x7, starting transfers between devices, exchange(): lax.ppermute(value, axis, [(i, partner(i)) for i in range(lax.axis_size(a...  15.9 us
    pallas_call x1, Pallas kernels, on_device(): call(update_body, (f32(K, CR, CC), f32(K, CR, CC), f32(DEVICES, 384)), sc...  15 us
    pallas_call x1, Pallas kernels, on_device(): call(products_body, (f32(8, 128), f32(32, CC), f32(32, CC), f32(CR, 128),...  12.5 us
    ppermute x7, waiting for transfers between devices, exchange(): lax.ppermute(value, axis, [(i, partner(i)) for i in range(lax.axis_size(a...  8.05 us
    unnamed x24, local copies, waits for them, and re-layouts  6.22 us
    ppermute x1, starting transfers between devices, on_device(): north = lax.ppermute(bottom, 'row', [(i, i + 1) for i in range(rows - 1)])  3.99 us
    ppermute x1, starting transfers between devices, on_device(): east = lax.ppermute(left, 'col', [(i + 1, i) for i in range(cols - 1)])  3.33 us
  transfers between devices with their start and end apart: 11, of which 7 were waited for; matrix products, arithmetic and copies ran while one was open for 1% of the time, Pallas kernels for 2%

profile of v1, /device:TPU:1, one launch (start us, length us, event | category | flops | bytes accessed | tf_op | source)
XLA Modules:
  0.0 99.3 jit_solution(8605609422447192534)
XLA Ops:
  0.6 1.6 %copy-done = f32[16,128,256]{2,1,0:T(8,128)S(1)} copy-done((f32[16,128,256]{2,1,0:T(8,128)S(1)}, f32[16,128,256]{2,1,0:T(8,128)}, u32[]{:S(2)}) %copy-start) | copy-done | bytes 2097176
  2.2 1.6 %copy-done.2 = f32[16,128,256]{2,1,0:T(8,128)S(1)} copy-done((f32[16,128,256]{2,1,0:T(8,128)S(1)}, f32[16,128,256]{2,1,0:T(8,128)}, u32[]{:S(2)}) %copy-start.2) | copy-done | bytes 2097176
  4.8 1.2 %shard_map.95 = (f32[40,256]{1,0:T(8,128)S(1)}, f32[40,256]{1,0:T(8,128)S(1)}, f32[128,128]{1,0:T(8,128)S(1)}, f32[128,128]{1,0:T(8,128)S(1)}) custom-call(f32[16,128,256]{2,1,0:T(8,128)S(1)} %copy-done, f32[16,128,256]{2,1,0:T(8,128)S(1)} %copy-done.2, f32[128,256]{1,0:T(8,128)S(1)} %copy-done.5), custom_call_target="tpu_custom_call" | custom-call | bytes 4500000 | tf_op jit(solution)/shard_map/pallas_call | solution.py:352
  6.0 3.3 %collective-permute-start.3 = (f32[128,128]{1,0:T(8,128)S(1)}, f32[128,128]{1,0:T(8,128)S(1)}, u32[]{:S(2)}, u32[]{:S(2)}) collective-permute-start(f32[128,128]{1,0:T(8,128)S(1)} %get-tuple-element.20.left_ref), channel_id=1, source_target_pairs={{1,0},{2,1},{3,2},{4,3},{5,4},{6,5},{7,6},{9,8},{10,9},{11,10},{12... | collective-permute-start | bytes 196616 | tf_op jit(solution)/shard_map/ppermute | solution.py:363
  9.3 3.2 %collective-permute-start.2 = (f32[128,128]{1,0:T(8,128)S(1)}, f32[128,128]{1,0:T(8,128)S(1)}, u32[]{:S(2)}, u32[]{:S(2)}) collective-permute-start(f32[128,128]{1,0:T(8,128)S(1)} %get-tuple-element.21.right_ref), channel_id=1, source_target_pairs={{0,1},{1,2},{2,3},{3,4},{4,5},{5,6},{6,7},{8,9},{9,10},{10,11},{11... | collective-permute-start | bytes 196616 | tf_op jit(solution)/shard_map/ppermute | solution.py:362
  12.5 1.3 %collective-permute-start.1 = (f32[40,256]{1,0:T(8,128)S(1)}, f32[40,256]{1,0:T(8,128)S(1)}, u32[]{:S(2)}, u32[]{:S(2)}) collective-permute-start(f32[40,256]{1,0:T(8,128)S(1)} %get-tuple-element.18.top_ref), channel_id=1, source_target_pairs={{8,0},{16,8},{24,16},{32,24},{40,32},{48,40},{56,48},{64,56},{72,6... | collective-permute-start | bytes 122888 | tf_op jit(solution)/shard_map/ppermute | solution.py:361
  13.8 4.0 %collective-permute-start = (f32[40,256]{1,0:T(8,128)S(1)}, f32[40,256]{1,0:T(8,128)S(1)}, u32[]{:S(2)}, u32[]{:S(2)}) collective-permute-start(f32[40,256]{1,0:T(8,128)S(1)} %get-tuple-element.19.bottom_ref), channel_id=1, source_target_pairs={{0,8},{8,16},{16,24},{24,32},{32,40},{40,48},{48,56},{56,64},{64,7... | collective-permute-start | bytes 122888 | tf_op jit(solution)/shard_map/ppermute | solution.py:360
  19.1 1.8 %shard_map.94 = (s32[2,128,128]{2,1,0:T(8,128)S(1)}, s32[8,256]{1,0:T(8,128)S(1)}) custom-call(s32[128,256]{1,0:T(8,128)S(1)} %copy-done.8, s32[16,128]{1,0:T(8,128)S(1)} %bitcast.7), custom_call_target="tpu_custom_call" | custom-call | bytes 10000000 | tf_op jit(solution)/shard_map/pallas_call | solution.py:365
  21.0 1.6 %copy-done.3 = f32[16,128,256]{2,1,0:T(8,128)S(1)} copy-done((f32[16,128,256]{2,1,0:T(8,128)S(1)}, f32[16,128,256]{2,1,0:T(8,128)}, u32[]{:S(2)}) %copy-start.3) | copy-done | bytes 2097176
  22.6 12.5 %shard_map.96 = (f32[8,128]{1,0:T(8,128)S(1)}, f32[32,256]{1,0:T(8,128)S(1)}, f32[32,256]{1,0:T(8,128)S(1)}, f32[128,128]{1,0:T(8,128)S(1)}, f32[128,128]{1,0:T(8,128)S(1)}) custom-call(s32[16]{0:T(128)S(1)} %copy-done.9, f32[16,128,256]{2,1,0:T(8,128)S(1)} %copy-done.1, f32[16,128,256]{2,1,0:T(8,128)S(1)} %copy-done.3, f32[128,256]{1,0:T(8,128)S(1)} %copy-done.6, ...), custom_call_target="tpu_custom_call" | custom-call | bytes 20000000 | tf_op jit(solution)/shard_map/pallas_call | solution.py:373
  35.1 1.2 %collective-permute-done.4 = f32[8,128]{1,0:T(8,128)S(1)} collective-permute-done((f32[8,128]{1,0:T(8,128)S(1)}, f32[8,128]{1,0:T(8,128)S(1)}, u32[]{:S(2)}, u32[]{:S(2)}) %collective-permute-start.4) | collective-permute-done | bytes 4128 | tf_op jit(solution)/shard_map/ppermute | solution.py:324
  36.3 1.3 %collective-permute-start.5 = (f32[8,128]{1,0:T(8,128)S(1)}, f32[8,128]{1,0:T(8,128)S(1)}, u32[]{:S(2)}, u32[]{:S(2)}) collective-permute-start(f32[8,128]{1,0:T(8,128)S(1)} %add.23), channel_id=1, source_target_pairs={{0,2},{1,3},{2,0},{3,1},{4,6},{5,7},{6,4},{7,5},{8,10},{9,11},{10,... | collective-permute-start | bytes 12296 | tf_op jit(solution)/shard_map/ppermute | solution.py:324
  37.6 1.2 %collective-permute-done.5 = f32[8,128]{1,0:T(8,128)S(1)} collective-permute-done((f32[8,128]{1,0:T(8,128)S(1)}, f32[8,128]{1,0:T(8,128)S(1)}, u32[]{:S(2)}, u32[]{:S(2)}) %collective-permute-start.5) | collective-permute-done | bytes 4128 | tf_op jit(solution)/shard_map/ppermute | solution.py:324
  38.8 2.3 %collective-permute-start.6 = (f32[8,128]{1,0:T(8,128)S(1)}, f32[8,128]{1,0:T(8,128)S(1)}, u32[]{:S(2)}, u32[]{:S(2)}) collective-permute-start(f32[8,128]{1,0:T(8,128)S(1)} %add.24), channel_id=1, source_target_pairs={{0,6},{1,7},{2,4},{3,5},{4,2},{5,3},{6,0},{7,1},{8,14},{9,15},{10,... | collective-permute-start | bytes 12296 | tf_op jit(solution)/shard_map/ppermute | solution.py:324
  41.0 1.4 %collective-permute-done.6 = f32[8,128]{1,0:T(8,128)S(1)} collective-permute-done((f32[8,128]{1,0:T(8,128)S(1)}, f32[8,128]{1,0:T(8,128)S(1)}, u32[]{:S(2)}, u32[]{:S(2)}) %collective-permute-start.6) | collective-permute-done | bytes 4128 | tf_op jit(solution)/shard_map/ppermute | solution.py:324
  42.4 1.2 %collective-permute-start.7 = (f32[8,128]{1,0:T(8,128)S(1)}, f32[8,128]{1,0:T(8,128)S(1)}, u32[]{:S(2)}, u32[]{:S(2)}) collective-permute-start(f32[8,128]{1,0:T(8,128)S(1)} %add.25), channel_id=1, source_target_pairs={{0,8},{8,0},{16,24},{24,16},{32,40},{40,32},{48,56},{56,48},{64,72... | collective-permute-start | bytes 12296 | tf_op jit(solution)/shard_map/ppermute | solution.py:324
  43.7 1.2 %collective-permute-done.7 = f32[8,128]{1,0:T(8,128)S(1)} collective-permute-done((f32[8,128]{1,0:T(8,128)S(1)}, f32[8,128]{1,0:T(8,128)S(1)}, u32[]{:S(2)}, u32[]{:S(2)}) %collective-permute-start.7) | collective-permute-done | bytes 4128 | tf_op jit(solution)/shard_map/ppermute | solution.py:324
  44.9 4.6 %collective-permute-start.8 = (f32[8,128]{1,0:T(8,128)S(1)}, f32[8,128]{1,0:T(8,128)S(1)}, u32[]{:S(2)}, u32[]{:S(2)}) collective-permute-start(f32[8,128]{1,0:T(8,128)S(1)} %add.26), channel_id=1, source_target_pairs={{0,24},{8,16},{16,8},{24,0},{32,56},{40,48},{48,40},{56,32},{64,88... | collective-permute-start | bytes 12296 | tf_op jit(solution)/shard_map/ppermute | solution.py:324
  50.5 2.9 %collective-permute-start.9 = (f32[8,128]{1,0:T(8,128)S(1)}, f32[8,128]{1,0:T(8,128)S(1)}, u32[]{:S(2)}, u32[]{:S(2)}) collective-permute-start(f32[8,128]{1,0:T(8,128)S(1)} %add.27), channel_id=1, source_target_pairs={{0,32},{8,40},{16,48},{24,56},{32,0},{40,8},{48,16},{56,24},{64,96... | collective-permute-start | bytes 12296 | tf_op jit(solution)/shard_map/ppermute | solution.py:324
  53.4 1.2 %collective-permute-done.9 = f32[8,128]{1,0:T(8,128)S(1)} collective-permute-done((f32[8,128]{1,0:T(8,128)S(1)}, f32[8,128]{1,0:T(8,128)S(1)}, u32[]{:S(2)}, u32[]{:S(2)}) %collective-permute-start.9) | collective-permute-done | bytes 4128 | tf_op jit(solution)/shard_map/ppermute | solution.py:324
  54.6 3.7 %collective-permute-start.10 = (f32[8,128]{1,0:T(8,128)S(1)}, f32[8,128]{1,0:T(8,128)S(1)}, u32[]{:S(2)}, u32[]{:S(2)}) collective-permute-start(f32[8,128]{1,0:T(8,128)S(1)} %add.28), channel_id=1, source_target_pairs={{0,96},{8,104},{16,112},{24,120},{32,64},{40,72},{48,80},{56,88},{... | collective-permute-start | bytes 12296 | tf_op jit(solution)/shard_map/ppermute | solution.py:324
  59.2 15.0 %shard_map.97 = (f32[16,128,256]{2,1,0:T(8,128)}, f32[16,128,256]{2,1,0:T(8,128)}, f32[128,384]{1,0:T(8,128)S(1)}) custom-call(s32[16]{0:T(128)S(1)} %copy-done.9, f32[8,128]{1,0:T(8,128)S(1)} %add.29.gram_ref, f32[16,128,256]{2,1,0:T(8,128)S(1)} %copy-done.1, f32[16,128,256]{2,1,0:T(8,128)S(1)} %copy-done.4, f32[128,256]{1,0:T(8,128)S(1)} %copy-done.6, ...), custom_call_target="tpu_custom_call" | custom-call | bytes 20000000 | tf_op jit(solution)/shard_map/pallas_call | solution.py:392
  74.4 23.5 %all_to_all.11 = f32[128,1,384]{2,1,0:T(1,128)S(1)} all-to-all(f32[128,1,384]{2,1,0:T(1,128)S(1)} %copy.13), channel_id=1, replica_groups=mesh['row'=16,'col'=8] {'row','col'}, dimensions={0} | all-to-all | bytes 393216 | tf_op jit(solution)/shard_map/all_to_all | solution.py:413
  97.9 1.4 %shard_map.98 = f32[16,512]{1,0:T(8,128)} custom-call(f32[128,384]{1,0:T(8,128)S(1)} %bitcast.5), custom_call_target="tpu_custom_call" | custom-call | bytes 1000000 | tf_op jit(solution)/shard_map/pallas_call | solution.py:414
  (42 shorter events, 4.5 us)
Async XLA Ops:
  0.6 1.6 %copy-start = (f32[16,128,256]{2,1,0:T(8,128)S(1)}, f32[16,128,256]{2,1,0:T(8,128)}, u32[]{:S(2)}) copy-start(f32[16,128,256]{2,1,0:T(8,128)} %x_ref.5) | copy-start | bytes 6291460
  2.2 1.6 %copy-start.2 = (f32[16,128,256]{2,1,0:T(8,128)S(1)}, f32[16,128,256]{2,1,0:T(8,128)}, u32[]{:S(2)}) copy-start(f32[16,128,256]{2,1,0:T(8,128)} %d_ref.5) | copy-start | bytes 6291460
  3.8 0.9 copy-start.5
  4.7 13.6 %copy-start.10 = (s32[1,1,2048]{2,1,0:T(1,128)S(1)}, s32[1,1,2048]{2,1,0:T(1,128)}, u32[]{:S(2)}) copy-start(s32[1,1,2048]{2,1,0:T(1,128)} %param.12) | copy-start | bytes 24580
  4.7 14.4 %copy-start.8 = (s32[128,256]{1,0:T(8,128)S(1)}, s32[128,256]{1,0:T(8,128)}, u32[]{:S(2)}) copy-start(s32[128,256]{1,0:T(8,128)} %lp_ref.1) | copy-start | bytes 393220
  4.7 16.2 %copy-start.1 = (f32[16,128,256]{2,1,0:T(8,128)S(1)}, f32[16,128,256]{2,1,0:T(8,128)}, u32[]{:S(2)}) copy-start(f32[16,128,256]{2,1,0:T(8,128)} %x_ref.5) | copy-start | bytes 6291460
  4.7 16.2 %copy-start.6 = (f32[128,256]{1,0:T(8,128)S(1)}, f32[128,256]{1,0:T(8,128)}, u32[]{:S(2)}) copy-start(f32[128,256]{1,0:T(8,128)} %c_ref.5) | copy-start | bytes 393220
  4.7 16.2 %copy-start.7 = (s32[128,256]{1,0:T(8,128)S(1)}, s32[128,256]{1,0:T(8,128)}, u32[]{:S(2)}) copy-start(s32[128,256]{1,0:T(8,128)} %gr_ref.3) | copy-start | bytes 393220
  4.7 16.2 %copy-start.9 = (s32[16]{0:T(128)S(1)}, s32[16]{0:T(128)}, u32[]{:S(2)}) copy-start(s32[16]{0:T(128)} %src_ref.3) | copy-start | bytes 196
  6.0 14.9 %collective-permute-start.3 = (f32[128,128]{1,0:T(8,128)S(1)}, f32[128,128]{1,0:T(8,128)S(1)}, u32[]{:S(2)}, u32[]{:S(2)}) collective-permute-start(f32[128,128]{1,0:T(8,128)S(1)} %get-tuple-element.20.left_ref), channel_id=1, source_target_pairs={{1,0},{2,1},{3,2},{4,3},{5,4},{6,5},{7,6},{9,8},{10,9},{11,10},{12... | collective-permute-start | bytes 196616 | tf_op jit(solution)/shard_map/ppermute | solution.py:363
  9.3 11.6 %collective-permute-start.2 = (f32[128,128]{1,0:T(8,128)S(1)}, f32[128,128]{1,0:T(8,128)S(1)}, u32[]{:S(2)}, u32[]{:S(2)}) collective-permute-start(f32[128,128]{1,0:T(8,128)S(1)} %get-tuple-element.21.right_ref), channel_id=1, source_target_pairs={{0,1},{1,2},{2,3},{3,4},{4,5},{5,6},{6,7},{8,9},{9,10},{10,11},{11... | collective-permute-start | bytes 196616 | tf_op jit(solution)/shard_map/ppermute | solution.py:362
  12.5 8.4 %collective-permute-start.1 = (f32[40,256]{1,0:T(8,128)S(1)}, f32[40,256]{1,0:T(8,128)S(1)}, u32[]{:S(2)}, u32[]{:S(2)}) collective-permute-start(f32[40,256]{1,0:T(8,128)S(1)} %get-tuple-element.18.top_ref), channel_id=1, source_target_pairs={{8,0},{16,8},{24,16},{32,24},{40,32},{48,40},{56,48},{64,56},{72,6... | collective-permute-start | bytes 122888 | tf_op jit(solution)/shard_map/ppermute | solution.py:361
  13.8 7.1 %collective-permute-start = (f32[40,256]{1,0:T(8,128)S(1)}, f32[40,256]{1,0:T(8,128)S(1)}, u32[]{:S(2)}, u32[]{:S(2)}) collective-permute-start(f32[40,256]{1,0:T(8,128)S(1)} %get-tuple-element.19.bottom_ref), channel_id=1, source_target_pairs={{0,8},{8,16},{16,24},{24,32},{32,40},{40,48},{48,56},{56,64},{64,7... | collective-permute-start | bytes 122888 | tf_op jit(solution)/shard_map/ppermute | solution.py:360
  21.0 1.6 %copy-start.3 = (f32[16,128,256]{2,1,0:T(8,128)S(1)}, f32[16,128,256]{2,1,0:T(8,128)}, u32[]{:S(2)}) copy-start(f32[16,128,256]{2,1,0:T(8,128)} %d_ref.5) | copy-start | bytes 6291460
  22.6 36.7 %copy-start.4 = (f32[16,128,256]{2,1,0:T(8,128)S(1)}, f32[16,128,256]{2,1,0:T(8,128)}, u32[]{:S(2)}) copy-start(f32[16,128,256]{2,1,0:T(8,128)} %d_ref.5) | copy-start | bytes 6291460
  35.1 1.2 %collective-permute-start.4 = (f32[8,128]{1,0:T(8,128)S(1)}, f32[8,128]{1,0:T(8,128)S(1)}, u32[]{:S(2)}, u32[]{:S(2)}) collective-permute-start(f32[8,128]{1,0:T(8,128)S(1)} %get-tuple-element.22), channel_id=1, source_target_pairs={{0,1},{1,0},{2,3},{3,2},{4,5},{5,4},{6,7},{7,6},{8,9},{9,8},{10,11... | collective-permute-start | bytes 12296 | tf_op jit(solution)/shard_map/ppermute | solution.py:324
  36.3 2.5 %collective-permute-start.5 = (f32[8,128]{1,0:T(8,128)S(1)}, f32[8,128]{1,0:T(8,128)S(1)}, u32[]{:S(2)}, u32[]{:S(2)}) collective-permute-start(f32[8,128]{1,0:T(8,128)S(1)} %add.23), channel_id=1, source_target_pairs={{0,2},{1,3},{2,0},{3,1},{4,6},{5,7},{6,4},{7,5},{8,10},{9,11},{10,... | collective-permute-start | bytes 12296 | tf_op jit(solution)/shard_map/ppermute | solution.py:324
  38.8 3.7 %collective-permute-start.6 = (f32[8,128]{1,0:T(8,128)S(1)}, f32[8,128]{1,0:T(8,128)S(1)}, u32[]{:S(2)}, u32[]{:S(2)}) collective-permute-start(f32[8,128]{1,0:T(8,128)S(1)} %add.24), channel_id=1, source_target_pairs={{0,6},{1,7},{2,4},{3,5},{4,2},{5,3},{6,0},{7,1},{8,14},{9,15},{10,... | collective-permute-start | bytes 12296 | tf_op jit(solution)/shard_map/ppermute | solution.py:324
  42.4 2.5 %collective-permute-start.7 = (f32[8,128]{1,0:T(8,128)S(1)}, f32[8,128]{1,0:T(8,128)S(1)}, u32[]{:S(2)}, u32[]{:S(2)}) collective-permute-start(f32[8,128]{1,0:T(8,128)S(1)} %add.25), channel_id=1, source_target_pairs={{0,8},{8,0},{16,24},{24,16},{32,40},{40,32},{48,56},{56,48},{64,72... | collective-permute-start | bytes 12296 | tf_op jit(solution)/shard_map/ppermute | solution.py:324
  44.9 5.6 %collective-permute-start.8 = (f32[8,128]{1,0:T(8,128)S(1)}, f32[8,128]{1,0:T(8,128)S(1)}, u32[]{:S(2)}, u32[]{:S(2)}) collective-permute-start(f32[8,128]{1,0:T(8,128)S(1)} %add.26), channel_id=1, source_target_pairs={{0,24},{8,16},{16,8},{24,0},{32,56},{40,48},{48,40},{56,32},{64,88... | collective-permute-start | bytes 12296 | tf_op jit(solution)/shard_map/ppermute | solution.py:324
  50.5 4.1 %collective-permute-start.9 = (f32[8,128]{1,0:T(8,128)S(1)}, f32[8,128]{1,0:T(8,128)S(1)}, u32[]{:S(2)}, u32[]{:S(2)}) collective-permute-start(f32[8,128]{1,0:T(8,128)S(1)} %add.27), channel_id=1, source_target_pairs={{0,32},{8,40},{16,48},{24,56},{32,0},{40,8},{48,16},{56,24},{64,96... | collective-permute-start | bytes 12296 | tf_op jit(solution)/shard_map/ppermute | solution.py:324
  54.6 4.7 %collective-permute-start.10 = (f32[8,128]{1,0:T(8,128)S(1)}, f32[8,128]{1,0:T(8,128)S(1)}, u32[]{:S(2)}, u32[]{:S(2)}) collective-permute-start(f32[8,128]{1,0:T(8,128)S(1)} %add.28), channel_id=1, source_target_pairs={{0,96},{8,104},{16,112},{24,120},{32,64},{40,72},{48,80},{56,88},{... | collective-permute-start | bytes 12296 | tf_op jit(solution)/shard_map/ppermute | solution.py:324

commit v2 on v1

v2 whole, which is shorter than its diff:
```python
import jax
import jax.numpy as jnp
from jax import lax
from jax.experimental import pallas as pl
from jax.experimental.pallas import tpu as pltpu
from jax.sharding import PartitionSpec as P

K = 16
CR = 128
CC = 256
PATCH_DEV = 512
DEVICES = 128
SLOTS = 16
SOURCE_AMPS = 4.0
GROUND_LEAK = 2.0
AXES = ("row", "col")
F32 = jnp.float32
BF16 = jnp.bfloat16
VMEM_BYTES = 20 * 1024 * 1024


def iota(shape, dim):
    return lax.broadcasted_iota(jnp.int32, shape, dim)


def dot(a, b, ca=1, cb=0, precision=None):
    return lax.dot_general(
        a, b, (((ca,), (cb,)), ((), ())), precision=precision, preferred_element_type=F32
    )


def dot_full(a, b, ca=1, cb=0):
    return dot(a, b, ca, cb, lax.Precision.HIGHEST)


def split(a):
    high = a.astype(BF16)
    return high, (a - high.astype(F32)).astype(BF16)


def one_hot(mask):
    return jnp.where(mask, 1.0, 0.0).astype(BF16)


def stack2(high, low):
    return jnp.concatenate([high, low], axis=0)


def call(body, outs, scratch=(), specs=None, places=None, vmem=VMEM_BYTES, flops=0, moved=0):
    return pl.pallas_call(
        body,
        out_shape=outs,
        in_specs=specs,
        **({} if places is None else {"out_specs": places}),
        scratch_shapes=list(scratch),
        compiler_params=pltpu.CompilerParams(vmem_limit_bytes=vmem),
        cost_estimate=pl.CostEstimate(flops=flops, bytes_accessed=moved, transcendentals=0),
    )


def f32(*shape):
    return jax.ShapeDtypeStruct(shape, F32)


def i32(*shape):
    return jax.ShapeDtypeStruct(shape, jnp.int32)


def rows_body(x_ref, d_ref, c_ref, first_ref, second_ref, x_s, d_s, c_s, sems):
    copies = []
    for at, row in ((0, 0), (1, CR - 8)):
        for n, (ref, buf) in enumerate(((x_ref, x_s), (d_ref, d_s))):
            copies.append(pltpu.make_async_copy(ref.at[:, pl.ds(row, 8), :], buf.at[at], sems.at[at, n]))
        copies.append(pltpu.make_async_copy(c_ref.at[pl.ds(row, 8), :], c_s.at[at], sems.at[at, 2]))
    for copy in copies:
        copy.start()
    for copy in copies:
        copy.wait()
    even = jnp.bitwise_and(lax.axis_index("row"), 1) == 0

    def pack(x0, d0, c0, x1, d1, c1, out):
        out[0:16, :] = jnp.where(even, x1, x0)
        out[16:32, :] = jnp.where(even, d1, d0)
        out[32:40, :] = jnp.broadcast_to(jnp.where(even, c1, c0), (8, CC))

    top = (x_s[0, :, 0, :], d_s[0, :, 0, :], c_s[0, 0:1, :])
    bottom = (x_s[1, :, 7, :], d_s[1, :, 7, :], c_s[1, 7:8, :])
    pack(*top, *bottom, first_ref)
    pack(*bottom, *top, second_ref)


def columns_body(x_ref, d_ref, c_ref, after_ref, out_ref, xv_ref, dv_ref):
    lane = iota((CR, 128), 1)
    packed = jnp.zeros((CR, 128), F32)
    for f in range(33):
        ref = x_ref.at[f] if f < 16 else (d_ref.at[f - 16] if f < 32 else c_ref)
        west = ref[:, 0:128]
        east = ref[:, 128:256]
        if f < 32:
            kept = xv_ref if f < 16 else dv_ref
            kept[f % 16, :, 0:128] = west
            kept[f % 16, :, 128:256] = east
        both = pltpu.roll(jnp.where(lane == 127, east, west), 2 * f + 1, 1)
        packed = jnp.where((lane >> 1) == f, both, packed)
    out_ref[...] = packed


def patches_body(lp_ref, tp_ref, after_ref, poc_ref, slot_ref, ids_ref, lp_s):
    lp_s[0] = lp_ref[:, 0:128]
    lp_s[1] = lp_ref[:, 128:256]
    listed = tp_ref[0]
    lane = iota((8, 128), 1)
    row = iota((8, 128), 0)
    for j in range(16):
        chunk = jnp.broadcast_to(listed[:, 128 * j : 128 * j + 128], (8, 128))
        chunk = chunk - (8 * j + row) * PATCH_DEV
        ids_ref[8 * j : 8 * j + 8, :] = jnp.where((lane >> 4) == row, chunk, 0).astype(F32)
    cell = iota((CC, CC), 0)
    spot = iota((CC, CC), 1)
    acc = jnp.zeros((16, CC), F32)
    for q in range(4):
        every = pl.ds(4 * q, 8, stride=16)
        rows = jnp.concatenate([lp_s[0, every, :], lp_s[1, every, :]], axis=1)
        parts = stack2(rows >> 4, rows & 15).astype(F32).astype(BF16)
        pick = one_hot(((spot >> 6) == q) & (cell == 4 * (spot & 63)))
        acc = acc + dot(parts, pick)
    slot_ref[...] = (acc[8:16] * 128.0 + acc[0:8]).astype(jnp.int32)
    place = (acc[0:8] * 16.0 + acc[8:16]).astype(jnp.int32)
    table = stack2(jnp.broadcast_to(listed >> 8, (8, 2048)), jnp.broadcast_to(listed & 255, (8, 2048)))
    table = table.astype(F32).astype(BF16)
    entry = iota((2048, CC), 0)
    highs = []
    lows = []
    for i in range(8):
        found = dot(table, one_hot(entry == place[i : i + 1, :]))
        highs.append(found[0:1])
        lows.append(found[8:9])
    found = jnp.concatenate(highs + lows, axis=0).astype(BF16)
    for q in range(4):
        spread = dot(found, one_hot(spot == q * 64 + (cell >> 2)), 1, 1)
        ids = (spread[0:8] * 256.0 + spread[8:16]).astype(jnp.int32)
        for r in range(4):
            poc_ref[0, pl.ds(4 * q + r, 8, stride=16), :] = ids[:, 0:128]
            poc_ref[1, pl.ds(4 * q + r, 8, stride=16), :] = ids[:, 128:256]


def edges(c, east_ref, south_ref):
    east = 0.5 * (c + pltpu.roll(c, CC - 1, 1))
    east_ref[...] = jnp.where(iota((CR, CC), 1) == CC - 1, 0.0, east)
    south = 0.5 * (c + pltpu.roll(c, CR - 1, 0))
    south_ref[...] = jnp.where(iota((CR, CC), 0) == CR - 1, 0.0, south)


def operate(v, ee_s, es_s, leak_s):
    flow = ee_s[...] * (v - pltpu.roll(v, CC - 1, 1))
    total = flow - pltpu.roll(flow, 1, 1) + leak_s[...] * v
    flow = es_s[...] * (v - pltpu.roll(v, CR - 1, 0))
    return total + flow - pltpu.roll(flow, 1, 0)


def outer_columns(flows, field, lane):
    turned = pltpu.roll(flows, lax.rem(127 - 2 * field + 128, 128), 1)
    return jnp.where(lane == 0, turned, 0.0), jnp.where(lane == 127, turned, 0.0)


def products_body(
    src_ref, x_ref, d_ref, c_ref, gr_ref, poc_ref,
    own_first_ref, own_second_ref, far_first_ref, far_second_ref,
    cols_ref, cols_first_ref, cols_second_ref,
    gram_ref, nf_ref, sf_ref, cf_ref,
    q_s, r_s, ee_s, es_s, leak_s,
):
    edges(c_ref[...], ee_s, es_s)
    leak_s[...] = GROUND_LEAK * gr_ref[...].astype(F32)
    even = jnp.bitwise_and(lax.axis_index("row"), 1) == 0
    first = (own_first_ref[...], far_first_ref[...])
    second = (own_second_ref[...], far_second_ref[...])
    for out, before, after in ((nf_ref, second, first), (sf_ref, first, second)):
        own = jnp.where(even, before[0], after[0])
        far = jnp.where(even, before[1], after[1])
        edge = jnp.where(far[32:33, :] > 0, 0.5 * (own[32:33, :] + far[32:33, :]), 0.0)
        out[...] = edge * (own[0:32, :] - far[0:32, :])
    lane = iota((CR, 128), 1)
    even = jnp.bitwise_and(lax.axis_index("col"), 1) == 0
    next_cols = jnp.where(even, cols_first_ref[...], cols_second_ref[...])
    last_cols = jnp.where(even, cols_second_ref[...], cols_first_ref[...])
    far = jnp.where((lane & 1) == 0, pltpu.roll(next_cols, 127, 1), pltpu.roll(last_cols, 1, 1))
    own = cols_ref[...]
    edge = jnp.where(far > 0, 0.5 * (own + far), 0.0)
    edge = jnp.where((lane & 1) == 0, edge[:, 64:65], edge[:, 65:66])
    cf_ref[...] = jnp.where(lane < 64, edge * (own - far), 0.0)

    def field_step(k, carry):
        total = operate(d_ref[k], ee_s, es_s, leak_s)
        west, east = outer_columns(cf_ref[...], k + 16, lane)
        q_s[k, :, 0:128] = total[:, 0:128] + west
        q_s[k, :, 128:256] = total[:, 128:256] + east
        q_s[k, 0:1, :] += nf_ref[pl.ds(k + 16, 1), :]
        q_s[k, CR - 1 : CR, :] += sf_ref[pl.ds(k + 16, 1), :]
        total = operate(x_ref[k], ee_s, es_s, leak_s)
        west, east = outer_columns(cf_ref[...], k, lane)
        patch = src_ref[k]
        r_s[k, :, 0:128] = jnp.where(poc_ref[0] == patch, SOURCE_AMPS, 0.0) - (total[:, 0:128] + west)
        r_s[k, :, 128:256] = jnp.where(poc_ref[1] == patch, SOURCE_AMPS, 0.0) - (total[:, 128:256] + east)
        r_s[k, 0:1, :] -= nf_ref[pl.ds(k, 1), :]
        r_s[k, CR - 1 : CR, :] -= sf_ref[pl.ds(k, 1), :]
        return carry

    lax.fori_loop(0, K, field_step, 0)
    acc = jnp.zeros((256, 256), F32)
    for b in range(CR // 8):
        rows = slice(8 * b, 8 * b + 8)
        dh, dl = split(d_ref[:, rows, :].reshape(128, CC))
        qh, ql = split(q_s[:, rows, :].reshape(128, CC))
        rh, rl = split(r_s[:, rows, :].reshape(128, CC))
        lh = stack2(dh, qh)
        ll = stack2(dl, ql)
        gh = stack2(qh, rh)
        gl = stack2(ql, rl)
        acc = acc + (dot(lh, gh, 1, 1) + (dot(lh, gl, 1, 1) + dot(ll, gh, 1, 1)))
    i = iota((256, 256), 0)
    j = iota((256, 256), 1)
    kept = jnp.where((i & 7) == (j & 7), acc, 0.0)
    fold_rows = jnp.where(iota((32, 256), 0) == (iota((32, 256), 1) >> 3), 1.0, 0.0)
    fold_lanes = jnp.where((iota((256, 128), 0) >> 3) == iota((256, 128), 1), 1.0, 0.0)
    small = dot_full(dot_full(fold_rows, kept), fold_lanes)
    packed = small[0:8]
    for q in range(1, 4):
        packed = packed + pltpu.roll(small[8 * q : 8 * q + 8], 32 * q, 1)
    for o in range(DEVICES):
        gram_ref[8 * o : 8 * o + 8, :] = packed


def mixer(mix):
    high, low = split(mix)
    return stack2(jnp.concatenate([high, high], axis=1), jnp.concatenate([low, jnp.zeros_like(low)], axis=1))


def mixed(mix, d):
    both = dot(mix, stack2(*split(d)))
    return both[0:128] + both[128:256]


def iterate_body(
    gram_ref, x_ref, d_ref, c_ref, slot_ref, ids_ref, nf_ref, sf_ref, cf_ref,
    out_ref, msg_ref, beta_ref, nn_ref, sn_ref, cn_ref,
    xn_ref, fe_s, cs_s, ee_s, es_s, bs_s, turn_s, sem,
):
    edges(c_ref[...], ee_s, es_s)
    packed = gram_ref[...].reshape(DEVICES, 8, 128).sum(axis=0)
    small = jnp.concatenate(
        [packed] + [pltpu.roll(packed, 128 - 32 * q, 1) for q in range(1, 4)], axis=0
    )
    lane = iota((16, 128), 1)
    row = iota((16, 128), 0)
    system = jnp.where(lane < 32, small[0:16], pltpu.roll(small[16:32], 32, 1))
    system = jnp.where(lane < 64, system, 0.0)
    for j in range(K):
        pivot = system[j : j + 1, :]
        pivot = pivot / pivot[:, j : j + 1]
        system = jnp.where(row == j, pivot, system - system[:, j : j + 1] * pivot)

    def part(p):
        return jnp.where(lane < 16, pltpu.roll(system, 128 - 16 * p, 1), 0.0)

    alpha = part(1)
    blank = jnp.zeros((112, 128), F32)
    alpha_pad = stack2(alpha, blank)
    i = iota((128, 128), 0)
    j = iota((128, 128), 1)
    same = (i & 7) == (j & 7)
    repeat_rows = jnp.where((i >> 3) == j, 1.0, 0.0)
    repeat_lanes = jnp.where(i == (j >> 3), 1.0, 0.0)

    def widen(coef):
        return jnp.where(same, dot_full(dot_full(repeat_rows, coef, 1, 1), repeat_lanes), 0.0)

    mix = mixer(widen(alpha_pad))
    for b in range(CR // 8):
        rows = slice(8 * b, 8 * b + 8)
        step = mixed(mix, d_ref[:, rows, :].reshape(128, CC))
        xn_ref[:, rows, :] = x_ref[:, rows, :] + step.reshape(16, 8, CC)
    leave = pltpu.make_async_copy(xn_ref, out_ref, sem)
    leave.start()
    beta = dot_full(part(2), alpha_pad) - part(3)
    beta_ref[...] = widen(stack2(beta, blank))
    base = jnp.concatenate(
        [jnp.where(row == lane, 1.0, 0.0), alpha, jnp.zeros((96, 128), F32)], axis=0
    )
    pair_rows = jnp.where((i >> 1) == j, 1.0, 0.0)
    pair_lanes = jnp.where(i == (j >> 1), 1.0, 0.0)
    pairs = dot_full(dot_full(pair_rows, base), pair_lanes)
    cn = dot_full(cf_ref[...], jnp.where((i & 1) == (j & 1), pairs, 0.0))
    cn_ref[...] = cn
    turn_s[...] = jnp.abs(cn).T
    turned = base.T[0:16, 0:32]
    nn_ref[...] = dot_full(turned, nf_ref[...])
    sn_ref[...] = dot_full(turned, sf_ref[...])

    def field_step(k, carry):
        v = xn_ref[k]
        flow = jnp.abs(ee_s[...] * (v - pltpu.roll(v, CC - 1, 1)))
        fe_s[0, k] = flow[:, 0:128]
        fe_s[1, k] = flow[:, 128:256]
        flow = jnp.abs(es_s[...] * (v - pltpu.roll(v, CR - 1, 0)))
        flow = flow + pltpu.roll(flow, 1, 0)
        north = jnp.abs(nn_ref[pl.ds(k, 1), :])
        south = jnp.abs(sn_ref[pl.ds(k, 1), :])
        for half in range(2):
            at = slice(128 * half, 128 * half + 128)
            cs_s[half, k] = flow[:, at]
            cs_s[half, k, 0:1, :] += north[:, at]
            cs_s[half, k, CR - 1 : CR, :] += south[:, at]
        return carry

    lax.fori_loop(0, K, field_step, 0)
    cell = iota((CC, CC), 0)
    spot = iota((CC, CC), 1)
    blocks = jnp.zeros((128, CC), F32)
    for q in range(4):

        def pool(ref):
            halves = []
            for half in range(2):
                rows = [ref[half, :, pl.ds(4 * q + r, 8, stride=16), :] for r in range(4)]
                halves.append(((rows[0] + rows[1]) + (rows[2] + rows[3])).reshape(128, 128))
            return split(jnp.concatenate(halves, axis=1))

        here = jnp.where(spot == q * 64 + (cell >> 2), 1.0, 0.0)
        ahead = jnp.where(spot == q * 64 + ((cell + 1) >> 2), 1.0, 0.0)
        ahead = jnp.where((cell & 3) == 3, jnp.where(((cell + 1) >> 2) < 64, ahead, 0.0), ahead)
        along = (here + ahead).astype(BF16)
        here = here.astype(BF16)
        high, low = pool(fe_s)
        blocks = blocks + (dot(high, along) + dot(low, along))
        high, low = pool(cs_s)
        blocks = blocks + (dot(high, here) + dot(low, here))
    bs_s[0] = blocks[:, 0:128]
    bs_s[1] = blocks[:, 128:256]
    outer = jnp.concatenate(
        [turn_s[pl.ds(1, 16, stride=2), :], turn_s[pl.ds(0, 16, stride=2), :]], axis=1
    )
    outer = stack2(*split(outer))
    target = ((cell >> 2) & 3) * 64 + jnp.where(cell < 128, 0, 63)
    band = (cell & 127) >> 4
    entry = iota((2048, CC), 0)
    sums = jnp.zeros((32, 2048), F32)
    for b in range(8):
        every = pl.ds(b, 16, stride=8)
        rim = dot(outer, one_hot((spot == target) & (band == b)))
        rim = rim[0:16] + rim[16:32]
        inner = jnp.concatenate([bs_s[0, every, :], bs_s[1, every, :]], axis=1)
        place = one_hot(entry == slot_ref[b : b + 1, :])
        sums = sums + dot(stack2(*split(0.5 * (inner + rim))), place, 1, 1)
    sums = sums[0:16] + sums[16:32]
    stacked = jnp.concatenate([sums[:, 128 * e : 128 * e + 128] for e in range(SLOTS)], axis=0)
    msg_ref[pl.ds(0, DEVICES, stride=3), :] = stacked[0:128].T
    msg_ref[pl.ds(1, DEVICES, stride=3), :] = stacked[128:256].T
    msg_ref[pl.ds(2, DEVICES, stride=3), :] = ids_ref[...]
    leave.wait()


def direction_body(
    src_ref, xn_ref, d_ref, c_ref, gr_ref, poc_ref, beta_ref, nn_ref, sn_ref, cn_ref,
    do_ref, db_s, ee_s, es_s, leak_s,
):
    edges(c_ref[...], ee_s, es_s)
    leak_s[...] = GROUND_LEAK * gr_ref[...].astype(F32)
    mix = mixer(beta_ref[...])
    for b in range(CR // 8):
        rows = slice(8 * b, 8 * b + 8)
        step = mixed(mix, d_ref[:, rows, :].reshape(128, CC))
        db_s[:, rows, :] = step.reshape(16, 8, CC)
    lane = iota((CR, 128), 1)

    def field_step(k, carry):
        v = xn_ref[k]
        total = operate(v, ee_s, es_s, leak_s)
        outer = outer_columns(cn_ref[...], k, lane)
        patch = src_ref[k]
        for half in range(2):
            at = slice(128 * half, 128 * half + 128)
            source = jnp.where(poc_ref[half] == patch, SOURCE_AMPS, 0.0)
            do_ref[k, :, at] = (source - (total[:, at] + outer[half])) + db_s[k, :, at]
        do_ref[k, 0:1, :] -= nn_ref[pl.ds(k, 1), :]
        do_ref[k, CR - 1 : CR, :] -= sn_ref[pl.ds(k, 1), :]
        return carry

    lax.fori_loop(0, K, field_step, 0)


def owner_body(msg_ref, out_ref, ids_s):
    me = lax.axis_index("row") * lax.axis_size("col") + lax.axis_index("col")
    values = stack2(
        msg_ref[pl.ds(0, DEVICES, stride=3), :].T, msg_ref[pl.ds(1, DEVICES, stride=3), :].T
    )
    ids_s[...] = msg_ref[pl.ds(2, DEVICES, stride=3), :].T
    ids = ids_s[pl.ds(pl.multiple_of(jnp.bitwise_and(me, 7) * 16, 16), 16), :]
    patch = iota((PATCH_DEV, 256), 0).astype(F32)
    total = jnp.zeros((32, PATCH_DEV), F32)
    for e in range(0, SLOTS, 2):
        pair = jnp.concatenate(
            [values[16 * e : 16 * e + 16], values[16 * e + 16 : 16 * e + 32]], axis=1
        )
        at = jnp.concatenate([ids[e : e + 1], ids[e + 1 : e + 2]], axis=1)
        total = total + dot(stack2(*split(pair)), one_hot(patch == at), 1, 1)
    out_ref[...] = total[0:16] + total[16:32]


def neighbours(value, axis, which):
    count = lax.axis_size(axis)
    starts = range(which, count - 1, 2)
    return lax.ppermute(value, axis, [(i, i + 1) for i in starts] + [(i + 1, i) for i in starts])


def on_device(iterate, direction, conductance, ground, local_patch, tile_patches, sources):
    vmem = pl.BlockSpec(memory_space=pltpu.VMEM)
    smem = pl.BlockSpec(memory_space=pltpu.SMEM)
    hbm = pl.BlockSpec(memory_space=pltpu.HBM)
    order = pl.BlockSpec(memory_space=pl.ANY)
    field = pltpu.VMEM((K, CR, CC), F32)
    halves = pltpu.VMEM((2, K, CR, 128), F32)
    plane = pltpu.VMEM((CR, CC), F32)

    first, second = call(
        rows_body,
        (f32(40, CC), f32(40, CC)),
        scratch=[
            pltpu.VMEM((2, K, 8, CC), F32),
            pltpu.VMEM((2, K, 8, CC), F32),
            pltpu.VMEM((2, 8, CC), F32),
            pltpu.SemaphoreType.DMA((2, 3)),
        ],
        specs=[hbm] * 3,
        vmem=60 * 1024 * 1024,
        moved=600_000,
    )(iterate, direction, conductance)
    far_first = neighbours(first, "row", 0)
    far_second = neighbours(second, "row", 1)
    patch_of_cell, slots, ids = call(
        patches_body,
        (i32(2, CR, 128), i32(8, CC), f32(DEVICES, 128)),
        scratch=[pltpu.VMEM((2, CR, 128), jnp.int32)],
        specs=[vmem] * 2 + [order],
        moved=10_000_000,
    )(local_patch, tile_patches, first)

    columns, x_held, d_held = call(
        columns_body,
        (f32(CR, 128), f32(K, CR, CC), f32(K, CR, CC)),
        specs=[vmem] * 3 + [order],
        moved=8_000_000,
    )(iterate, direction, conductance, slots)
    cols_first = neighbours(columns, "col", 0)
    cols_second = neighbours(columns, "col", 1)

    gram, nf, sf, cf = call(
        products_body,
        (f32(8 * DEVICES, 128), f32(32, CC), f32(32, CC), f32(CR, 128)),
        scratch=[field, field, plane, plane, plane],
        specs=[smem] + [vmem] * 12,
        moved=20_000_000,
    )(
        sources, x_held, d_held, conductance, ground, patch_of_cell,
        first, second, far_first, far_second, columns, cols_first, cols_second,
    )
    gram = lax.all_to_all(gram, AXES, 0, 0, tiled=True)

    new_iterate, message, beta, nn, sn, cn = call(
        iterate_body,
        (f32(K, CR, CC), f32(DEVICES * 3, 128), f32(128, 128), f32(16, CC), f32(16, CC), f32(CR, 128)),
        scratch=[
            field,
            halves,
            halves,
            plane,
            plane,
            pltpu.VMEM((2, 128, 128), F32),
            pltpu.VMEM((128, 128), F32),
            pltpu.SemaphoreType.DMA(()),
        ],
        specs=[vmem] * 9,
        places=(hbm,) + (vmem,) * 5,
        moved=20_000_000,
    )(gram, x_held, d_held, conductance, slots, ids, nf, sf, cf)
    received = lax.all_to_all(message.reshape(DEVICES, 1, 384), AXES, 0, 0, tiled=True)
    new_direction = call(
        direction_body,
        f32(K, CR, CC),
        scratch=[field, plane, plane, plane],
        specs=[smem] + [vmem] * 9,
        moved=20_000_000,
    )(sources, new_iterate, direction, conductance, ground, patch_of_cell, beta, nn, sn, cn)
    migration = call(
        owner_body,
        f32(K, PATCH_DEV),
        scratch=[pltpu.VMEM((128, 128), F32)],
        specs=[vmem],
        moved=1_000_000,
    )(received.reshape(DEVICES * 3, 128))
    return new_iterate, new_direction, migration


def solution(mesh):
    in_specs = (
        P(None, "row", "col"),
        P(None, "row", "col"),
        P("row", "col"),
        P("row", "col"),
        P("row", "col"),
        P("row", "col", None),
        P(),
    )
    out_specs = (P(None, "row", "col"), P(None, "row", "col"), P(None, ("row", "col")))
    return jax.shard_map(
        on_device, mesh=mesh, in_specs=in_specs, out_specs=out_specs, check_vma=False
    )
```

time: 99.6 us -> 82 us (0.82)
  starting transfers between devices: 27.7 us -> 13.7 us
  waiting for transfers between devices: 8.06 us -> 4.26 us
  local copies, waits for them, and re-layouts: 6.56 us -> 3.98 us
  blocking collectives: 23.5 us -> 25.3 us
  Pallas kernels: 31.9 us -> 33.6 us
    ppermute x11 -> x4, starting transfers between devices: 27.7 us -> 9.09 us  [neighbours(): lax.ppermute(value, axis, [(i, i + 1) for i in starts] + [(i + 1, i) for...]
    ppermute x11 -> x4, waiting for transfers between devices: 8.06 us -> 1.4 us  [neighbours(): lax.ppermute(value, axis, [(i, i + 1) for i in starts] + [(i + 1, i) for...]
    all_to_all x0 -> x1, starting transfers between devices: none -> 4.59 us  [on_device(): lax.all_to_all(message.reshape(DEVICES, 1, 384), AXES, 0, 0, tiled=True)]
    all_to_all x0 -> x1, waiting for transfers between devices: none -> 2.86 us  [on_device(): lax.all_to_all(message.reshape(DEVICES, 1, 384), AXES, 0, 0, tiled=True)]
    unnamed x24 -> x22, local copies, waits for them, and re-layouts: 6.22 us -> 3.98 us
    pallas_call x5 -> x7, Pallas kernels: 31.9 us -> 33.6 us  [the longest x1 12.4 us: on_device(): call(iterate_body, (f32(K, CR, CC), f32(DEVICES * 3, 128), f32(128, 128),...]
    all_to_all x1, blocking collectives: 23.5 us -> 25.3 us  [on_device(): gram = lax.all_to_all(gram, AXES, 0, 0, tiled=True)]
  transfers between devices with their start and end apart: 11 -> 5, of which waited for: 7 -> 2; matrix products, arithmetic and copies ran while one was open for 1% -> 0% of each run, Pallas kernels for 2% -> 7%
where the time goes in v2:
time: 82 us; the launch traced here: 81.6 us
  Pallas kernels  33.6 us (41%)
  blocking collectives  25.3 us (31%)
  starting transfers between devices  13.7 us (17%)
  waiting for transfers between devices  4.26 us (5%)
  local copies, waits for them, and re-layouts  3.98 us (5%)
    all_to_all x1, blocking collectives, on_device(): gram = lax.all_to_all(gram, AXES, 0, 0, tiled=True)  25.3 us
    pallas_call x1, Pallas kernels, on_device(): call(iterate_body, (f32(K, CR, CC), f32(DEVICES * 3, 128), f32(128, 128),...  12.4 us
    pallas_call x1, Pallas kernels, on_device(): call(products_body, (f32(8 * DEVICES, 128), f32(32, CC), f32(32, CC), f32...  9.36 us
    ppermute x4, starting transfers between devices, neighbours(): lax.ppermute(value, axis, [(i, i + 1) for i in starts] + [(i + 1, i) for...  9.09 us
    pallas_call x1, Pallas kernels, on_device(): call(direction_body, f32(K, CR, CC), scratch=[field, plane, plane, plane]...  6.1 us
    all_to_all x1, starting transfers between devices, on_device(): lax.all_to_all(message.reshape(DEVICES, 1, 384), AXES, 0, 0, tiled=True)  4.59 us
    unnamed x22, local copies, waits for them, and re-layouts  3.98 us
    all_to_all x1, waiting for transfers between devices, on_device(): lax.all_to_all(message.reshape(DEVICES, 1, 384), AXES, 0, 0, tiled=True)  2.86 us
  transfers between devices with their start and end apart: 5, of which 2 were waited for; matrix products, arithmetic and copies ran while one was open for 0% of the time, Pallas kernels for 7%

profile of v2, /device:TPU:1, one launch (start us, length us, event | category | flops | bytes accessed | tf_op | source)
XLA Modules:
  0.0 81.6 jit_solution(4892913596124391484)
XLA Ops:
  0.7 2.0 %shard_map.94 = (f32[40,256]{1,0:T(8,128)}, f32[40,256]{1,0:T(8,128)}) custom-call(f32[16,128,256]{2,1,0:T(8,128)} %x_ref.3, f32[16,128,256]{2,1,0:T(8,128)} %d_ref.5, f32[128,256]{1,0:T(8,128)} %c_ref.9), custom_call_target="tpu_custom_call" | custom-call | bytes 600000 | tf_op jit(solution)/shard_map/pallas_call | solution.py:425
  2.7 0.0 copy-start.5
  2.7 0.8 copy-done.5
  3.5 1.7 %shard_map.95 = (s32[2,128,128]{2,1,0:T(8,128)S(1)}, s32[8,256]{1,0:T(8,128)S(1)}, f32[128,128]{1,0:T(8,128)S(1)}) custom-call(s32[128,256]{1,0:T(8,128)S(1)} %copy-done.7, s32[1,1,2048]{2,1,0:T(1,128)S(1)} %copy-done.9, f32[40,256]{1,0:T(8,128)S(1)} %copy-done.5), custom_call_target="tpu_custom_call" | custom-call | bytes 10000000 | tf_op jit(solution)/shard_map/pallas_call | solution.py:440
  5.2 0.0 copy-start.1
  5.2 1.6 %copy-done.1 = f32[16,128,256]{2,1,0:T(8,128)S(1)} copy-done((f32[16,128,256]{2,1,0:T(8,128)S(1)}, f32[16,128,256]{2,1,0:T(8,128)}, u32[]{:S(2)}) %copy-start.1) | copy-done | bytes 2097176
  6.8 0.7 shard_map.96
  7.5 4.6 %collective-permute-start.3 = (f32[128,128]{1,0:T(8,128)S(1)}, f32[128,128]{1,0:T(8,128)S(1)}, u32[]{:S(2)}, u32[]{:S(2)}) collective-permute-start(f32[128,128]{1,0:T(8,128)S(1)} %get-tuple-element.27.cols_ref), channel_id=1, source_target_pairs={{1,2},{3,4},{5,6},{2,1},{4,3},{6,5},{9,10},{11,12},{13,14},{10,9},... | collective-permute-start | bytes 196616 | tf_op jit(solution)/shard_map/ppermute | solution.py:413
  12.1 0.1 collective-permute-start.2
  12.2 0.7 collective-permute-start.1
  12.9 3.7 %collective-permute-start = (f32[40,256]{1,0:T(8,128)S(1)}, f32[40,256]{1,0:T(8,128)S(1)}, u32[]{:S(2)}, u32[]{:S(2)}) collective-permute-start(f32[40,256]{1,0:T(8,128)S(1)} %copy-done.6), channel_id=1, source_target_pairs={{0,8},{16,24},{32,40},{48,56},{64,72},{80,88},{96,104},{112,120},{... | collective-permute-start | bytes 122888 | tf_op jit(solution)/shard_map/ppermute | solution.py:413
  16.6 0.0 collective-permute-done.1.far_second_ref
  16.6 1.4 %collective-permute-done.far_first_ref = f32[40,256]{1,0:T(8,128)S(1)} collective-permute-done((f32[40,256]{1,0:T(8,128)S(1)}, f32[40,256]{1,0:T(8,128)S(1)}, u32[]{:S(2)}, u32[]{:S(2)}) %collective-permute-start) | collective-permute-done | bytes 40992 | tf_op jit(solution)/shard_map/ppermute | solution.py:413
  18.0 0.0 collective-permute-done.3.cols_second_ref
  18.0 0.0 collective-permute-done.2.cols_first_ref
  18.0 9.4 %shard_map.97 = (f32[1024,128]{1,0:T(8,128)S(1)}, f32[32,256]{1,0:T(8,128)S(1)}, f32[32,256]{1,0:T(8,128)S(1)}, f32[128,128]{1,0:T(8,128)S(1)}) custom-call(s32[16]{0:T(128)S(1)} %copy-done.10, f32[16,128,256]{2,1,0:T(8,128)S(1)} %get-tuple-element.23.x_ref, f32[16,128,256]{2,1,0:T(8,128)S(1)} %get-tuple-element.24.d_ref, f32[128,256]{1,0:T(8,128)S(1)} %copy-done.2, ...), custom_call_target="tpu_custom_call" | custom-call | bytes 20000000 | tf_op jit(solution)/shard_map/pallas_call | solution.py:457
  27.4 25.3 %all_to_all.16 = f32[128,8,128]{2,1,0:T(8,128)S(1)} all-to-all(f32[128,8,128]{2,1,0:T(8,128)S(1)} %bitcast.6), channel_id=1, replica_groups=mesh['row'=16,'col'=8] {'row','col'}, dimensions={0} | all-to-all | bytes 1048576 | tf_op jit(solution)/shard_map/all_to_all | solution.py:467
  52.7 12.4 %shard_map.98 = (f32[16,128,256]{2,1,0:T(8,128)}, f32[384,128]{1,0:T(8,128)}, f32[128,128]{1,0:T(8,128)S(1)}, f32[16,256]{1,0:T(8,128)S(1)}, f32[16,256]{1,0:T(8,128)S(1)}, /*index=5*/f32[128,128]{1,0:T(8,128)S(1)}) custom-call(f32[1024,128]{1,0:T(8,128)S(1)} %bitcast.4, f32[16,128,256]{2,1,0:T(8,128)S(1)} %get-tuple-element.23.x_ref, ...), custom_call_target="tpu_custom_call" | custom-call | bytes 20000000 | tf_op jit(solution)/shard_map/pallas_call | solution.py:469
  65.0 4.6 %all-to-all-start.1 = ((f32[128,1,384]{2,1,0:T(1,128)}), f32[128,1,384]{2,1,0:T(1,128)S(1)}, u32[]{:S(2)}, u32[]{:S(2)}) async-start(f32[128,1,384]{2,1,0:T(1,128)} %bitcast.2), calls=%async_computation.1 | async-start | bytes 393216 | tf_op jit(solution)/shard_map/all_to_all | solution.py:486
  69.6 0.0 copy-start.3
  69.6 1.6 %copy-done.3 = f32[16,128,256]{2,1,0:T(8,128)S(1)} copy-done((f32[16,128,256]{2,1,0:T(8,128)S(1)}, f32[16,128,256]{2,1,0:T(8,128)}, u32[]{:S(2)}) %copy-start.3) | copy-done | bytes 2097176
  71.2 6.1 %shard_map.99 = f32[16,128,256]{2,1,0:T(8,128)} custom-call(s32[16]{0:T(128)S(1)} %copy-done.10, f32[16,128,256]{2,1,0:T(8,128)S(1)} %copy-done.3, f32[16,128,256]{2,1,0:T(8,128)S(1)} %copy-done, f32[128,256]{1,0:T(8,128)S(1)} %copy-done.2, s32[128,256]{1,0:T(8,128)S(1)} %copy-done.4, s32[2,128,128]{2,1,0:T(8,128)S(1)} %get-tuple-element.25.poc_ref, ...), custom_call_target="tpu_custom_call" | custom-call | bytes 20000000 | tf_op jit(solution)/shard_map/pallas_call | solution.py:487
  77.3 2.9 %all-to-all-done.1 = f32[128,1,384]{2,1,0:T(1,128)S(1)} async-done(((f32[128,1,384]{2,1,0:T(1,128)}), f32[128,1,384]{2,1,0:T(1,128)S(1)}, u32[]{:S(2)}, u32[]{:S(2)}) %all-to-all-start.1) | async-done | bytes 196640 | tf_op jit(solution)/shard_map/all_to_all | solution.py:486
  80.2 1.4 %shard_map.100 = f32[16,512]{1,0:T(8,128)} custom-call(f32[384,128]{1,0:T(8,128)S(1)} %bitcast.5), custom_call_target="tpu_custom_call" | custom-call | bytes 1000000 | tf_op jit(solution)/shard_map/pallas_call | solution.py:494
  (16 shorter events, 0.0 us)
Async XLA Ops:
  0.6 4.6 %copy-start.2 = (f32[128,256]{1,0:T(8,128)S(1)}, f32[128,256]{1,0:T(8,128)}, u32[]{:S(2)}) copy-start(f32[128,256]{1,0:T(8,128)} %c_ref.9) | copy-start | bytes 393220
  0.6 4.6 %copy-start = (f32[16,128,256]{2,1,0:T(8,128)S(1)}, f32[16,128,256]{2,1,0:T(8,128)}, u32[]{:S(2)}) copy-start(f32[16,128,256]{2,1,0:T(8,128)} %d_ref.5) | copy-start | bytes 6291460
  0.7 2.0 %copy-start.9 = (s32[1,1,2048]{2,1,0:T(1,128)S(1)}, s32[1,1,2048]{2,1,0:T(1,128)}, u32[]{:S(2)}) copy-start(s32[1,1,2048]{2,1,0:T(1,128)} %tp_ref.1) | copy-start | bytes 24580
  0.7 2.0 %copy-start.7 = (s32[128,256]{1,0:T(8,128)S(1)}, s32[128,256]{1,0:T(8,128)}, u32[]{:S(2)}) copy-start(s32[128,256]{1,0:T(8,128)} %lp_ref.1) | copy-start | bytes 393220
  2.7 0.8 copy-start.5
  5.2 1.6 %copy-start.1 = (f32[16,128,256]{2,1,0:T(8,128)S(1)}, f32[16,128,256]{2,1,0:T(8,128)}, u32[]{:S(2)}) copy-start(f32[16,128,256]{2,1,0:T(8,128)} %x_ref.3) | copy-start | bytes 6291460
  6.8 5.4 %copy-start.8 = (f32[40,256]{1,0:T(8,128)S(1)}, f32[40,256]{1,0:T(8,128)}, u32[]{:S(2)}) copy-start(f32[40,256]{1,0:T(8,128)} %get-tuple-element.26.own_second_ref) | copy-start | bytes 122884
  6.8 6.0 %copy-start.6 = (f32[40,256]{1,0:T(8,128)S(1)}, f32[40,256]{1,0:T(8,128)}, u32[]{:S(2)}) copy-start(f32[40,256]{1,0:T(8,128)} %get-tuple-element.21.after_ref.own_first_ref) | copy-start | bytes 122884
  6.8 11.2 %copy-start.4 = (s32[128,256]{1,0:T(8,128)S(1)}, s32[128,256]{1,0:T(8,128)}, u32[]{:S(2)}) copy-start(s32[128,256]{1,0:T(8,128)} %gr_ref.3) | copy-start | bytes 393220
  6.8 11.2 %copy-start.10 = (s32[16]{0:T(128)S(1)}, s32[16]{0:T(128)}, u32[]{:S(2)}) copy-start(s32[16]{0:T(128)} %src_ref.3) | copy-start | bytes 196
  7.5 10.5 %collective-permute-start.3 = (f32[128,128]{1,0:T(8,128)S(1)}, f32[128,128]{1,0:T(8,128)S(1)}, u32[]{:S(2)}, u32[]{:S(2)}) collective-permute-start(f32[128,128]{1,0:T(8,128)S(1)} %get-tuple-element.27.cols_ref), channel_id=1, source_target_pairs={{1,2},{3,4},{5,6},{2,1},{4,3},{6,5},{9,10},{11,12},{13,14},{10,9},... | collective-permute-start | bytes 196616 | tf_op jit(solution)/shard_map/ppermute | solution.py:413
  12.1 5.9 %collective-permute-start.2 = (f32[128,128]{1,0:T(8,128)S(1)}, f32[128,128]{1,0:T(8,128)S(1)}, u32[]{:S(2)}, u32[]{:S(2)}) collective-permute-start(f32[128,128]{1,0:T(8,128)S(1)} %get-tuple-element.27.cols_ref), channel_id=1, source_target_pairs={{0,1},{2,3},{4,5},{6,7},{1,0},{3,2},{5,4},{7,6},{8,9},{10,11},{12,... | collective-permute-start | bytes 196616 | tf_op jit(solution)/shard_map/ppermute | solution.py:413
  12.2 4.4 %collective-permute-start.1 = (f32[40,256]{1,0:T(8,128)S(1)}, f32[40,256]{1,0:T(8,128)S(1)}, u32[]{:S(2)}, u32[]{:S(2)}) collective-permute-start(f32[40,256]{1,0:T(8,128)S(1)} %copy-done.8), channel_id=1, source_target_pairs={{8,16},{24,32},{40,48},{56,64},{72,80},{88,96},{104,112},{16,8},{3... | collective-permute-start | bytes 122888 | tf_op jit(solution)/shard_map/ppermute | solution.py:413
  12.9 5.1 %collective-permute-start = (f32[40,256]{1,0:T(8,128)S(1)}, f32[40,256]{1,0:T(8,128)S(1)}, u32[]{:S(2)}, u32[]{:S(2)}) collective-permute-start(f32[40,256]{1,0:T(8,128)S(1)} %copy-done.6), channel_id=1, source_target_pairs={{0,8},{16,24},{32,40},{48,56},{64,72},{80,88},{96,104},{112,120},{... | collective-permute-start | bytes 122888 | tf_op jit(solution)/shard_map/ppermute | solution.py:413
  65.0 15.2 %all-to-all-start.1 = ((f32[128,1,384]{2,1,0:T(1,128)}), f32[128,1,384]{2,1,0:T(1,128)S(1)}, u32[]{:S(2)}, u32[]{:S(2)}) async-start(f32[128,1,384]{2,1,0:T(1,128)} %bitcast.2), calls=%async_computation.1 | async-start | bytes 393216 | tf_op jit(solution)/shard_map/all_to_all | solution.py:486
  69.6 1.6 %copy-start.3 = (f32[16,128,256]{2,1,0:T(8,128)S(1)}, f32[16,128,256]{2,1,0:T(8,128)}, u32[]{:S(2)}) copy-start(f32[16,128,256]{2,1,0:T(8,128)} %get-tuple-element.18.xn_ref) | copy-start | bytes 6291460

commit v3 on v2

--- a/solution.py
+++ b/solution.py
@@ -66,43 +66,28 @@
     return jax.ShapeDtypeStruct(shape, jnp.int32)
 
 
-def rows_body(x_ref, d_ref, c_ref, first_ref, second_ref, x_s, d_s, c_s, sems):
-    copies = []
-    for at, row in ((0, 0), (1, CR - 8)):
-        for n, (ref, buf) in enumerate(((x_ref, x_s), (d_ref, d_s))):
-            copies.append(pltpu.make_async_copy(ref.at[:, pl.ds(row, 8), :], buf.at[at], sems.at[at, n]))
-        copies.append(pltpu.make_async_copy(c_ref.at[pl.ds(row, 8), :], c_s.at[at], sems.at[at, 2]))
+def front_body(x_ref, d_ref, c_ref, first_ref, second_ref, cols_ref, xv_ref, dv_ref, c_s, sems):
+    pairs = [(x_ref.at[k], xv_ref.at[k]) for k in range(K)]
+    pairs += [(d_ref.at[k], dv_ref.at[k]) for k in range(K)]
+    pairs += [(c_ref, c_s)]
+    copies = [pltpu.make_async_copy(*pair, sems.at[f]) for f, pair in enumerate(pairs)]
     for copy in copies:
         copy.start()
-    for copy in copies:
-        copy.wait()
     even = jnp.bitwise_and(lax.axis_index("row"), 1) == 0
-
-    def pack(x0, d0, c0, x1, d1, c1, out):
-        out[0:16, :] = jnp.where(even, x1, x0)
-        out[16:32, :] = jnp.where(even, d1, d0)
-        out[32:40, :] = jnp.broadcast_to(jnp.where(even, c1, c0), (8, CC))
-
-    top = (x_s[0, :, 0, :], d_s[0, :, 0, :], c_s[0, 0:1, :])
-    bottom = (x_s[1, :, 7, :], d_s[1, :, 7, :], c_s[1, 7:8, :])
-    pack(*top, *bottom, first_ref)
-    pack(*bottom, *top, second_ref)
-
-
-def columns_body(x_ref, d_ref, c_ref, after_ref, out_ref, xv_ref, dv_ref):
     lane = iota((CR, 128), 1)
     packed = jnp.zeros((CR, 128), F32)
-    for f in range(33):
-        ref = x_ref.at[f] if f < 16 else (d_ref.at[f - 16] if f < 32 else c_ref)
-        west = ref[:, 0:128]
-        east = ref[:, 128:256]
-        if f < 32:
-            kept = xv_ref if f < 16 else dv_ref
-            kept[f % 16, :, 0:128] = west
-            kept[f % 16, :, 128:256] = east
-        both = pltpu.roll(jnp.where(lane == 127, east, west), 2 * f + 1, 1)
+    for f, copy in enumerate(copies):
+        copy.wait()
+        ref = pairs[f][1]
+        top = ref[0:1, :]
+        bottom = ref[CR - 1 : CR, :]
+        first_ref[f : f + 1, :] = jnp.where(even, bottom, top)
+        second_ref[f : f + 1, :] = jnp.where(even, top, bottom)
+        both = pltpu.roll(jnp.where(lane == 127, ref[:, 128:256], ref[:, 0:128]), 2 * f + 1, 1)
         packed = jnp.where((lane >> 1) == f, both, packed)
-    out_ref[...] = packed
+    for ref in (first_ref, second_ref):
+        ref[33:40, :] = jnp.zeros((7, CC), F32)
+    cols_ref[...] = packed
 
 
 def patches_body(lp_ref, tp_ref, after_ref, poc_ref, slot_ref, ids_ref, lp_s):
@@ -151,16 +136,23 @@
     south_ref[...] = jnp.where(iota((CR, CC), 0) == CR - 1, 0.0, south)
 
 
-def operate(v, ee_s, es_s, leak_s):
-    flow = ee_s[...] * (v - pltpu.roll(v, CC - 1, 1))
-    total = flow - pltpu.roll(flow, 1, 1) + leak_s[...] * v
+def turn_columns(flows, field):
+    return pltpu.roll(flows, lax.rem(127 - 2 * field + 128, 128), 1)
+
+
+def operate(v, outer, ee_s, es_s, leak_s):
+    lane = iota((CR, 128), 1)
+    a = v[:, 0:128]
+    b = v[:, 128:256]
+    after = pltpu.roll(b, 127, 1)
+    flow_a = ee_s[:, 0:128] * (a - jnp.where(lane == 127, after, pltpu.roll(a, 127, 1)))
+    flow_b = jnp.where(lane == 127, outer, ee_s[:, 128:256] * (b - after))
+    before = pltpu.roll(flow_a, 1, 1)
+    total_a = flow_a - jnp.where(lane == 0, -outer, before)
+    total_b = flow_b - jnp.where(lane == 0, before, pltpu.roll(flow_b, 1, 1))
     flow = es_s[...] * (v - pltpu.roll(v, CR - 1, 0))
-    return total + flow - pltpu.roll(flow, 1, 0)
-
-
-def outer_columns(flows, field, lane):
-    turned = pltpu.roll(flows, lax.rem(127 - 2 * field + 128, 128), 1)
-    return jnp.where(lane == 0, turned, 0.0), jnp.where(lane == 127, turned, 0.0)
+    down = (flow - pltpu.roll(flow, 1, 0)) + leak_s[...] * v
+    return total_a + down[:, 0:128], total_b + down[:, 128:256]
 
 
 def products_body(
@@ -191,17 +183,15 @@
     cf_ref[...] = jnp.where(lane < 64, edge * (own - far), 0.0)
 
     def field_step(k, carry):
-        total = operate(d_ref[k], ee_s, es_s, leak_s)
-        west, east = outer_columns(cf_ref[...], k + 16, lane)
-        q_s[k, :, 0:128] = total[:, 0:128] + west
-        q_s[k, :, 128:256] = total[:, 128:256] + east
+        image = operate(d_ref[k], turn_columns(cf_ref[...], k + 16), ee_s, es_s, leak_s)
+        part = operate(x_ref[k], turn_columns(cf_ref[...], k), ee_s, es_s, leak_s)
+        patch = src_ref[k]
+        for half in range(2):
+            at = slice(128 * half, 128 * half + 128)
+            q_s[k, :, at] = image[half]
+            r_s[k, :, at] = jnp.where(poc_ref[half] == patch, SOURCE_AMPS, 0.0) - part[half]
         q_s[k, 0:1, :] += nf_ref[pl.ds(k + 16, 1), :]
         q_s[k, CR - 1 : CR, :] += sf_ref[pl.ds(k + 16, 1), :]
-        total = operate(x_ref[k], ee_s, es_s, leak_s)
-        west, east = outer_columns(cf_ref[...], k, lane)
-        patch = src_ref[k]
-        r_s[k, :, 0:128] = jnp.where(poc_ref[0] == patch, SOURCE_AMPS, 0.0) - (total[:, 0:128] + west)
-        r_s[k, :, 128:256] = jnp.where(poc_ref[1] == patch, SOURCE_AMPS, 0.0) - (total[:, 128:256] + east)
         r_s[k, 0:1, :] -= nf_ref[pl.ds(k, 1), :]
         r_s[k, CR - 1 : CR, :] -= sf_ref[pl.ds(k, 1), :]
         return carry
@@ -244,7 +234,7 @@
 def iterate_body(
     gram_ref, x_ref, d_ref, c_ref, slot_ref, ids_ref, nf_ref, sf_ref, cf_ref,
     out_ref, msg_ref, beta_ref, nn_ref, sn_ref, cn_ref,
-    xn_ref, fe_s, cs_s, ee_s, es_s, bs_s, turn_s, sem,
+    xn_ref, cur_s, ee_s, es_s, turn_s, sem,
 ):
     edges(c_ref[...], ee_s, es_s)
     packed = gram_ref[...].reshape(DEVICES, 8, 128).sum(axis=0)
@@ -300,60 +290,46 @@
     def field_step(k, carry):
         v = xn_ref[k]
         flow = jnp.abs(ee_s[...] * (v - pltpu.roll(v, CC - 1, 1)))
-        fe_s[0, k] = flow[:, 0:128]
-        fe_s[1, k] = flow[:, 128:256]
+        total = flow + pltpu.roll(flow, 1, 1)
         flow = jnp.abs(es_s[...] * (v - pltpu.roll(v, CR - 1, 0)))
-        flow = flow + pltpu.roll(flow, 1, 0)
-        north = jnp.abs(nn_ref[pl.ds(k, 1), :])
-        south = jnp.abs(sn_ref[pl.ds(k, 1), :])
-        for half in range(2):
-            at = slice(128 * half, 128 * half + 128)
-            cs_s[half, k] = flow[:, at]
-            cs_s[half, k, 0:1, :] += north[:, at]
-            cs_s[half, k, CR - 1 : CR, :] += south[:, at]
+        cur_s[k] = total + (flow + pltpu.roll(flow, 1, 0))
+        cur_s[k, 0:1, :] += jnp.abs(nn_ref[pl.ds(k, 1), :])
+        cur_s[k, CR - 1 : CR, :] += jnp.abs(sn_ref[pl.ds(k, 1), :])
         return carry
 
     lax.fori_loop(0, K, field_step, 0)
+    take = iota((32, 256), 0)
+    given = iota((32, 256), 1) & 127
+    rows_of = one_hot(((given >> 3) == (take & 15)) & (((given >> 2) & 1) == (take >> 4)))
+    strips = []
+    for b in range(CR // 8):
+        high, low = split(cur_s[:, 8 * b : 8 * b + 8, :].reshape(128, CC))
+        both = dot(rows_of, stack2(high, low))
+        strips += [both[0:16], both[16:32]]
     cell = iota((CC, CC), 0)
     spot = iota((CC, CC), 1)
     blocks = jnp.zeros((128, CC), F32)
     for q in range(4):
-
-        def pool(ref):
-            halves = []
-            for half in range(2):
-                rows = [ref[half, :, pl.ds(4 * q + r, 8, stride=16), :] for r in range(4)]
-                halves.append(((rows[0] + rows[1]) + (rows[2] + rows[3])).reshape(128, 128))
-            return split(jnp.concatenate(halves, axis=1))
-
-        here = jnp.where(spot == q * 64 + (cell >> 2), 1.0, 0.0)
-        ahead = jnp.where(spot == q * 64 + ((cell + 1) >> 2), 1.0, 0.0)
-        ahead = jnp.where((cell & 3) == 3, jnp.where(((cell + 1) >> 2) < 64, ahead, 0.0), ahead)
-        along = (here + ahead).astype(BF16)
-        here = here.astype(BF16)
-        high, low = pool(fe_s)
-        blocks = blocks + (dot(high, along) + dot(low, along))
-        high, low = pool(cs_s)
-        blocks = blocks + (dot(high, here) + dot(low, here))
-    bs_s[0] = blocks[:, 0:128]
-    bs_s[1] = blocks[:, 128:256]
+        high, low = split(jnp.concatenate([strips[4 * i + q] for i in range(8)], axis=0))
+        spread = one_hot(spot == q * 64 + (cell >> 2))
+        blocks = blocks + (dot(high, spread) + dot(low, spread))
     outer = jnp.concatenate(
         [turn_s[pl.ds(1, 16, stride=2), :], turn_s[pl.ds(0, 16, stride=2), :]], axis=1
     )
     outer = stack2(*split(outer))
     target = ((cell >> 2) & 3) * 64 + jnp.where(cell < 128, 0, 63)
     band = (cell & 127) >> 4
-    entry = iota((2048, CC), 0)
-    sums = jnp.zeros((32, 2048), F32)
+    owner = iota((128, CC), 0)
+    stacked = jnp.zeros((256, 128), F32)
     for b in range(8):
-        every = pl.ds(b, 16, stride=8)
         rim = dot(outer, one_hot((spot == target) & (band == b)))
-        rim = rim[0:16] + rim[16:32]
-        inner = jnp.concatenate([bs_s[0, every, :], bs_s[1, every, :]], axis=1)
-        place = one_hot(entry == slot_ref[b : b + 1, :])
-        sums = sums + dot(stack2(*split(0.5 * (inner + rim))), place, 1, 1)
-    sums = sums[0:16] + sums[16:32]
-    stacked = jnp.concatenate([sums[:, 128 * e : 128 * e + 128] for e in range(SLOTS)], axis=0)
+        inner = 0.5 * (blocks[16 * b : 16 * b + 16] + (rim[0:16] + rim[16:32]))
+        slot = slot_ref[b : b + 1, :]
+        entry = jnp.broadcast_to(slot >> 7, (16, CC))
+        spread = jnp.concatenate([jnp.where(entry == e, inner, 0.0) for e in range(SLOTS)], axis=0)
+        high, low = split(spread)
+        place = one_hot(owner == (slot & 127))
+        stacked = stacked + (dot(high, place, 1, 1) + dot(low, place, 1, 1))
     msg_ref[pl.ds(0, DEVICES, stride=3), :] = stacked[0:128].T
     msg_ref[pl.ds(1, DEVICES, stride=3), :] = stacked[128:256].T
     msg_ref[pl.ds(2, DEVICES, stride=3), :] = ids_ref[...]
@@ -371,17 +347,14 @@
         rows = slice(8 * b, 8 * b + 8)
         step = mixed(mix, d_ref[:, rows, :].reshape(128, CC))
         db_s[:, rows, :] = step.reshape(16, 8, CC)
-    lane = iota((CR, 128), 1)
 
     def field_step(k, carry):
-        v = xn_ref[k]
-        total = operate(v, ee_s, es_s, leak_s)
-        outer = outer_columns(cn_ref[...], k, lane)
+        total = operate(xn_ref[k], turn_columns(cn_ref[...], k), ee_s, es_s, leak_s)
         patch = src_ref[k]
         for half in range(2):
             at = slice(128 * half, 128 * half + 128)
             source = jnp.where(poc_ref[half] == patch, SOURCE_AMPS, 0.0)
-            do_ref[k, :, at] = (source - (total[:, at] + outer[half])) + db_s[k, :, at]
+            do_ref[k, :, at] = (source - total[half]) + db_s[k, :, at]
         do_ref[k, 0:1, :] -= nn_ref[pl.ds(k, 1), :]
         do_ref[k, CR - 1 : CR, :] -= sn_ref[pl.ds(k, 1), :]
         return carry
@@ -396,15 +369,20 @@
     )
     ids_s[...] = msg_ref[pl.ds(2, DEVICES, stride=3), :].T
     ids = ids_s[pl.ds(pl.multiple_of(jnp.bitwise_and(me, 7) * 16, 16), 16), :]
-    patch = iota((PATCH_DEV, 256), 0).astype(F32)
-    total = jnp.zeros((32, PATCH_DEV), F32)
+    patch = iota((128, 256), 0)
+    total = jnp.zeros((64, 128), F32)
     for e in range(0, SLOTS, 2):
         pair = jnp.concatenate(
             [values[16 * e : 16 * e + 16], values[16 * e + 16 : 16 * e + 32]], axis=1
         )
-        at = jnp.concatenate([ids[e : e + 1], ids[e + 1 : e + 2]], axis=1)
-        total = total + dot(stack2(*split(pair)), one_hot(patch == at), 1, 1)
-    out_ref[...] = total[0:16] + total[16:32]
+        at = jnp.concatenate([ids[e : e + 1], ids[e + 1 : e + 2]], axis=1).astype(jnp.int32)
+        group = jnp.broadcast_to(at >> 7, (16, 256))
+        spread = jnp.concatenate([jnp.where(group == g, pair, 0.0) for g in range(4)], axis=0)
+        high, low = split(spread)
+        place = one_hot(patch == (at & 127))
+        total = total + (dot(high, place, 1, 1) + dot(low, place, 1, 1))
+    for g in range(4):
+        out_ref[:, 128 * g : 128 * g + 128] = total[16 * g : 16 * g + 16]
 
 
 def neighbours(value, axis, which):
@@ -419,40 +397,34 @@
     hbm = pl.BlockSpec(memory_space=pltpu.HBM)
     order = pl.BlockSpec(memory_space=pl.ANY)
     field = pltpu.VMEM((K, CR, CC), F32)
-    halves = pltpu.VMEM((2, K, CR, 128), F32)
     plane = pltpu.VMEM((CR, CC), F32)
 
-    first, second = call(
-        rows_body,
-        (f32(40, CC), f32(40, CC)),
-        scratch=[
-            pltpu.VMEM((2, K, 8, CC), F32),
-            pltpu.VMEM((2, K, 8, CC), F32),
-            pltpu.VMEM((2, 8, CC), F32),
-            pltpu.SemaphoreType.DMA((2, 3)),
-        ],
+    first, second, columns, x_held, d_held = call(
+        front_body,
+        (
+            pltpu.VMEM((40, CC), F32),
+            pltpu.VMEM((40, CC), F32),
+            pltpu.VMEM((CR, 128), F32),
+            field,
+            field,
+        ),
+        scratch=[plane, pltpu.SemaphoreType.DMA((33,))],
         specs=[hbm] * 3,
-        vmem=60 * 1024 * 1024,
-        moved=600_000,
-    )(iterate, direction, conductance)
+        places=(vmem,) * 5,
+        moved=8_000_000,
+    )(*[pltpu.with_memory_space_constraint(a, pltpu.HBM) for a in (iterate, direction, conductance)])
+    far_second = neighbours(second, "row", 1)
+    cols_second = neighbours(columns, "col", 1)
     far_first = neighbours(first, "row", 0)
-    far_second = neighbours(second, "row", 1)
+    cols_first = neighbours(columns, "col", 0)
+
     patch_of_cell, slots, ids = call(
         patches_body,
         (i32(2, CR, 128), i32(8, CC), f32(DEVICES, 128)),
         scratch=[pltpu.VMEM((2, CR, 128), jnp.int32)],
         specs=[vmem] * 2 + [order],
         moved=10_000_000,
-    )(local_patch, tile_patches, first)
-
-    columns, x_held, d_held = call(
-        columns_body,
-        (f32(CR, 128), f32(K, CR, CC), f32(K, CR, CC)),
-        specs=[vmem] * 3 + [order],
-        moved=8_000_000,
-    )(iterate, direction, conductance, slots)
-    cols_first = neighbours(columns, "col", 0)
-    cols_second = neighbours(columns, "col", 1)
+    )(local_patch, tile_patches, columns)
 
     gram, nf, sf, cf = call(
         products_body,
@@ -471,11 +443,9 @@
         (f32(K, CR, CC), f32(DEVICES * 3, 128), f32(128, 128), f32(16, CC), f32(16, CC), f32(CR, 128)),
         scratch=[
             field,
-            halves,
-            halves,
+            field,
             plane,
             plane,
-            pltpu.VMEM((2, 128, 128), F32),
             pltpu.VMEM((128, 128), F32),
             pltpu.SemaphoreType.DMA(()),
         ],

time: 82 us -> 77 us (0.939)
  blocking collectives: 25.3 us -> 28.2 us
  starting transfers between devices: 13.7 us -> 11.2 us
  local copies, waits for them, and re-layouts: 3.98 us -> 1.61 us
  Pallas kernels: 33.6 us -> 31.9 us
  waiting for transfers between devices: 4.26 us -> 3.04 us
    all_to_all x1, blocking collectives: 25.3 us -> 28.2 us  [on_device(): gram = lax.all_to_all(gram, AXES, 0, 0, tiled=True)]
    pallas_call x1, Pallas kernels: 12.4 us -> 9.84 us  [on_device(): call(iterate_body, (f32(K, CR, CC), f32(DEVICES * 3, 128), f32(128, 128),...]
    ppermute x4, starting transfers between devices: 9.09 us -> 6.62 us  [neighbours(): lax.ppermute(value, axis, [(i, i + 1) for i in starts] + [(i + 1, i) for...]
    unnamed x22 -> x14, local copies, waits for them, and re-layouts: 3.98 us -> 1.61 us
    pallas_call x2 -> x1, Pallas kernels: 2.64 us -> 4.12 us  [on_device(): call(front_body, (pltpu.VMEM((40, CC), F32), pltpu.VMEM((40, CC), F32), p...]
    ppermute x4, waiting for transfers between devices: 1.4 us -> 0.01 us  [neighbours(): lax.ppermute(value, axis, [(i, i + 1) for i in starts] + [(i + 1, i) for...]
  transfers between devices with their start and end apart: 5 -> 5, of which waited for: 2 -> 1; matrix products, arithmetic and copies ran while one was open for 0% -> 0% of each run, Pallas kernels for 7% -> 10%
where the time goes in v3:
time: 77 us; the launch traced here: 76.8 us
  Pallas kernels  31.9 us (41%)
  blocking collectives  28.2 us (37%)
  starting transfers between devices  11.2 us (15%)
  waiting for transfers between devices  3.04 us (4%)
  local copies, waits for them, and re-layouts  1.61 us (2%)
  between operations  0.82 us (1%)
    all_to_all x1, blocking collectives, on_device(): gram = lax.all_to_all(gram, AXES, 0, 0, tiled=True)  28.2 us
    pallas_call x1, Pallas kernels, on_device(): call(iterate_body, (f32(K, CR, CC), f32(DEVICES * 3, 128), f32(128, 128),...  9.84 us
    pallas_call x1, Pallas kernels, on_device(): call(products_body, (f32(8 * DEVICES, 128), f32(32, CC), f32(32, CC), f32...  9.09 us
    ppermute x4, starting transfers between devices, neighbours(): lax.ppermute(value, axis, [(i, i + 1) for i in starts] + [(i + 1, i) for...  6.62 us
    pallas_call x1, Pallas kernels, on_device(): call(direction_body, f32(K, CR, CC), scratch=[field, plane, plane, plane]...  5.94 us
    all_to_all x1, starting transfers between devices, on_device(): lax.all_to_all(message.reshape(DEVICES, 1, 384), AXES, 0, 0, tiled=True)  4.59 us
    pallas_call x1, Pallas kernels, on_device(): call(front_body, (pltpu.VMEM((40, CC), F32), pltpu.VMEM((40, CC), F32), p...  4.12 us
    all_to_all x1, waiting for transfers between devices, on_device(): lax.all_to_all(message.reshape(DEVICES, 1, 384), AXES, 0, 0, tiled=True)  3.03 us
  transfers between devices with their start and end apart: 5, of which 1 were waited for; matrix products, arithmetic and copies ran while one was open for 0% of the time, Pallas kernels for 10%

profile of v3, /device:TPU:1, one launch (start us, length us, event | category | flops | bytes accessed | tf_op | source)
XLA Modules:
  0.0 76.8 jit_solution(2073207549932564105)
XLA Ops:
  0.6 0.0 copy-start.1
  0.6 0.0 copy-start.5
  0.7 0.0 copy-start.4
  0.7 4.1 %shard_map.94 = (f32[40,256]{1,0:T(8,128)S(1)}, f32[40,256]{1,0:T(8,128)S(1)}, f32[128,128]{1,0:T(8,128)S(1)}, f32[16,128,256]{2,1,0:T(8,128)S(1)}, f32[16,128,256]{2,1,0:T(8,128)S(1)}) custom-call(f32[16,128,256]{2,1,0:T(8,128)} %x_ref.1, f32[16,128,256]{2,1,0:T(8,128)} %d_ref.3, f32[128,256]{1,0:T(8,128)} %c_ref.7), custom_call_target="tpu_custom_call" | custom-call | bytes 8000000 | tf_op jit(solution)/shard_map/pallas_call | solution.py:402
  4.8 4.6 %collective-permute-start.3 = (f32[128,128]{1,0:T(8,128)S(1)}, f32[128,128]{1,0:T(8,128)S(1)}, u32[]{:S(2)}, u32[]{:S(2)}) collective-permute-start(f32[128,128]{1,0:T(8,128)S(1)} %get-tuple-element.23.after_ref.cols_ref), channel_id=1, source_target_pairs={{1,2},{3,4},{5,6},{2,1},{4,3},{6,5},{9,10},{11,12},{13,14},{10,9},... | collective-permute-start | bytes 196616 | tf_op jit(solution)/shard_map/ppermute | solution.py:391
  9.4 0.1 collective-permute-start.2
  9.5 1.3 %collective-permute-start = (f32[40,256]{1,0:T(8,128)S(1)}, f32[40,256]{1,0:T(8,128)S(1)}, u32[]{:S(2)}, u32[]{:S(2)}) collective-permute-start(f32[40,256]{1,0:T(8,128)S(1)} %get-tuple-element.25.own_first_ref), channel_id=1, source_target_pairs={{0,8},{16,24},{32,40},{48,56},{64,72},{80,88},{96,104},{112,120},{... | collective-permute-start | bytes 122888 | tf_op jit(solution)/shard_map/ppermute | solution.py:391
  10.8 0.7 collective-permute-start.1
  11.5 0.0 copy-done.5
  11.5 0.0 copy-done.4
  11.5 1.7 %shard_map.95 = (s32[2,128,128]{2,1,0:T(8,128)S(1)}, s32[8,256]{1,0:T(8,128)S(1)}, f32[128,128]{1,0:T(8,128)S(1)}) custom-call(s32[128,256]{1,0:T(8,128)S(1)} %copy-done.4, s32[1,1,2048]{2,1,0:T(1,128)S(1)} %copy-done.5, f32[128,128]{1,0:T(8,128)S(1)} %get-tuple-element.23.after_ref.cols_ref), custom_call_target="tpu_custom_call" | custom-call | bytes 10000000 | tf_op jit(solution)/shard_map/pallas_call | solution.py:421
  13.2 0.0 collective-permute-done.far_first_ref
  13.2 0.0 collective-permute-done.1.far_second_ref
  13.2 0.0 collective-permute-done.3.cols_second_ref
  13.2 0.0 collective-permute-done.2.cols_first_ref
  13.3 9.1 %shard_map.96 = (f32[1024,128]{1,0:T(8,128)S(1)}, f32[32,256]{1,0:T(8,128)S(1)}, f32[32,256]{1,0:T(8,128)S(1)}, f32[128,128]{1,0:T(8,128)S(1)}) custom-call(s32[16]{0:T(128)S(1)} %copy-done.6, f32[16,128,256]{2,1,0:T(8,128)S(1)} %get-tuple-element.21.x_ref, f32[16,128,256]{2,1,0:T(8,128)S(1)} %get-tuple-element.22.d_ref, f32[128,256]{1,0:T(8,128)S(1)} %copy-done.1, ...), custom_call_target="tpu_custom_call" | custom-call | bytes 20000000 | tf_op jit(solution)/shard_map/pallas_call | solution.py:429
  22.4 28.2 %all_to_all.16 = f32[128,8,128]{2,1,0:T(8,128)S(1)} all-to-all(f32[128,8,128]{2,1,0:T(8,128)S(1)} %bitcast.6), channel_id=1, replica_groups=mesh['row'=16,'col'=8] {'row','col'}, dimensions={0} | all-to-all | bytes 1048576 | tf_op jit(solution)/shard_map/all_to_all | solution.py:439
  50.5 9.8 %shard_map.97 = (f32[16,128,256]{2,1,0:T(8,128)}, f32[384,128]{1,0:T(8,128)}, f32[128,128]{1,0:T(8,128)S(1)}, f32[16,256]{1,0:T(8,128)S(1)}, f32[16,256]{1,0:T(8,128)S(1)}, /*index=5*/f32[128,128]{1,0:T(8,128)S(1)}) custom-call(f32[1024,128]{1,0:T(8,128)S(1)} %bitcast.4, f32[16,128,256]{2,1,0:T(8,128)S(1)} %get-tuple-element.21.x_ref, ...), custom_call_target="tpu_custom_call" | custom-call | bytes 20000000 | tf_op jit(solution)/shard_map/pallas_call | solution.py:441
  60.4 4.6 %all-to-all-start.1 = ((f32[128,1,384]{2,1,0:T(1,128)}), f32[128,1,384]{2,1,0:T(1,128)S(1)}, u32[]{:S(2)}, u32[]{:S(2)}) async-start(f32[128,1,384]{2,1,0:T(1,128)} %bitcast.2), calls=%async_computation.1 | async-start | bytes 393216 | tf_op jit(solution)/shard_map/all_to_all | solution.py:456
  65.0 0.0 copy-start.2
  65.0 1.6 %copy-done.2 = f32[16,128,256]{2,1,0:T(8,128)S(1)} copy-done((f32[16,128,256]{2,1,0:T(8,128)S(1)}, f32[16,128,256]{2,1,0:T(8,128)}, u32[]{:S(2)}) %copy-start.2) | copy-done | bytes 2097176
  66.6 5.9 %shard_map.98 = f32[16,128,256]{2,1,0:T(8,128)} custom-call(s32[16]{0:T(128)S(1)} %copy-done.6, f32[16,128,256]{2,1,0:T(8,128)S(1)} %copy-done.2, f32[16,128,256]{2,1,0:T(8,128)S(1)} %copy-done, f32[128,256]{1,0:T(8,128)S(1)} %copy-done.1, s32[128,256]{1,0:T(8,128)S(1)} %copy-done.3, s32[2,128,128]{2,1,0:T(8,128)S(1)} %get-tuple-element.24.poc_ref, ...), custom_call_target="tpu_custom_call" | custom-call | bytes 20000000 | tf_op jit(solution)/shard_map/pallas_call | solution.py:457
  72.5 3.0 %all-to-all-done.1 = f32[128,1,384]{2,1,0:T(1,128)S(1)} async-done(((f32[128,1,384]{2,1,0:T(1,128)}), f32[128,1,384]{2,1,0:T(1,128)S(1)}, u32[]{:S(2)}, u32[]{:S(2)}) %all-to-all-start.1) | async-done | bytes 196640 | tf_op jit(solution)/shard_map/all_to_all | solution.py:456
  75.6 1.2 %shard_map.99 = f32[16,512]{1,0:T(8,128)} custom-call(f32[384,128]{1,0:T(8,128)S(1)} %bitcast.5), custom_call_target="tpu_custom_call" | custom-call | bytes 1000000 | tf_op jit(solution)/shard_map/pallas_call | solution.py:464
  (7 shorter events, 0.0 us)
Async XLA Ops:
  0.6 12.6 %copy-start.1 = (f32[128,256]{1,0:T(8,128)S(1)}, f32[128,256]{1,0:T(8,128)}, u32[]{:S(2)}) copy-start(f32[128,256]{1,0:T(8,128)} %c_ref.7) | copy-start | bytes 393220
  0.6 10.8 %copy-start.5 = (s32[1,1,2048]{2,1,0:T(1,128)S(1)}, s32[1,1,2048]{2,1,0:T(1,128)}, u32[]{:S(2)}) copy-start(s32[1,1,2048]{2,1,0:T(1,128)} %tp_ref.1) | copy-start | bytes 24580
  0.7 10.8 %copy-start.4 = (s32[128,256]{1,0:T(8,128)S(1)}, s32[128,256]{1,0:T(8,128)}, u32[]{:S(2)}) copy-start(s32[128,256]{1,0:T(8,128)} %lp_ref.1) | copy-start | bytes 393220
  0.7 12.6 %copy-start.6 = (s32[16]{0:T(128)S(1)}, s32[16]{0:T(128)}, u32[]{:S(2)}) copy-start(s32[16]{0:T(128)} %src_ref.3) | copy-start | bytes 196
  0.7 12.6 %copy-start.3 = (s32[128,256]{1,0:T(8,128)S(1)}, s32[128,256]{1,0:T(8,128)}, u32[]{:S(2)}) copy-start(s32[128,256]{1,0:T(8,128)} %gr_ref.3) | copy-start | bytes 393220
  4.8 8.4 %collective-permute-start.3 = (f32[128,128]{1,0:T(8,128)S(1)}, f32[128,128]{1,0:T(8,128)S(1)}, u32[]{:S(2)}, u32[]{:S(2)}) collective-permute-start(f32[128,128]{1,0:T(8,128)S(1)} %get-tuple-element.23.after_ref.cols_ref), channel_id=1, source_target_pairs={{1,2},{3,4},{5,6},{2,1},{4,3},{6,5},{9,10},{11,12},{13,14},{10,9},... | collective-permute-start | bytes 196616 | tf_op jit(solution)/shard_map/ppermute | solution.py:391
  9.4 3.8 %collective-permute-start.2 = (f32[128,128]{1,0:T(8,128)S(1)}, f32[128,128]{1,0:T(8,128)S(1)}, u32[]{:S(2)}, u32[]{:S(2)}) collective-permute-start(f32[128,128]{1,0:T(8,128)S(1)} %get-tuple-element.23.after_ref.cols_ref), channel_id=1, source_target_pairs={{0,1},{2,3},{4,5},{6,7},{1,0},{3,2},{5,4},{7,6},{8,9},{10,11},{12,... | collective-permute-start | bytes 196616 | tf_op jit(solution)/shard_map/ppermute | solution.py:391
  9.5 3.7 %collective-permute-start = (f32[40,256]{1,0:T(8,128)S(1)}, f32[40,256]{1,0:T(8,128)S(1)}, u32[]{:S(2)}, u32[]{:S(2)}) collective-permute-start(f32[40,256]{1,0:T(8,128)S(1)} %get-tuple-element.25.own_first_ref), channel_id=1, source_target_pairs={{0,8},{16,24},{32,40},{48,56},{64,72},{80,88},{96,104},{112,120},{... | collective-permute-start | bytes 122888 | tf_op jit(solution)/shard_map/ppermute | solution.py:391
  10.8 2.4 %collective-permute-start.1 = (f32[40,256]{1,0:T(8,128)S(1)}, f32[40,256]{1,0:T(8,128)S(1)}, u32[]{:S(2)}, u32[]{:S(2)}) collective-permute-start(f32[40,256]{1,0:T(8,128)S(1)} %get-tuple-element.26.own_second_ref), channel_id=1, source_target_pairs={{8,16},{24,32},{40,48},{56,64},{72,80},{88,96},{104,112},{16,8},{3... | collective-permute-start | bytes 122888 | tf_op jit(solution)/shard_map/ppermute | solution.py:391
  50.5 14.4 %copy-start = (f32[16,128,256]{2,1,0:T(8,128)S(1)}, f32[16,128,256]{2,1,0:T(8,128)}, u32[]{:S(2)}) copy-start(f32[16,128,256]{2,1,0:T(8,128)} %d_ref.3) | copy-start | bytes 6291460
  60.4 15.2 %all-to-all-start.1 = ((f32[128,1,384]{2,1,0:T(1,128)}), f32[128,1,384]{2,1,0:T(1,128)S(1)}, u32[]{:S(2)}, u32[]{:S(2)}) async-start(f32[128,1,384]{2,1,0:T(1,128)} %bitcast.2), calls=%async_computation.1 | async-start | bytes 393216 | tf_op jit(solution)/shard_map/all_to_all | solution.py:456
  65.0 1.6 %copy-start.2 = (f32[16,128,256]{2,1,0:T(8,128)S(1)}, f32[16,128,256]{2,1,0:T(8,128)}, u32[]{:S(2)}) copy-start(f32[16,128,256]{2,1,0:T(8,128)} %get-tuple-element.18.xn_ref) | copy-start | bytes 6291460

commit v4 on v3

--- a/solution.py
+++ b/solution.py
@@ -76,21 +76,27 @@
     even = jnp.bitwise_and(lax.axis_index("row"), 1) == 0
     lane = iota((CR, 128), 1)
     packed = jnp.zeros((CR, 128), F32)
-    for f, copy in enumerate(copies):
-        copy.wait()
-        ref = pairs[f][1]
-        top = ref[0:1, :]
-        bottom = ref[CR - 1 : CR, :]
-        first_ref[f : f + 1, :] = jnp.where(even, bottom, top)
-        second_ref[f : f + 1, :] = jnp.where(even, top, bottom)
-        both = pltpu.roll(jnp.where(lane == 127, ref[:, 128:256], ref[:, 0:128]), 2 * f + 1, 1)
-        packed = jnp.where((lane >> 1) == f, both, packed)
+    for group in (range(0, 8), range(8, 16), range(16, 24), range(24, 33)):
+        for f in group:
+            copies[f].wait()
+        for f in group:
+            ref = pairs[f][1]
+            top = ref[0:1, :]
+            bottom = ref[CR - 1 : CR, :]
+            first_ref[f : f + 1, :] = jnp.where(even, bottom, top)
+            second_ref[f : f + 1, :] = jnp.where(even, top, bottom)
+            both = pltpu.roll(jnp.where(lane == 127, ref[:, 128:256], ref[:, 0:128]), (2 * f + 1) % 128, 1)
+            packed = jnp.where((lane >> 1) == f, both, packed)
     for ref in (first_ref, second_ref):
         ref[33:40, :] = jnp.zeros((7, CC), F32)
     cols_ref[...] = packed
 
 
-def patches_body(lp_ref, tp_ref, after_ref, poc_ref, slot_ref, ids_ref, lp_s):
+def prepare_body(
+    lp_ref, tp_ref, c_ref, gr_ref, after_ref, poc_ref, slot_ref, ids_ref, ee_ref, es_ref, leak_ref, lp_s
+):
+    edges(c_ref[...], ee_ref, es_ref)
+    leak_ref[...] = GROUND_LEAK * gr_ref[...].astype(F32)
     lp_s[0] = lp_ref[:, 0:128]
     lp_s[1] = lp_ref[:, 128:256]
     listed = tp_ref[0]
@@ -137,7 +143,7 @@
 
 
 def turn_columns(flows, field):
-    return pltpu.roll(flows, lax.rem(127 - 2 * field + 128, 128), 1)
+    return pltpu.roll(flows, 127 - 2 * field, 1)
 
 
 def operate(v, outer, ee_s, es_s, leak_s):
@@ -156,14 +162,12 @@
 
 
 def products_body(
-    src_ref, x_ref, d_ref, c_ref, gr_ref, poc_ref,
+    src_ref, x_ref, d_ref, ee_s, es_s, leak_s, poc_ref,
     own_first_ref, own_second_ref, far_first_ref, far_second_ref,
     cols_ref, cols_first_ref, cols_second_ref,
     gram_ref, nf_ref, sf_ref, cf_ref,
-    q_s, r_s, ee_s, es_s, leak_s,
+    q_s, r_s,
 ):
-    edges(c_ref[...], ee_s, es_s)
-    leak_s[...] = GROUND_LEAK * gr_ref[...].astype(F32)
     even = jnp.bitwise_and(lax.axis_index("row"), 1) == 0
     first = (own_first_ref[...], far_first_ref[...])
     second = (own_second_ref[...], far_second_ref[...])
@@ -182,7 +186,7 @@
     edge = jnp.where((lane & 1) == 0, edge[:, 64:65], edge[:, 65:66])
     cf_ref[...] = jnp.where(lane < 64, edge * (own - far), 0.0)
 
-    def field_step(k, carry):
+    def field_step(k):
         image = operate(d_ref[k], turn_columns(cf_ref[...], k + 16), ee_s, es_s, leak_s)
         part = operate(x_ref[k], turn_columns(cf_ref[...], k), ee_s, es_s, leak_s)
         patch = src_ref[k]
@@ -190,13 +194,13 @@
             at = slice(128 * half, 128 * half + 128)
             q_s[k, :, at] = image[half]
             r_s[k, :, at] = jnp.where(poc_ref[half] == patch, SOURCE_AMPS, 0.0) - part[half]
-        q_s[k, 0:1, :] += nf_ref[pl.ds(k + 16, 1), :]
-        q_s[k, CR - 1 : CR, :] += sf_ref[pl.ds(k + 16, 1), :]
-        r_s[k, 0:1, :] -= nf_ref[pl.ds(k, 1), :]
-        r_s[k, CR - 1 : CR, :] -= sf_ref[pl.ds(k, 1), :]
-        return carry
-
-    lax.fori_loop(0, K, field_step, 0)
+        q_s[k, 0:1, :] += nf_ref[k + 16 : k + 17, :]
+        q_s[k, CR - 1 : CR, :] += sf_ref[k + 16 : k + 17, :]
+        r_s[k, 0:1, :] -= nf_ref[k : k + 1, :]
+        r_s[k, CR - 1 : CR, :] -= sf_ref[k : k + 1, :]
+
+    for k in range(K):
+        field_step(k)
     acc = jnp.zeros((256, 256), F32)
     for b in range(CR // 8):
         rows = slice(8 * b, 8 * b + 8)
@@ -211,9 +215,8 @@
     i = iota((256, 256), 0)
     j = iota((256, 256), 1)
     kept = jnp.where((i & 7) == (j & 7), acc, 0.0)
-    fold_rows = jnp.where(iota((32, 256), 0) == (iota((32, 256), 1) >> 3), 1.0, 0.0)
     fold_lanes = jnp.where((iota((256, 128), 0) >> 3) == iota((256, 128), 1), 1.0, 0.0)
-    small = dot_full(dot_full(fold_rows, kept), fold_lanes)
+    small = dot_full(kept.reshape(32, 8, 256).sum(axis=1), fold_lanes)
     packed = small[0:8]
     for q in range(1, 4):
         packed = packed + pltpu.roll(small[8 * q : 8 * q + 8], 32 * q, 1)
@@ -232,11 +235,10 @@
 
 
 def iterate_body(
-    gram_ref, x_ref, d_ref, c_ref, slot_ref, ids_ref, nf_ref, sf_ref, cf_ref,
+    gram_ref, x_ref, d_ref, ee_s, es_s, slot_ref, ids_ref, nf_ref, sf_ref, cf_ref,
     out_ref, msg_ref, beta_ref, nn_ref, sn_ref, cn_ref,
-    xn_ref, cur_s, ee_s, es_s, turn_s, sem,
+    xn_ref, cur_s, turn_s, sem,
 ):
-    edges(c_ref[...], ee_s, es_s)
     packed = gram_ref[...].reshape(DEVICES, 8, 128).sum(axis=0)
     small = jnp.concatenate(
         [packed] + [pltpu.roll(packed, 128 - 32 * q, 1) for q in range(1, 4)], axis=0
@@ -287,17 +289,17 @@
     nn_ref[...] = dot_full(turned, nf_ref[...])
     sn_ref[...] = dot_full(turned, sf_ref[...])
 
-    def field_step(k, carry):
+    def field_step(k):
         v = xn_ref[k]
         flow = jnp.abs(ee_s[...] * (v - pltpu.roll(v, CC - 1, 1)))
         total = flow + pltpu.roll(flow, 1, 1)
         flow = jnp.abs(es_s[...] * (v - pltpu.roll(v, CR - 1, 0)))
         cur_s[k] = total + (flow + pltpu.roll(flow, 1, 0))
-        cur_s[k, 0:1, :] += jnp.abs(nn_ref[pl.ds(k, 1), :])
-        cur_s[k, CR - 1 : CR, :] += jnp.abs(sn_ref[pl.ds(k, 1), :])
-        return carry
-
-    lax.fori_loop(0, K, field_step, 0)
+        cur_s[k, 0:1, :] += jnp.abs(nn_ref[k : k + 1, :])
+        cur_s[k, CR - 1 : CR, :] += jnp.abs(sn_ref[k : k + 1, :])
+
+    for k in range(K):
+        field_step(k)
     take = iota((32, 256), 0)
     given = iota((32, 256), 1) & 127
     rows_of = one_hot(((given >> 3) == (take & 15)) & (((given >> 2) & 1) == (take >> 4)))
@@ -337,29 +339,27 @@
 
 
 def direction_body(
-    src_ref, xn_ref, d_ref, c_ref, gr_ref, poc_ref, beta_ref, nn_ref, sn_ref, cn_ref,
-    do_ref, db_s, ee_s, es_s, leak_s,
+    src_ref, xn_ref, d_ref, ee_s, es_s, leak_s, poc_ref, beta_ref, nn_ref, sn_ref, cn_ref,
+    do_ref, db_s,
 ):
-    edges(c_ref[...], ee_s, es_s)
-    leak_s[...] = GROUND_LEAK * gr_ref[...].astype(F32)
     mix = mixer(beta_ref[...])
     for b in range(CR // 8):
         rows = slice(8 * b, 8 * b + 8)
         step = mixed(mix, d_ref[:, rows, :].reshape(128, CC))
         db_s[:, rows, :] = step.reshape(16, 8, CC)
 
-    def field_step(k, carry):
+    def field_step(k):
         total = operate(xn_ref[k], turn_columns(cn_ref[...], k), ee_s, es_s, leak_s)
         patch = src_ref[k]
         for half in range(2):
             at = slice(128 * half, 128 * half + 128)
             source = jnp.where(poc_ref[half] == patch, SOURCE_AMPS, 0.0)
             do_ref[k, :, at] = (source - total[half]) + db_s[k, :, at]
-        do_ref[k, 0:1, :] -= nn_ref[pl.ds(k, 1), :]
-        do_ref[k, CR - 1 : CR, :] -= sn_ref[pl.ds(k, 1), :]
-        return carry
-
-    lax.fori_loop(0, K, field_step, 0)
+        do_ref[k, 0:1, :] -= nn_ref[k : k + 1, :]
+        do_ref[k, CR - 1 : CR, :] -= sn_ref[k : k + 1, :]
+
+    for k in range(K):
+        field_step(k)
 
 
 def owner_body(msg_ref, out_ref, ids_s):
@@ -418,22 +418,22 @@
     far_first = neighbours(first, "row", 0)
     cols_first = neighbours(columns, "col", 0)
 
-    patch_of_cell, slots, ids = call(
-        patches_body,
-        (i32(2, CR, 128), i32(8, CC), f32(DEVICES, 128)),
+    patch_of_cell, slots, ids, ee, es, leak = call(
+        prepare_body,
+        (i32(2, CR, 128), i32(8, CC), f32(DEVICES, 128), f32(CR, CC), f32(CR, CC), f32(CR, CC)),
         scratch=[pltpu.VMEM((2, CR, 128), jnp.int32)],
-        specs=[vmem] * 2 + [order],
+        specs=[vmem] * 4 + [order],
         moved=10_000_000,
-    )(local_patch, tile_patches, columns)
+    )(local_patch, tile_patches, conductance, ground, columns)
 
     gram, nf, sf, cf = call(
         products_body,
         (f32(8 * DEVICES, 128), f32(32, CC), f32(32, CC), f32(CR, 128)),
-        scratch=[field, field, plane, plane, plane],
-        specs=[smem] + [vmem] * 12,
+        scratch=[field, field],
+        specs=[smem] + [vmem] * 13,
         moved=20_000_000,
     )(
-        sources, x_held, d_held, conductance, ground, patch_of_cell,
+        sources, x_held, d_held, ee, es, leak, patch_of_cell,
         first, second, far_first, far_second, columns, cols_first, cols_second,
     )
     gram = lax.all_to_all(gram, AXES, 0, 0, tiled=True)
@@ -444,23 +444,21 @@
         scratch=[
             field,
             field,
-            plane,
-            plane,
             pltpu.VMEM((128, 128), F32),
             pltpu.SemaphoreType.DMA(()),
         ],
-        specs=[vmem] * 9,
+        specs=[vmem] * 10,
         places=(hbm,) + (vmem,) * 5,
         moved=20_000_000,
-    )(gram, x_held, d_held, conductance, slots, ids, nf, sf, cf)
+    )(gram, x_held, d_held, ee, es, slots, ids, nf, sf, cf)
     received = lax.all_to_all(message.reshape(DEVICES, 1, 384), AXES, 0, 0, tiled=True)
     new_direction = call(
         direction_body,
         f32(K, CR, CC),
-        scratch=[field, plane, plane, plane],
-        specs=[smem] + [vmem] * 9,
+        scratch=[field],
+        specs=[smem] + [vmem] * 10,
         moved=20_000_000,
-    )(sources, new_iterate, direction, conductance, ground, patch_of_cell, beta, nn, sn, cn)
+    )(sources, new_iterate, direction, ee, es, leak, patch_of_cell, beta, nn, sn, cn)
     migration = call(
         owner_body,
         f32(K, PATCH_DEV),

time: 77 us -> 70 us (0.909)
  Pallas kernels: 31.9 us -> 23.5 us
  waiting for transfers between devices: 3.04 us -> 4.57 us
    pallas_call x1, Pallas kernels: 9.09 us -> 6.18 us  [on_device(): call(products_body, (f32(8 * DEVICES, 128), f32(32, CC), f32(32, CC), f32...]
    pallas_call x1, Pallas kernels: 9.84 us -> 7.04 us  [on_device(): call(iterate_body, (f32(K, CR, CC), f32(DEVICES * 3, 128), f32(128, 128),...]
    all_to_all x1, waiting for transfers between devices: 3.03 us -> 4.56 us  [on_device(): lax.all_to_all(message.reshape(DEVICES, 1, 384), AXES, 0, 0, tiled=True)]
    pallas_call x2, Pallas kernels: 7.67 us -> 6.16 us  [the longest x1 4.41 us: on_device(): call(direction_body, f32(K, CR, CC), scratch=[field], specs=[smem] + [vme...]
    pallas_call x1, Pallas kernels: 4.12 us -> 2.85 us  [on_device(): call(front_body, (pltpu.VMEM((40, CC), F32), pltpu.VMEM((40, CC), F32), p...]
  transfers between devices with their start and end apart: 5 -> 5, of which waited for: 1 -> 1; matrix products, arithmetic and copies ran while one was open for 0% -> 0% of each run, Pallas kernels for 10% -> 9%
where the time goes in v4:
time: 70 us; the launch traced here: 69.8 us
  blocking collectives  28.1 us (40%)
  Pallas kernels  23.5 us (34%)
  starting transfers between devices  11.2 us (16%)
  waiting for transfers between devices  4.57 us (7%)
  local copies, waits for them, and re-layouts  1.61 us (2%)
  between operations  0.83 us (1%)
    all_to_all x1, blocking collectives, on_device(): gram = lax.all_to_all(gram, AXES, 0, 0, tiled=True)  28.1 us
    pallas_call x1, Pallas kernels, on_device(): call(iterate_body, (f32(K, CR, CC), f32(DEVICES * 3, 128), f32(128, 128),...  7.04 us
    ppermute x4, starting transfers between devices, neighbours(): lax.ppermute(value, axis, [(i, i + 1) for i in starts] + [(i + 1, i) for...  6.62 us
    pallas_call x1, Pallas kernels, on_device(): call(products_body, (f32(8 * DEVICES, 128), f32(32, CC), f32(32, CC), f32...  6.18 us
    all_to_all x1, starting transfers between devices, on_device(): lax.all_to_all(message.reshape(DEVICES, 1, 384), AXES, 0, 0, tiled=True)  4.59 us
    all_to_all x1, waiting for transfers between devices, on_device(): lax.all_to_all(message.reshape(DEVICES, 1, 384), AXES, 0, 0, tiled=True)  4.56 us
    pallas_call x1, Pallas kernels, on_device(): call(direction_body, f32(K, CR, CC), scratch=[field], specs=[smem] + [vme...  4.41 us
    pallas_call x1, Pallas kernels, on_device(): call(front_body, (pltpu.VMEM((40, CC), F32), pltpu.VMEM((40, CC), F32), p...  2.85 us
  transfers between devices with their start and end apart: 5, of which 1 were waited for; matrix products, arithmetic and copies ran while one was open for 0% of the time, Pallas kernels for 9%

profile of v4, /device:TPU:1, one launch (start us, length us, event | category | flops | bytes accessed | tf_op | source)
XLA Modules:
  0.0 69.8 jit_solution(11603376952194995811)
XLA Ops:
  0.6 0.0 copy-start.2
  0.6 0.0 copy-start.5
  0.7 0.0 copy-start.3
  0.7 0.0 copy-start.4
  0.7 0.0 copy-start.6
  0.7 2.9 %shard_map.94 = (f32[40,256]{1,0:T(8,128)S(1)}, f32[40,256]{1,0:T(8,128)S(1)}, f32[128,128]{1,0:T(8,128)S(1)}, f32[16,128,256]{2,1,0:T(8,128)S(1)}, f32[16,128,256]{2,1,0:T(8,128)S(1)}) custom-call(f32[16,128,256]{2,1,0:T(8,128)} %x_ref.1, f32[16,128,256]{2,1,0:T(8,128)} %d_ref.3, f32[128,256]{1,0:T(8,128)} %c_ref.3), custom_call_target="tpu_custom_call" | custom-call | bytes 8000000 | tf_op jit(solution)/shard_map/pallas_call | solution.py:402
  3.5 4.6 %collective-permute-start.3 = (f32[128,128]{1,0:T(8,128)S(1)}, f32[128,128]{1,0:T(8,128)S(1)}, u32[]{:S(2)}, u32[]{:S(2)}) collective-permute-start(f32[128,128]{1,0:T(8,128)S(1)} %get-tuple-element.26.after_ref.cols_ref), channel_id=1, source_target_pairs={{1,2},{3,4},{5,6},{2,1},{4,3},{6,5},{9,10},{11,12},{13,14},{10,9},... | collective-permute-start | bytes 196616 | tf_op jit(solution)/shard_map/ppermute | solution.py:391
  8.1 0.1 collective-permute-start.2
  8.2 1.3 %collective-permute-start = (f32[40,256]{1,0:T(8,128)S(1)}, f32[40,256]{1,0:T(8,128)S(1)}, u32[]{:S(2)}, u32[]{:S(2)}) collective-permute-start(f32[40,256]{1,0:T(8,128)S(1)} %get-tuple-element.31.own_first_ref), channel_id=1, source_target_pairs={{0,8},{16,24},{32,40},{48,56},{64,72},{80,88},{96,104},{112,120},{... | collective-permute-start | bytes 122888 | tf_op jit(solution)/shard_map/ppermute | solution.py:391
  9.5 0.7 collective-permute-start.1
  10.2 1.7 %shard_map.95 = (s32[2,128,128]{2,1,0:T(8,128)S(1)}, s32[8,256]{1,0:T(8,128)S(1)}, f32[128,128]{1,0:T(8,128)S(1)}, f32[128,256]{1,0:T(8,128)S(1)}, f32[128,256]{1,0:T(8,128)S(1)}, /*index=5*/f32[128,256]{1,0:T(8,128)S(1)}) custom-call(s32[128,256]{1,0:T(8,128)S(1)} %copy-done.3, s32[1,1,2048]{2,1,0:T(1,128)S(1)} %copy-done.5, f32[128,256]{1,0:T(8,128)S(1)} %copy-done.2, ...), custom_call_target="tpu_custom_call" | custom-call | bytes 10000000 | tf_op jit(solution)/shard_map/pallas_call | solution.py:421
  12.0 0.0 collective-permute-done.far_first_ref
  12.0 0.0 collective-permute-done.1.far_second_ref
  12.0 0.0 collective-permute-done.3.cols_second_ref
  12.0 0.0 collective-permute-done.2.cols_first_ref
  12.0 6.2 %shard_map.96 = (f32[1024,128]{1,0:T(8,128)S(1)}, f32[32,256]{1,0:T(8,128)S(1)}, f32[32,256]{1,0:T(8,128)S(1)}, f32[128,128]{1,0:T(8,128)S(1)}) custom-call(s32[16]{0:T(128)S(1)} %copy-done.6, f32[16,128,256]{2,1,0:T(8,128)S(1)} %get-tuple-element.24.x_ref, f32[16,128,256]{2,1,0:T(8,128)S(1)} %get-tuple-element.25.d_ref, ...), custom_call_target="tpu_custom_call" | custom-call | bytes 20000000 | tf_op jit(solution)/shard_map/pallas_call | solution.py:429
  18.2 28.1 %all_to_all.16 = f32[128,8,128]{2,1,0:T(8,128)S(1)} all-to-all(f32[128,8,128]{2,1,0:T(8,128)S(1)} %bitcast.6), channel_id=1, replica_groups=mesh['row'=16,'col'=8] {'row','col'}, dimensions={0} | all-to-all | bytes 1048576 | tf_op jit(solution)/shard_map/all_to_all | solution.py:439
  46.4 7.0 %shard_map.97 = (f32[16,128,256]{2,1,0:T(8,128)}, f32[384,128]{1,0:T(8,128)}, f32[128,128]{1,0:T(8,128)S(1)}, f32[16,256]{1,0:T(8,128)S(1)}, f32[16,256]{1,0:T(8,128)S(1)}, /*index=5*/f32[128,128]{1,0:T(8,128)S(1)}) custom-call(f32[1024,128]{1,0:T(8,128)S(1)} %bitcast.4, f32[16,128,256]{2,1,0:T(8,128)S(1)} %get-tuple-element.24.x_ref, ...), custom_call_target="tpu_custom_call" | custom-call | bytes 20000000 | tf_op jit(solution)/shard_map/pallas_call | solution.py:441
  53.4 4.6 %all-to-all-start.1 = ((f32[128,1,384]{2,1,0:T(1,128)}), f32[128,1,384]{2,1,0:T(1,128)S(1)}, u32[]{:S(2)}, u32[]{:S(2)}) async-start(f32[128,1,384]{2,1,0:T(1,128)} %bitcast.2), calls=%async_computation.1 | async-start | bytes 393216 | tf_op jit(solution)/shard_map/all_to_all | solution.py:454
  58.0 0.0 copy-start.1
  58.0 1.6 %copy-done.1 = f32[16,128,256]{2,1,0:T(8,128)S(1)} copy-done((f32[16,128,256]{2,1,0:T(8,128)S(1)}, f32[16,128,256]{2,1,0:T(8,128)}, u32[]{:S(2)}) %copy-start.1) | copy-done | bytes 2097176
  59.6 4.4 %shard_map.98 = f32[16,128,256]{2,1,0:T(8,128)} custom-call(s32[16]{0:T(128)S(1)} %copy-done.6, f32[16,128,256]{2,1,0:T(8,128)S(1)} %copy-done.1, f32[16,128,256]{2,1,0:T(8,128)S(1)} %copy-done, f32[128,256]{1,0:T(8,128)S(1)} %get-tuple-element.27.ee_s, f32[128,256]{1,0:T(8,128)S(1)} %get-tuple-element.28.es_s, f32[128,256]{1,0:T(8,128)S(1)} %get-tuple-element.29.leak_s, ...), custom_call_target="tpu_custom_call" | custom-call | bytes 20000000 | tf_op jit(solution)/shard_map/pallas_call | solution.py:455
  64.0 4.6 %all-to-all-done.1 = f32[128,1,384]{2,1,0:T(1,128)S(1)} async-done(((f32[128,1,384]{2,1,0:T(1,128)}), f32[128,1,384]{2,1,0:T(1,128)S(1)}, u32[]{:S(2)}, u32[]{:S(2)}) %all-to-all-start.1) | async-done | bytes 196640 | tf_op jit(solution)/shard_map/all_to_all | solution.py:454
  68.6 1.2 %shard_map.99 = f32[16,512]{1,0:T(8,128)} custom-call(f32[384,128]{1,0:T(8,128)S(1)} %bitcast.5), custom_call_target="tpu_custom_call" | custom-call | bytes 1000000 | tf_op jit(solution)/shard_map/pallas_call | solution.py:462
  (7 shorter events, 0.0 us)
Async XLA Ops:
  0.6 9.6 %copy-start.2 = (f32[128,256]{1,0:T(8,128)S(1)}, f32[128,256]{1,0:T(8,128)}, u32[]{:S(2)}) copy-start(f32[128,256]{1,0:T(8,128)} %c_ref.3) | copy-start | bytes 393220
  0.6 9.6 %copy-start.5 = (s32[1,1,2048]{2,1,0:T(1,128)S(1)}, s32[1,1,2048]{2,1,0:T(1,128)}, u32[]{:S(2)}) copy-start(s32[1,1,2048]{2,1,0:T(1,128)} %tp_ref.1) | copy-start | bytes 24580
  0.7 9.6 %copy-start.3 = (s32[128,256]{1,0:T(8,128)S(1)}, s32[128,256]{1,0:T(8,128)}, u32[]{:S(2)}) copy-start(s32[128,256]{1,0:T(8,128)} %lp_ref.1) | copy-start | bytes 393220
  0.7 9.6 %copy-start.4 = (s32[128,256]{1,0:T(8,128)S(1)}, s32[128,256]{1,0:T(8,128)}, u32[]{:S(2)}) copy-start(s32[128,256]{1,0:T(8,128)} %gr_ref.1) | copy-start | bytes 393220
  0.7 11.4 %copy-start.6 = (s32[16]{0:T(128)S(1)}, s32[16]{0:T(128)}, u32[]{:S(2)}) copy-start(s32[16]{0:T(128)} %src_ref.3) | copy-start | bytes 196
  3.5 8.5 %collective-permute-start.3 = (f32[128,128]{1,0:T(8,128)S(1)}, f32[128,128]{1,0:T(8,128)S(1)}, u32[]{:S(2)}, u32[]{:S(2)}) collective-permute-start(f32[128,128]{1,0:T(8,128)S(1)} %get-tuple-element.26.after_ref.cols_ref), channel_id=1, source_target_pairs={{1,2},{3,4},{5,6},{2,1},{4,3},{6,5},{9,10},{11,12},{13,14},{10,9},... | collective-permute-start | bytes 196616 | tf_op jit(solution)/shard_map/ppermute | solution.py:391
  8.1 3.9 %collective-permute-start.2 = (f32[128,128]{1,0:T(8,128)S(1)}, f32[128,128]{1,0:T(8,128)S(1)}, u32[]{:S(2)}, u32[]{:S(2)}) collective-permute-start(f32[128,128]{1,0:T(8,128)S(1)} %get-tuple-element.26.after_ref.cols_ref), channel_id=1, source_target_pairs={{0,1},{2,3},{4,5},{6,7},{1,0},{3,2},{5,4},{7,6},{8,9},{10,11},{12,... | collective-permute-start | bytes 196616 | tf_op jit(solution)/shard_map/ppermute | solution.py:391
  8.2 3.7 %collective-permute-start = (f32[40,256]{1,0:T(8,128)S(1)}, f32[40,256]{1,0:T(8,128)S(1)}, u32[]{:S(2)}, u32[]{:S(2)}) collective-permute-start(f32[40,256]{1,0:T(8,128)S(1)} %get-tuple-element.31.own_first_ref), channel_id=1, source_target_pairs={{0,8},{16,24},{32,40},{48,56},{64,72},{80,88},{96,104},{112,120},{... | collective-permute-start | bytes 122888 | tf_op jit(solution)/shard_map/ppermute | solution.py:391
  9.5 2.5 %collective-permute-start.1 = (f32[40,256]{1,0:T(8,128)S(1)}, f32[40,256]{1,0:T(8,128)S(1)}, u32[]{:S(2)}, u32[]{:S(2)}) collective-permute-start(f32[40,256]{1,0:T(8,128)S(1)} %get-tuple-element.32.own_second_ref), channel_id=1, source_target_pairs={{8,16},{24,32},{40,48},{56,64},{72,80},{88,96},{104,112},{16,8},{3... | collective-permute-start | bytes 122888 | tf_op jit(solution)/shard_map/ppermute | solution.py:391
  46.4 11.7 %copy-start = (f32[16,128,256]{2,1,0:T(8,128)S(1)}, f32[16,128,256]{2,1,0:T(8,128)}, u32[]{:S(2)}) copy-start(f32[16,128,256]{2,1,0:T(8,128)} %d_ref.3) | copy-start | bytes 6291460
  53.4 15.2 %all-to-all-start.1 = ((f32[128,1,384]{2,1,0:T(1,128)}), f32[128,1,384]{2,1,0:T(1,128)S(1)}, u32[]{:S(2)}, u32[]{:S(2)}) async-start(f32[128,1,384]{2,1,0:T(1,128)} %bitcast.2), calls=%async_computation.1 | async-start | bytes 393216 | tf_op jit(solution)/shard_map/all_to_all | solution.py:454
  58.0 1.6 %copy-start.1 = (f32[16,128,256]{2,1,0:T(8,128)S(1)}, f32[16,128,256]{2,1,0:T(8,128)}, u32[]{:S(2)}) copy-start(f32[16,128,256]{2,1,0:T(8,128)} %get-tuple-element.21.xn_ref) | copy-start | bytes 6291460

commit v5 on v4

--- a/solution.py
+++ b/solution.py
@@ -66,19 +66,28 @@
     return jax.ShapeDtypeStruct(shape, jnp.int32)
 
 
-def front_body(x_ref, d_ref, c_ref, first_ref, second_ref, cols_ref, xv_ref, dv_ref, c_s, sems):
+def front_body(
+    x_ref, d_ref, c_ref, gr_ref, lp_ref, tp_ref,
+    first_ref, second_ref, cols_ref, xv_ref, dv_ref,
+    poc_ref, slot_ref, ids_ref, ee_ref, es_ref, leak_ref,
+    c_s, gr_s, whole_s, tp_s, lp_s, sems,
+):
     pairs = [(x_ref.at[k], xv_ref.at[k]) for k in range(K)]
     pairs += [(d_ref.at[k], dv_ref.at[k]) for k in range(K)]
-    pairs += [(c_ref, c_s)]
+    pairs += [(c_ref, c_s), (gr_ref, gr_s), (lp_ref, whole_s), (tp_ref, tp_s)]
     copies = [pltpu.make_async_copy(*pair, sems.at[f]) for f, pair in enumerate(pairs)]
-    for copy in copies:
+    for copy in copies[32:] + copies[:32]:
         copy.start()
+    for copy in copies[32:]:
+        copy.wait()
+    prepare(whole_s, tp_s, c_s, gr_s, poc_ref, slot_ref, ids_ref, ee_ref, es_ref, leak_ref, lp_s)
     even = jnp.bitwise_and(lax.axis_index("row"), 1) == 0
     lane = iota((CR, 128), 1)
     packed = jnp.zeros((CR, 128), F32)
     for group in (range(0, 8), range(8, 16), range(16, 24), range(24, 33)):
         for f in group:
-            copies[f].wait()
+            if f < 32:
+                copies[f].wait()
         for f in group:
             ref = pairs[f][1]
             top = ref[0:1, :]
@@ -92,9 +101,7 @@
     cols_ref[...] = packed
 
 
-def prepare_body(
-    lp_ref, tp_ref, c_ref, gr_ref, after_ref, poc_ref, slot_ref, ids_ref, ee_ref, es_ref, leak_ref, lp_s
-):
+def prepare(lp_ref, tp_ref, c_ref, gr_ref, poc_ref, slot_ref, ids_ref, ee_ref, es_ref, leak_ref, lp_s):
     edges(c_ref[...], ee_ref, es_ref)
     leak_ref[...] = GROUND_LEAK * gr_ref[...].astype(F32)
     lp_s[0] = lp_ref[:, 0:128]
@@ -117,15 +124,18 @@
         acc = acc + dot(parts, pick)
     slot_ref[...] = (acc[8:16] * 128.0 + acc[0:8]).astype(jnp.int32)
     place = (acc[0:8] * 16.0 + acc[8:16]).astype(jnp.int32)
-    table = stack2(jnp.broadcast_to(listed >> 8, (8, 2048)), jnp.broadcast_to(listed & 255, (8, 2048)))
-    table = table.astype(F32).astype(BF16)
-    entry = iota((2048, CC), 0)
+    table = jnp.concatenate([listed[:, 128 * j : 128 * j + 128] for j in range(16)], axis=0)
+    table = stack2(table >> 8, table & 255).astype(F32).astype(BF16)
+    low = iota((128, CC), 0)
+    high = iota((16, CC), 0)
     highs = []
     lows = []
     for i in range(8):
-        found = dot(table, one_hot(entry == place[i : i + 1, :]))
-        highs.append(found[0:1])
-        lows.append(found[8:9])
+        at = place[i : i + 1, :]
+        options = dot(table, one_hot(low == (at & 127)))
+        here = high == (at >> 7)
+        highs.append(jnp.where(here, options[0:16], 0.0).sum(axis=0, keepdims=True))
+        lows.append(jnp.where(here, options[16:32], 0.0).sum(axis=0, keepdims=True))
     found = jnp.concatenate(highs + lows, axis=0).astype(BF16)
     for q in range(4):
         spread = dot(found, one_hot(spot == q * 64 + (cell >> 2)), 1, 1)
@@ -152,17 +162,32 @@
     b = v[:, 128:256]
     after = pltpu.roll(b, 127, 1)
     flow_a = ee_s[:, 0:128] * (a - jnp.where(lane == 127, after, pltpu.roll(a, 127, 1)))
-    flow_b = jnp.where(lane == 127, outer, ee_s[:, 128:256] * (b - after))
+    flow_b = ee_s[:, 128:256] * (b - after)
     before = pltpu.roll(flow_a, 1, 1)
-    total_a = flow_a - jnp.where(lane == 0, -outer, before)
+    if outer is None:
+        total_a = flow_a - jnp.where(lane == 0, 0.0, before)
+    else:
+        flow_b = jnp.where(lane == 127, outer, flow_b)
+        total_a = flow_a - jnp.where(lane == 0, -outer, before)
     total_b = flow_b - jnp.where(lane == 0, before, pltpu.roll(flow_b, 1, 1))
     flow = es_s[...] * (v - pltpu.roll(v, CR - 1, 0))
     down = (flow - pltpu.roll(flow, 1, 0)) + leak_s[...] * v
     return total_a + down[:, 0:128], total_b + down[:, 128:256]
 
 
+def fields_body(src_ref, x_ref, d_ref, ee_s, es_s, leak_s, poc_ref, q_ref, r_ref):
+    for k in range(K):
+        image = operate(d_ref[k], None, ee_s, es_s, leak_s)
+        part = operate(x_ref[k], None, ee_s, es_s, leak_s)
+        patch = src_ref[k]
+        for half in range(2):
+            at = slice(128 * half, 128 * half + 128)
+            q_ref[k, :, at] = image[half]
+            r_ref[k, :, at] = jnp.where(poc_ref[half] == patch, SOURCE_AMPS, 0.0) - part[half]
+
+
 def products_body(
-    src_ref, x_ref, d_ref, ee_s, es_s, leak_s, poc_ref,
+    d_ref, q_ref, r_ref,
     own_first_ref, own_second_ref, far_first_ref, far_second_ref,
     cols_ref, cols_first_ref, cols_second_ref,
     gram_ref, nf_ref, sf_ref, cf_ref,
@@ -186,27 +211,37 @@
     edge = jnp.where((lane & 1) == 0, edge[:, 64:65], edge[:, 65:66])
     cf_ref[...] = jnp.where(lane < 64, edge * (own - far), 0.0)
 
-    def field_step(k):
-        image = operate(d_ref[k], turn_columns(cf_ref[...], k + 16), ee_s, es_s, leak_s)
-        part = operate(x_ref[k], turn_columns(cf_ref[...], k), ee_s, es_s, leak_s)
-        patch = src_ref[k]
-        for half in range(2):
-            at = slice(128 * half, 128 * half + 128)
-            q_s[k, :, at] = image[half]
-            r_s[k, :, at] = jnp.where(poc_ref[half] == patch, SOURCE_AMPS, 0.0) - part[half]
-        q_s[k, 0:1, :] += nf_ref[k + 16 : k + 17, :]
-        q_s[k, CR - 1 : CR, :] += sf_ref[k + 16 : k + 17, :]
-        r_s[k, 0:1, :] -= nf_ref[k : k + 1, :]
-        r_s[k, CR - 1 : CR, :] -= sf_ref[k : k + 1, :]
-
-    for k in range(K):
-        field_step(k)
+    for n, at, row, flows in ((0, 0, 0, nf_ref), (1, CR - 8, 7, sf_ref)):
+        q_s[n] = q_ref[:, at : at + 8, :]
+        r_s[n] = r_ref[:, at : at + 8, :]
+        for k in range(K):
+            q_s[n, k, row : row + 1, :] += flows[k + 16 : k + 17, :]
+            r_s[n, k, row : row + 1, :] -= flows[k : k + 1, :]
+    side = iota((K, 8, 128), 2)
+
+    def complete(inner, flows, base):
+        turned = jnp.concatenate(
+            [turn_columns(flows, base + k).reshape(1, 8, 128) for k in range(K)], axis=0
+        )
+        if base == 0:
+            turned = -turned
+        return jnp.concatenate(
+            [
+                inner[:, :, 0:128] + jnp.where(side == 0, turned, 0.0),
+                inner[:, :, 128:256] + jnp.where(side == 127, turned, 0.0),
+            ],
+            axis=2,
+        ).reshape(128, CC)
+
     acc = jnp.zeros((256, 256), F32)
     for b in range(CR // 8):
         rows = slice(8 * b, 8 * b + 8)
         dh, dl = split(d_ref[:, rows, :].reshape(128, CC))
-        qh, ql = split(q_s[:, rows, :].reshape(128, CC))
-        rh, rl = split(r_s[:, rows, :].reshape(128, CC))
+        image = q_s[0] if b == 0 else (q_s[1] if b == CR // 8 - 1 else q_ref[:, rows, :])
+        part = r_s[0] if b == 0 else (r_s[1] if b == CR // 8 - 1 else r_ref[:, rows, :])
+        flows = cf_ref[rows, :]
+        qh, ql = split(complete(image, flows, 16))
+        rh, rl = split(complete(part, flows, 0))
         lh = stack2(dh, qh)
         ll = stack2(dl, ql)
         gh = stack2(qh, rh)
@@ -395,11 +430,10 @@
     vmem = pl.BlockSpec(memory_space=pltpu.VMEM)
     smem = pl.BlockSpec(memory_space=pltpu.SMEM)
     hbm = pl.BlockSpec(memory_space=pltpu.HBM)
-    order = pl.BlockSpec(memory_space=pl.ANY)
     field = pltpu.VMEM((K, CR, CC), F32)
     plane = pltpu.VMEM((CR, CC), F32)
 
-    first, second, columns, x_held, d_held = call(
+    first, second, columns, x_held, d_held, patch_of_cell, slots, ids, ee, es, leak = call(
         front_body,
         (
             pltpu.VMEM((40, CC), F32),
@@ -407,33 +441,46 @@
             pltpu.VMEM((CR, 128), F32),
             field,
             field,
+            pltpu.VMEM((2, CR, 128), jnp.int32),
+            pltpu.VMEM((8, CC), jnp.int32),
+            pltpu.VMEM((DEVICES, 128), F32),
+            plane,
+            plane,
+            plane,
         ),
-        scratch=[plane, pltpu.SemaphoreType.DMA((33,))],
-        specs=[hbm] * 3,
-        places=(vmem,) * 5,
+        scratch=[
+            plane,
+            pltpu.VMEM((CR, CC), jnp.int32),
+            pltpu.VMEM((CR, CC), jnp.int32),
+            pltpu.VMEM((1, 1, 2048), jnp.int32),
+            pltpu.VMEM((2, CR, 128), jnp.int32),
+            pltpu.SemaphoreType.DMA((36,)),
+        ],
+        specs=[hbm] * 6,
+        places=(vmem,) * 11,
         moved=8_000_000,
-    )(*[pltpu.with_memory_space_constraint(a, pltpu.HBM) for a in (iterate, direction, conductance)])
+    )(*[pltpu.with_memory_space_constraint(a, pltpu.HBM) for a in (iterate, direction, conductance, ground, local_patch, tile_patches)])
     far_second = neighbours(second, "row", 1)
     cols_second = neighbours(columns, "col", 1)
     far_first = neighbours(first, "row", 0)
     cols_first = neighbours(columns, "col", 0)
 
-    patch_of_cell, slots, ids, ee, es, leak = call(
-        prepare_body,
-        (i32(2, CR, 128), i32(8, CC), f32(DEVICES, 128), f32(CR, CC), f32(CR, CC), f32(CR, CC)),
-        scratch=[pltpu.VMEM((2, CR, 128), jnp.int32)],
-        specs=[vmem] * 4 + [order],
-        moved=10_000_000,
-    )(local_patch, tile_patches, conductance, ground, columns)
+    image, part = call(
+        fields_body,
+        (pltpu.VMEM((K, CR, CC), F32), pltpu.VMEM((K, CR, CC), F32)),
+        specs=[smem] + [vmem] * 6,
+        places=(vmem, vmem),
+        moved=12_000_000,
+    )(sources, x_held, d_held, ee, es, leak, patch_of_cell)
 
     gram, nf, sf, cf = call(
         products_body,
         (f32(8 * DEVICES, 128), f32(32, CC), f32(32, CC), f32(CR, 128)),
-        scratch=[field, field],
-        specs=[smem] + [vmem] * 13,
+        scratch=[pltpu.VMEM((2, K, 8, CC), F32), pltpu.VMEM((2, K, 8, CC), F32)],
+        specs=[vmem] * 10,
         moved=20_000_000,
     )(
-        sources, x_held, d_held, ee, es, leak, patch_of_cell,
+        d_held, image, part,
         first, second, far_first, far_second, columns, cols_first, cols_second,
     )
     gram = lax.all_to_all(gram, AXES, 0, 0, tiled=True)

time: 70 us -> 67.5 us (0.964)
  blocking collectives: 28.1 us -> 26.1 us
    pallas_call x1, Pallas kernels: 6.18 us -> 2.75 us  [on_device(): call(products_body, (f32(8 * DEVICES, 128), f32(32, CC), f32(32, CC), f32...]
    pallas_call x1, Pallas kernels: 1.74 us -> 4.63 us  [on_device(): call(fields_body, (pltpu.VMEM((K, CR, CC), F32), pltpu.VMEM((K, CR, CC),...]
    all_to_all x1, blocking collectives: 28.1 us -> 26.1 us  [on_device(): gram = lax.all_to_all(gram, AXES, 0, 0, tiled=True)]
    unnamed x14 -> x6, local copies, waits for them, and re-layouts: 1.61 us -> 1.59 us
  transfers between devices with their start and end apart: 5 -> 5, of which waited for: 1 -> 1; matrix products, arithmetic and copies ran while one was open for 0% -> 0% of each run, Pallas kernels for 9% -> 13%
where the time goes in v5:
time: 67.5 us; the launch traced here: 67.3 us
  blocking collectives  26.1 us (39%)
  Pallas kernels  23.1 us (34%)
  starting transfers between devices  11.2 us (17%)
  waiting for transfers between devices  4.55 us (7%)
  local copies, waits for them, and re-layouts  1.59 us (2%)
  between operations  0.76 us (1%)
    all_to_all x1, blocking collectives, on_device(): gram = lax.all_to_all(gram, AXES, 0, 0, tiled=True)  26.1 us
    pallas_call x1, Pallas kernels, on_device(): call(iterate_body, (f32(K, CR, CC), f32(DEVICES * 3, 128), f32(128, 128),...  7.05 us
    ppermute x4, starting transfers between devices, neighbours(): lax.ppermute(value, axis, [(i, i + 1) for i in starts] + [(i + 1, i) for...  6.62 us
    pallas_call x1, Pallas kernels, on_device(): call(fields_body, (pltpu.VMEM((K, CR, CC), F32), pltpu.VMEM((K, CR, CC),...  4.63 us
    all_to_all x1, starting transfers between devices, on_device(): lax.all_to_all(message.reshape(DEVICES, 1, 384), AXES, 0, 0, tiled=True)  4.59 us
    all_to_all x1, waiting for transfers between devices, on_device(): lax.all_to_all(message.reshape(DEVICES, 1, 384), AXES, 0, 0, tiled=True)  4.54 us
    pallas_call x1, Pallas kernels, on_device(): call(direction_body, f32(K, CR, CC), scratch=[field], specs=[smem] + [vme...  4.41 us
    pallas_call x1, Pallas kernels, on_device(): call(front_body, (pltpu.VMEM((40, CC), F32), pltpu.VMEM((40, CC), F32), p...  3.02 us
  transfers between devices with their start and end apart: 5, of which 1 were waited for; matrix products, arithmetic and copies ran while one was open for 0% of the time, Pallas kernels for 13%

profile of v5, /device:TPU:1, one launch (start us, length us, event | category | flops | bytes accessed | tf_op | source)
XLA Modules:
  0.0 67.3 jit_solution(15838887498605077681)
XLA Ops:
  0.6 0.0 copy-start.2
  0.6 3.0 %shard_map.94 = (f32[40,256]{1,0:T(8,128)S(1)}, f32[40,256]{1,0:T(8,128)S(1)}, f32[128,128]{1,0:T(8,128)S(1)}, f32[16,128,256]{2,1,0:T(8,128)S(1)}, f32[16,128,2...) custom-call(f32[16,128,256]{2,1,0:T(8,128)} %x_ref.1, ...), custom_call_target="tpu_custom_call" | custom-call | bytes 8000000 | tf_op jit(solution)/shard_map/pallas_call | solution.py:436
  3.7 4.6 %collective-permute-start.3 = (f32[128,128]{1,0:T(8,128)S(1)}, f32[128,128]{1,0:T(8,128)S(1)}, u32[]{:S(2)}, u32[]{:S(2)}) collective-permute-start(f32[128,128]{1,0:T(8,128)S(1)} %get-tuple-element.36.cols_ref), channel_id=1, source_target_pairs={{1,2},{3,4},{5,6},{2,1},{4,3},{6,5},{9,10},{11,12},{13,14},{10,9},... | collective-permute-start | bytes 196616 | tf_op jit(solution)/shard_map/ppermute | solution.py:426
  8.3 0.1 collective-permute-start.2
  8.4 1.3 %collective-permute-start = (f32[40,256]{1,0:T(8,128)S(1)}, f32[40,256]{1,0:T(8,128)S(1)}, u32[]{:S(2)}, u32[]{:S(2)}) collective-permute-start(f32[40,256]{1,0:T(8,128)S(1)} %get-tuple-element.34.own_first_ref), channel_id=1, source_target_pairs={{0,8},{16,24},{32,40},{48,56},{64,72},{80,88},{96,104},{112,120},{... | collective-permute-start | bytes 122888 | tf_op jit(solution)/shard_map/ppermute | solution.py:426
  9.7 0.7 collective-permute-start.1
  10.3 0.0 copy-done.2
  10.3 4.6 %shard_map.95 = (f32[16,128,256]{2,1,0:T(8,128)S(1)}, f32[16,128,256]{2,1,0:T(8,128)S(1)}) custom-call(s32[16]{0:T(128)S(1)} %copy-done.2, f32[16,128,256]{2,1,0:T(8,128)S(1)} %get-tuple-element.27.x_ref, f32[16,128,256]{2,1,0:T(8,128)S(1)} %get-tuple-element.26.d_ref, f32[128,256]{1,0:T(8,128)S(1)} %get-tuple-element.28.ee_s, ...), custom_call_target="tpu_custom_call" | custom-call | bytes 12000000 | tf_op jit(solution)/shard_map/pallas_call | solution.py:468
  15.0 0.0 collective-permute-done.far_first_ref
  15.0 0.0 collective-permute-done.1.far_second_ref
  15.0 0.0 collective-permute-done.3.cols_second_ref
  15.0 0.0 collective-permute-done.2.cols_first_ref
  15.0 2.8 %shard_map.96 = (f32[1024,128]{1,0:T(8,128)S(1)}, f32[32,256]{1,0:T(8,128)S(1)}, f32[32,256]{1,0:T(8,128)S(1)}, f32[128,128]{1,0:T(8,128)S(1)}) custom-call(f32[16,128,256]{2,1,0:T(8,128)S(1)} %get-tuple-element.26.d_ref, f32[16,128,256]{2,1,0:T(8,128)S(1)} %get-tuple-element.32.q_ref, f32[16,128,256]{2,1,0:T(8,128)S(1)} %get-tuple-element.33.r_ref, ...), custom_call_target="tpu_custom_call" | custom-call | bytes 20000000 | tf_op jit(solution)/shard_map/pallas_call | solution.py:476
  17.8 26.1 %all_to_all.16 = f32[128,8,128]{2,1,0:T(8,128)S(1)} all-to-all(f32[128,8,128]{2,1,0:T(8,128)S(1)} %bitcast.6), channel_id=1, replica_groups=mesh['row'=16,'col'=8] {'row','col'}, dimensions={0} | all-to-all | bytes 1048576 | tf_op jit(solution)/shard_map/all_to_all | solution.py:486
  43.8 0.0 copy-start
  43.8 7.0 %shard_map.97 = (f32[16,128,256]{2,1,0:T(8,128)}, f32[384,128]{1,0:T(8,128)}, f32[128,128]{1,0:T(8,128)S(1)}, f32[16,256]{1,0:T(8,128)S(1)}, f32[16,256]{1,0:T(8,128)S(1)}, /*index=5*/f32[128,128]{1,0:T(8,128)S(1)}) custom-call(f32[1024,128]{1,0:T(8,128)S(1)} %bitcast.4, f32[16,128,256]{2,1,0:T(8,128)S(1)} %get-tuple-element.27.x_ref, ...), custom_call_target="tpu_custom_call" | custom-call | bytes 20000000 | tf_op jit(solution)/shard_map/pallas_call | solution.py:488
  50.9 4.6 %all-to-all-start.1 = ((f32[128,1,384]{2,1,0:T(1,128)}), f32[128,1,384]{2,1,0:T(1,128)S(1)}, u32[]{:S(2)}, u32[]{:S(2)}) async-start(f32[128,1,384]{2,1,0:T(1,128)} %bitcast.2), calls=%async_computation.1 | async-start | bytes 393216 | tf_op jit(solution)/shard_map/all_to_all | solution.py:501
  55.5 0.0 copy-done
  55.5 0.0 copy-start.1
  55.5 1.6 %copy-done.1 = f32[16,128,256]{2,1,0:T(8,128)S(1)} copy-done((f32[16,128,256]{2,1,0:T(8,128)S(1)}, f32[16,128,256]{2,1,0:T(8,128)}, u32[]{:S(2)}) %copy-start.1) | copy-done | bytes 2097176
  57.1 4.4 %shard_map.98 = f32[16,128,256]{2,1,0:T(8,128)} custom-call(s32[16]{0:T(128)S(1)} %copy-done.2, f32[16,128,256]{2,1,0:T(8,128)S(1)} %copy-done.1, f32[16,128,256]{2,1,0:T(8,128)S(1)} %copy-done, f32[128,256]{1,0:T(8,128)S(1)} %get-tuple-element.28.ee_s, f32[128,256]{1,0:T(8,128)S(1)} %get-tuple-element.29.es_s, f32[128,256]{1,0:T(8,128)S(1)} %get-tuple-element.30.leak_s, ...), custom_call_target="tpu_custom_call" | custom-call | bytes 20000000 | tf_op jit(solution)/shard_map/pallas_call | solution.py:502
  61.5 4.5 %all-to-all-done.1 = f32[128,1,384]{2,1,0:T(1,128)S(1)} async-done(((f32[128,1,384]{2,1,0:T(1,128)}), f32[128,1,384]{2,1,0:T(1,128)S(1)}, u32[]{:S(2)}, u32[]{:S(2)}) %all-to-all-start.1) | async-done | bytes 196640 | tf_op jit(solution)/shard_map/all_to_all | solution.py:501
  66.1 1.2 %shard_map.99 = f32[16,512]{1,0:T(8,128)} custom-call(f32[384,128]{1,0:T(8,128)S(1)} %bitcast.5), custom_call_target="tpu_custom_call" | custom-call | bytes 1000000 | tf_op jit(solution)/shard_map/pallas_call | solution.py:509
Async XLA Ops:
  0.6 9.7 %copy-start.2 = (s32[16]{0:T(128)S(1)}, s32[16]{0:T(128)}, u32[]{:S(2)}) copy-start(s32[16]{0:T(128)} %src_ref.3) | copy-start | bytes 196
  3.7 11.3 %collective-permute-start.3 = (f32[128,128]{1,0:T(8,128)S(1)}, f32[128,128]{1,0:T(8,128)S(1)}, u32[]{:S(2)}, u32[]{:S(2)}) collective-permute-start(f32[128,128]{1,0:T(8,128)S(1)} %get-tuple-element.36.cols_ref), channel_id=1, source_target_pairs={{1,2},{3,4},{5,6},{2,1},{4,3},{6,5},{9,10},{11,12},{13,14},{10,9},... | collective-permute-start | bytes 196616 | tf_op jit(solution)/shard_map/ppermute | solution.py:426
  8.3 6.7 %collective-permute-start.2 = (f32[128,128]{1,0:T(8,128)S(1)}, f32[128,128]{1,0:T(8,128)S(1)}, u32[]{:S(2)}, u32[]{:S(2)}) collective-permute-start(f32[128,128]{1,0:T(8,128)S(1)} %get-tuple-element.36.cols_ref), channel_id=1, source_target_pairs={{0,1},{2,3},{4,5},{6,7},{1,0},{3,2},{5,4},{7,6},{8,9},{10,11},{12,... | collective-permute-start | bytes 196616 | tf_op jit(solution)/shard_map/ppermute | solution.py:426
  8.4 6.6 %collective-permute-start = (f32[40,256]{1,0:T(8,128)S(1)}, f32[40,256]{1,0:T(8,128)S(1)}, u32[]{:S(2)}, u32[]{:S(2)}) collective-permute-start(f32[40,256]{1,0:T(8,128)S(1)} %get-tuple-element.34.own_first_ref), channel_id=1, source_target_pairs={{0,8},{16,24},{32,40},{48,56},{64,72},{80,88},{96,104},{112,120},{... | collective-permute-start | bytes 122888 | tf_op jit(solution)/shard_map/ppermute | solution.py:426
  9.7 5.3 %collective-permute-start.1 = (f32[40,256]{1,0:T(8,128)S(1)}, f32[40,256]{1,0:T(8,128)S(1)}, u32[]{:S(2)}, u32[]{:S(2)}) collective-permute-start(f32[40,256]{1,0:T(8,128)S(1)} %get-tuple-element.35.own_second_ref), channel_id=1, source_target_pairs={{8,16},{24,32},{40,48},{56,64},{72,80},{88,96},{104,112},{16,8},{3... | collective-permute-start | bytes 122888 | tf_op jit(solution)/shard_map/ppermute | solution.py:426
  43.8 11.7 %copy-start = (f32[16,128,256]{2,1,0:T(8,128)S(1)}, f32[16,128,256]{2,1,0:T(8,128)}, u32[]{:S(2)}) copy-start(f32[16,128,256]{2,1,0:T(8,128)} %d_ref.3) | copy-start | bytes 6291460
  50.9 15.2 %all-to-all-start.1 = ((f32[128,1,384]{2,1,0:T(1,128)}), f32[128,1,384]{2,1,0:T(1,128)S(1)}, u32[]{:S(2)}, u32[]{:S(2)}) async-start(f32[128,1,384]{2,1,0:T(1,128)} %bitcast.2), calls=%async_computation.1 | async-start | bytes 393216 | tf_op jit(solution)/shard_map/all_to_all | solution.py:501
  55.5 1.6 %copy-start.1 = (f32[16,128,256]{2,1,0:T(8,128)S(1)}, f32[16,128,256]{2,1,0:T(8,128)}, u32[]{:S(2)}) copy-start(f32[16,128,256]{2,1,0:T(8,128)} %get-tuple-element.23.xn_ref) | copy-start | bytes 6291460

commit v6 on v5

--- a/solution.py
+++ b/solution.py
@@ -188,8 +188,7 @@
 
 def products_body(
     d_ref, q_ref, r_ref,
-    own_first_ref, own_second_ref, far_first_ref, far_second_ref,
-    cols_ref, cols_first_ref, cols_second_ref,
+    own_first_ref, own_second_ref, cols_ref, far_second_ref, cols_second_ref, far_first_ref, cols_first_ref,
     gram_ref, nf_ref, sf_ref, cf_ref,
     q_s, r_s,
 ):
@@ -269,9 +268,27 @@
     return both[0:128] + both[128:256]
 
 
+def part(system, p):
+    lane = iota((16, 128), 1)
+    return jnp.where(lane < 16, pltpu.roll(system, 128 - 16 * p, 1), 0.0)
+
+
+def padded(coef):
+    return stack2(coef, jnp.zeros((112, 128), F32))
+
+
+def widen(coef):
+    i = iota((128, 128), 0)
+    j = iota((128, 128), 1)
+    repeat_rows = jnp.where((i >> 3) == j, 1.0, 0.0)
+    repeat_lanes = jnp.where(i == (j >> 3), 1.0, 0.0)
+    wide = dot_full(dot_full(repeat_rows, padded(coef), 1, 1), repeat_lanes)
+    return jnp.where((i & 7) == (j & 7), wide, 0.0)
+
+
 def iterate_body(
     gram_ref, x_ref, d_ref, ee_s, es_s, slot_ref, ids_ref, nf_ref, sf_ref, cf_ref,
-    out_ref, msg_ref, beta_ref, nn_ref, sn_ref, cn_ref,
+    out_ref, msg_ref, system_ref, nn_ref, sn_ref, cn_ref,
     xn_ref, cur_s, turn_s, sem,
 ):
     packed = gram_ref[...].reshape(DEVICES, 8, 128).sum(axis=0)
@@ -287,30 +304,17 @@
         pivot = pivot / pivot[:, j : j + 1]
         system = jnp.where(row == j, pivot, system - system[:, j : j + 1] * pivot)
 
-    def part(p):
-        return jnp.where(lane < 16, pltpu.roll(system, 128 - 16 * p, 1), 0.0)
-
-    alpha = part(1)
-    blank = jnp.zeros((112, 128), F32)
-    alpha_pad = stack2(alpha, blank)
+    system_ref[...] = system
+    alpha = part(system, 1)
     i = iota((128, 128), 0)
     j = iota((128, 128), 1)
-    same = (i & 7) == (j & 7)
-    repeat_rows = jnp.where((i >> 3) == j, 1.0, 0.0)
-    repeat_lanes = jnp.where(i == (j >> 3), 1.0, 0.0)
-
-    def widen(coef):
-        return jnp.where(same, dot_full(dot_full(repeat_rows, coef, 1, 1), repeat_lanes), 0.0)
-
-    mix = mixer(widen(alpha_pad))
+    mix = mixer(widen(alpha))
     for b in range(CR // 8):
         rows = slice(8 * b, 8 * b + 8)
         step = mixed(mix, d_ref[:, rows, :].reshape(128, CC))
         xn_ref[:, rows, :] = x_ref[:, rows, :] + step.reshape(16, 8, CC)
     leave = pltpu.make_async_copy(xn_ref, out_ref, sem)
     leave.start()
-    beta = dot_full(part(2), alpha_pad) - part(3)
-    beta_ref[...] = widen(stack2(beta, blank))
     base = jnp.concatenate(
         [jnp.where(row == lane, 1.0, 0.0), alpha, jnp.zeros((96, 128), F32)], axis=0
     )
@@ -353,14 +357,15 @@
     outer = jnp.concatenate(
         [turn_s[pl.ds(1, 16, stride=2), :], turn_s[pl.ds(0, 16, stride=2), :]], axis=1
     )
-    outer = stack2(*split(outer))
+    band = (iota((K, CC), 1) & 127) >> 4
+    outer = jnp.concatenate([jnp.where(band == i, outer, 0.0) for i in range(8)], axis=0)
     target = ((cell >> 2) & 3) * 64 + jnp.where(cell < 128, 0, 63)
-    band = (cell & 127) >> 4
+    rim = dot(stack2(*split(outer)), one_hot(spot == target))
+    blocks = 0.5 * (blocks + (rim[0:128] + rim[128:256]))
     owner = iota((128, CC), 0)
     stacked = jnp.zeros((256, 128), F32)
     for b in range(8):
-        rim = dot(outer, one_hot((spot == target) & (band == b)))
-        inner = 0.5 * (blocks[16 * b : 16 * b + 16] + (rim[0:16] + rim[16:32]))
+        inner = blocks[16 * b : 16 * b + 16]
         slot = slot_ref[b : b + 1, :]
         entry = jnp.broadcast_to(slot >> 7, (16, CC))
         spread = jnp.concatenate([jnp.where(entry == e, inner, 0.0) for e in range(SLOTS)], axis=0)
@@ -374,10 +379,12 @@
 
 
 def direction_body(
-    src_ref, xn_ref, d_ref, ee_s, es_s, leak_s, poc_ref, beta_ref, nn_ref, sn_ref, cn_ref,
+    src_ref, xn_ref, d_ref, ee_s, es_s, leak_s, poc_ref, system_ref, nn_ref, sn_ref, cn_ref,
     do_ref, db_s,
 ):
-    mix = mixer(beta_ref[...])
+    system = system_ref[...]
+    beta = dot_full(part(system, 2), padded(part(system, 1))) - part(system, 3)
+    mix = mixer(widen(beta))
     for b in range(CR // 8):
         rows = slice(8 * b, 8 * b + 8)
         step = mixed(mix, d_ref[:, rows, :].reshape(128, CC))
@@ -481,13 +488,13 @@
         moved=20_000_000,
     )(
         d_held, image, part,
-        first, second, far_first, far_second, columns, cols_first, cols_second,
+        first, second, columns, far_second, cols_second, far_first, cols_first,
     )
     gram = lax.all_to_all(gram, AXES, 0, 0, tiled=True)
 
-    new_iterate, message, beta, nn, sn, cn = call(
+    new_iterate, message, system, nn, sn, cn = call(
         iterate_body,
-        (f32(K, CR, CC), f32(DEVICES * 3, 128), f32(128, 128), f32(16, CC), f32(16, CC), f32(CR, 128)),
+        (f32(K, CR, CC), f32(DEVICES * 3, 128), f32(16, 128), f32(16, CC), f32(16, CC), f32(CR, 128)),
         scratch=[
             field,
             field,
@@ -505,7 +512,7 @@
         scratch=[field],
         specs=[smem] + [vmem] * 10,
         moved=20_000_000,
-    )(sources, new_iterate, direction, ee, es, leak, patch_of_cell, beta, nn, sn, cn)
+    )(sources, new_iterate, direction, ee, es, leak, patch_of_cell, system, nn, sn, cn)
     migration = call(
         owner_body,
         f32(K, PATCH_DEV),

time: 67.5 us -> 66.6 us (0.987)
  blocking collectives: 26.1 us -> 25.4 us
  transfers between devices with their start and end apart: 5 -> 5, of which waited for: 1 -> 1; matrix products, arithmetic and copies ran while one was open for 0% -> 0% of each run, Pallas kernels for 13% -> 14%
where the time goes in v6:
time: 66.6 us; the launch traced here: 66.4 us
  blocking collectives  25.4 us (38%)
  Pallas kernels  23.1 us (35%)
  starting transfers between devices  11.2 us (17%)
  waiting for transfers between devices  4.34 us (7%)
  local copies, waits for them, and re-layouts  1.59 us (2%)
  between operations  0.75 us (1%)
    all_to_all x1, blocking collectives, on_device(): gram = lax.all_to_all(gram, AXES, 0, 0, tiled=True)  25.4 us
    pallas_call x1, Pallas kernels, on_device(): call(iterate_body, (f32(K, CR, CC), f32(DEVICES * 3, 128), f32(16, 128),...  6.86 us
    ppermute x4, starting transfers between devices, neighbours(): lax.ppermute(value, axis, [(i, i + 1) for i in starts] + [(i + 1, i) for...  6.63 us
    pallas_call x1, Pallas kernels, on_device(): call(fields_body, (pltpu.VMEM((K, CR, CC), F32), pltpu.VMEM((K, CR, CC),...  4.63 us
    pallas_call x1, Pallas kernels, on_device(): call(direction_body, f32(K, CR, CC), scratch=[field], specs=[smem] + [vme...  4.63 us
    all_to_all x1, starting transfers between devices, on_device(): lax.all_to_all(message.reshape(DEVICES, 1, 384), AXES, 0, 0, tiled=True)  4.58 us
    all_to_all x1, waiting for transfers between devices, on_device(): lax.all_to_all(message.reshape(DEVICES, 1, 384), AXES, 0, 0, tiled=True)  4.33 us
    pallas_call x1, Pallas kernels, on_device(): call(front_body, (pltpu.VMEM((40, CC), F32), pltpu.VMEM((40, CC), F32), p...  3.02 us
  transfers between devices with their start and end apart: 5, of which 1 were waited for; matrix products, arithmetic and copies ran while one was open for 0% of the time, Pallas kernels for 14%

profile of v6, /device:TPU:1, one launch (start us, length us, event | category | flops | bytes accessed | tf_op | source)
XLA Modules:
  0.0 66.4 jit_solution(3987809038897042258)
XLA Ops:
  0.6 0.0 copy-start.2
  0.6 3.0 %shard_map.94 = (f32[40,256]{1,0:T(8,128)S(1)}, f32[40,256]{1,0:T(8,128)S(1)}, f32[128,128]{1,0:T(8,128)S(1)}, f32[16,128,256]{2,1,0:T(8,128)S(1)}, f32[16,128,2...) custom-call(f32[16,128,256]{2,1,0:T(8,128)} %x_ref.1, ...), custom_call_target="tpu_custom_call" | custom-call | bytes 8000000 | tf_op jit(solution)/shard_map/pallas_call | solution.py:443
  3.7 1.5 %collective-permute-start.3 = (f32[128,128]{1,0:T(8,128)S(1)}, f32[128,128]{1,0:T(8,128)S(1)}, u32[]{:S(2)}, u32[]{:S(2)}) collective-permute-start(f32[128,128]{1,0:T(8,128)S(1)} %get-tuple-element.36.cols_ref), channel_id=1, source_target_pairs={{0,1},{2,3},{4,5},{6,7},{1,0},{3,2},{5,4},{7,6},{8,9},{10,11},{12,... | collective-permute-start | bytes 196616 | tf_op jit(solution)/shard_map/ppermute | solution.py:433
  5.2 3.2 %collective-permute-start.1 = (f32[128,128]{1,0:T(8,128)S(1)}, f32[128,128]{1,0:T(8,128)S(1)}, u32[]{:S(2)}, u32[]{:S(2)}) collective-permute-start(f32[128,128]{1,0:T(8,128)S(1)} %get-tuple-element.36.cols_ref), channel_id=1, source_target_pairs={{1,2},{3,4},{5,6},{2,1},{4,3},{6,5},{9,10},{11,12},{13,14},{10,9},... | collective-permute-start | bytes 196616 | tf_op jit(solution)/shard_map/ppermute | solution.py:433
  8.4 1.3 %collective-permute-start.2 = (f32[40,256]{1,0:T(8,128)S(1)}, f32[40,256]{1,0:T(8,128)S(1)}, u32[]{:S(2)}, u32[]{:S(2)}) collective-permute-start(f32[40,256]{1,0:T(8,128)S(1)} %get-tuple-element.34.own_first_ref), channel_id=1, source_target_pairs={{0,8},{16,24},{32,40},{48,56},{64,72},{80,88},{96,104},{112,120},{... | collective-permute-start | bytes 122888 | tf_op jit(solution)/shard_map/ppermute | solution.py:433
  9.7 0.7 collective-permute-start
  10.3 0.0 copy-done.2
  10.3 4.6 %shard_map.95 = (f32[16,128,256]{2,1,0:T(8,128)S(1)}, f32[16,128,256]{2,1,0:T(8,128)S(1)}) custom-call(s32[16]{0:T(128)S(1)} %copy-done.2, f32[16,128,256]{2,1,0:T(8,128)S(1)} %get-tuple-element.27.x_ref, f32[16,128,256]{2,1,0:T(8,128)S(1)} %get-tuple-element.26.d_ref, f32[128,256]{1,0:T(8,128)S(1)} %get-tuple-element.28.ee_s, ...), custom_call_target="tpu_custom_call" | custom-call | bytes 12000000 | tf_op jit(solution)/shard_map/pallas_call | solution.py:475
  15.0 0.0 collective-permute-done.2.far_first_ref
  15.0 0.0 collective-permute-done.far_second_ref
  15.0 0.0 collective-permute-done.3.cols_first_ref
  15.0 0.0 collective-permute-done.1.cols_second_ref
  15.0 2.8 %shard_map.96 = (f32[1024,128]{1,0:T(8,128)S(1)}, f32[32,256]{1,0:T(8,128)S(1)}, f32[32,256]{1,0:T(8,128)S(1)}, f32[128,128]{1,0:T(8,128)S(1)}) custom-call(f32[16,128,256]{2,1,0:T(8,128)S(1)} %get-tuple-element.26.d_ref, f32[16,128,256]{2,1,0:T(8,128)S(1)} %get-tuple-element.32.q_ref, f32[16,128,256]{2,1,0:T(8,128)S(1)} %get-tuple-element.33.r_ref, ...), custom_call_target="tpu_custom_call" | custom-call | bytes 20000000 | tf_op jit(solution)/shard_map/pallas_call | solution.py:483
  17.8 25.4 %all_to_all.16 = f32[128,8,128]{2,1,0:T(8,128)S(1)} all-to-all(f32[128,8,128]{2,1,0:T(8,128)S(1)} %bitcast.6), channel_id=1, replica_groups=mesh['row'=16,'col'=8] {'row','col'}, dimensions={0} | all-to-all | bytes 1048576 | tf_op jit(solution)/shard_map/all_to_all | solution.py:493
  43.2 0.0 copy-start
  43.2 6.9 %shard_map.97 = (f32[16,128,256]{2,1,0:T(8,128)}, f32[384,128]{1,0:T(8,128)}, f32[16,128]{1,0:T(8,128)S(1)}, f32[16,256]{1,0:T(8,128)S(1)}, f32[16,256]{1,0:T(8,128)S(1)}, /*index=5*/f32[128,128]{1,0:T(8,128)S(1)}) custom-call(f32[1024,128]{1,0:T(8,128)S(1)} %bitcast.4, f32[16,128,256]{2,1,0:T(8,128)S(1)} %get-tuple-element.27.x_ref, ...), custom_call_target="tpu_custom_call" | custom-call | bytes 20000000 | tf_op jit(solution)/shard_map/pallas_call | solution.py:495
  50.0 4.6 %all-to-all-start.1 = ((f32[128,1,384]{2,1,0:T(1,128)}), f32[128,1,384]{2,1,0:T(1,128)S(1)}, u32[]{:S(2)}, u32[]{:S(2)}) async-start(f32[128,1,384]{2,1,0:T(1,128)} %bitcast.2), calls=%async_computation.1 | async-start | bytes 393216 | tf_op jit(solution)/shard_map/all_to_all | solution.py:508
  54.6 0.0 copy-done
  54.6 0.0 copy-start.1
  54.7 1.6 %copy-done.1 = f32[16,128,256]{2,1,0:T(8,128)S(1)} copy-done((f32[16,128,256]{2,1,0:T(8,128)S(1)}, f32[16,128,256]{2,1,0:T(8,128)}, u32[]{:S(2)}) %copy-start.1) | copy-done | bytes 2097176
  56.2 4.6 %shard_map.98 = f32[16,128,256]{2,1,0:T(8,128)} custom-call(s32[16]{0:T(128)S(1)} %copy-done.2, f32[16,128,256]{2,1,0:T(8,128)S(1)} %copy-done.1, f32[16,128,256]{2,1,0:T(8,128)S(1)} %copy-done, f32[128,256]{1,0:T(8,128)S(1)} %get-tuple-element.28.ee_s, f32[128,256]{1,0:T(8,128)S(1)} %get-tuple-element.29.es_s, f32[128,256]{1,0:T(8,128)S(1)} %get-tuple-element.30.leak_s, ...), custom_call_target="tpu_custom_call" | custom-call | bytes 20000000 | tf_op jit(solution)/shard_map/pallas_call | solution.py:509
  60.9 4.3 %all-to-all-done.1 = f32[128,1,384]{2,1,0:T(1,128)S(1)} async-done(((f32[128,1,384]{2,1,0:T(1,128)}), f32[128,1,384]{2,1,0:T(1,128)S(1)}, u32[]{:S(2)}, u32[]{:S(2)}) %all-to-all-start.1) | async-done | bytes 196640 | tf_op jit(solution)/shard_map/all_to_all | solution.py:508
  65.2 1.2 %shard_map.99 = f32[16,512]{1,0:T(8,128)} custom-call(f32[384,128]{1,0:T(8,128)S(1)} %bitcast.5), custom_call_target="tpu_custom_call" | custom-call | bytes 1000000 | tf_op jit(solution)/shard_map/pallas_call | solution.py:516
Async XLA Ops:
  0.6 9.7 %copy-start.2 = (s32[16]{0:T(128)S(1)}, s32[16]{0:T(128)}, u32[]{:S(2)}) copy-start(s32[16]{0:T(128)} %src_ref.3) | copy-start | bytes 196
  3.7 11.3 %collective-permute-start.3 = (f32[128,128]{1,0:T(8,128)S(1)}, f32[128,128]{1,0:T(8,128)S(1)}, u32[]{:S(2)}, u32[]{:S(2)}) collective-permute-start(f32[128,128]{1,0:T(8,128)S(1)} %get-tuple-element.36.cols_ref), channel_id=1, source_target_pairs={{0,1},{2,3},{4,5},{6,7},{1,0},{3,2},{5,4},{7,6},{8,9},{10,11},{12,... | collective-permute-start | bytes 196616 | tf_op jit(solution)/shard_map/ppermute | solution.py:433
  5.2 9.8 %collective-permute-start.1 = (f32[128,128]{1,0:T(8,128)S(1)}, f32[128,128]{1,0:T(8,128)S(1)}, u32[]{:S(2)}, u32[]{:S(2)}) collective-permute-start(f32[128,128]{1,0:T(8,128)S(1)} %get-tuple-element.36.cols_ref), channel_id=1, source_target_pairs={{1,2},{3,4},{5,6},{2,1},{4,3},{6,5},{9,10},{11,12},{13,14},{10,9},... | collective-permute-start | bytes 196616 | tf_op jit(solution)/shard_map/ppermute | solution.py:433
  8.4 6.6 %collective-permute-start.2 = (f32[40,256]{1,0:T(8,128)S(1)}, f32[40,256]{1,0:T(8,128)S(1)}, u32[]{:S(2)}, u32[]{:S(2)}) collective-permute-start(f32[40,256]{1,0:T(8,128)S(1)} %get-tuple-element.34.own_first_ref), channel_id=1, source_target_pairs={{0,8},{16,24},{32,40},{48,56},{64,72},{80,88},{96,104},{112,120},{... | collective-permute-start | bytes 122888 | tf_op jit(solution)/shard_map/ppermute | solution.py:433
  9.7 5.3 %collective-permute-start = (f32[40,256]{1,0:T(8,128)S(1)}, f32[40,256]{1,0:T(8,128)S(1)}, u32[]{:S(2)}, u32[]{:S(2)}) collective-permute-start(f32[40,256]{1,0:T(8,128)S(1)} %get-tuple-element.35.own_second_ref), channel_id=1, source_target_pairs={{8,16},{24,32},{40,48},{56,64},{72,80},{88,96},{104,112},{16,8},{3... | collective-permute-start | bytes 122888 | tf_op jit(solution)/shard_map/ppermute | solution.py:433
  43.2 11.5 %copy-start = (f32[16,128,256]{2,1,0:T(8,128)S(1)}, f32[16,128,256]{2,1,0:T(8,128)}, u32[]{:S(2)}) copy-start(f32[16,128,256]{2,1,0:T(8,128)} %d_ref.3) | copy-start | bytes 6291460
  50.0 15.1 %all-to-all-start.1 = ((f32[128,1,384]{2,1,0:T(1,128)}), f32[128,1,384]{2,1,0:T(1,128)S(1)}, u32[]{:S(2)}, u32[]{:S(2)}) async-start(f32[128,1,384]{2,1,0:T(1,128)} %bitcast.2), calls=%async_computation.1 | async-start | bytes 393216 | tf_op jit(solution)/shard_map/all_to_all | solution.py:508
  54.6 1.6 %copy-start.1 = (f32[16,128,256]{2,1,0:T(8,128)S(1)}, f32[16,128,256]{2,1,0:T(8,128)}, u32[]{:S(2)}) copy-start(f32[16,128,256]{2,1,0:T(8,128)} %get-tuple-element.23.xn_ref) | copy-start | bytes 6291460

commit v7 on v6

--- a/solution.py
+++ b/solution.py
@@ -72,24 +72,25 @@
     poc_ref, slot_ref, ids_ref, ee_ref, es_ref, leak_ref,
     c_s, gr_s, whole_s, tp_s, lp_s, sems,
 ):
-    pairs = [(x_ref.at[k], xv_ref.at[k]) for k in range(K)]
-    pairs += [(d_ref.at[k], dv_ref.at[k]) for k in range(K)]
+    fields = [xv_ref.at[k] for k in range(K)] + [dv_ref.at[k] for k in range(K)] + [c_s]
+    quads = [pl.ds(4 * g, 4) for g in range(4)]
+    pairs = [(x_ref.at[quad], xv_ref.at[quad]) for quad in quads]
+    pairs += [(d_ref.at[quad], dv_ref.at[quad]) for quad in quads]
     pairs += [(c_ref, c_s), (gr_ref, gr_s), (lp_ref, whole_s), (tp_ref, tp_s)]
     copies = [pltpu.make_async_copy(*pair, sems.at[f]) for f, pair in enumerate(pairs)]
-    for copy in copies[32:] + copies[:32]:
+    for copy in copies[8:] + copies[:8]:
         copy.start()
-    for copy in copies[32:]:
+    for copy in copies[8:]:
         copy.wait()
     prepare(whole_s, tp_s, c_s, gr_s, poc_ref, slot_ref, ids_ref, ee_ref, es_ref, leak_ref, lp_s)
     even = jnp.bitwise_and(lax.axis_index("row"), 1) == 0
     lane = iota((CR, 128), 1)
     packed = jnp.zeros((CR, 128), F32)
     for group in (range(0, 8), range(8, 16), range(16, 24), range(24, 33)):
+        for g in range(group[0] // 4, group[0] // 4 + 2):
+            copies[g].wait()
         for f in group:
-            if f < 32:
-                copies[f].wait()
-        for f in group:
-            ref = pairs[f][1]
+            ref = fields[f]
             top = ref[0:1, :]
             bottom = ref[CR - 1 : CR, :]
             first_ref[f : f + 1, :] = jnp.where(even, bottom, top)
@@ -300,9 +301,9 @@
     system = jnp.where(lane < 32, small[0:16], pltpu.roll(small[16:32], 32, 1))
     system = jnp.where(lane < 64, system, 0.0)
     for j in range(K):
-        pivot = system[j : j + 1, :]
-        pivot = pivot / pivot[:, j : j + 1]
-        system = jnp.where(row == j, pivot, system - system[:, j : j + 1] * pivot)
+        column = jnp.broadcast_to(system[:, j : j + 1], (16, 128))
+        pivot = system[j : j + 1, :] / column[j : j + 1, :]
+        system = jnp.where(row == j, pivot, system - column * pivot)
 
     system_ref[...] = system
     alpha = part(system, 1)
@@ -461,7 +462,7 @@
             pltpu.VMEM((CR, CC), jnp.int32),
             pltpu.VMEM((1, 1, 2048), jnp.int32),
             pltpu.VMEM((2, CR, 128), jnp.int32),
-            pltpu.SemaphoreType.DMA((36,)),
+            pltpu.SemaphoreType.DMA((12,)),
         ],
         specs=[hbm] * 6,
         places=(vmem,) * 11,

time: 66.6 us -> 66.4 us (level)
  no operation moved by 1% of the time
where the time goes in v7:
time: 66.4 us; the launch traced here: 66.2 us
  blocking collectives  25.4 us (38%)
  Pallas kernels  22.9 us (34%)
  starting transfers between devices  11.2 us (17%)
  waiting for transfers between devices  4.34 us (7%)
  local copies, waits for them, and re-layouts  1.59 us (2%)
  between operations  0.75 us (1%)
    all_to_all x1, blocking collectives, on_device(): gram = lax.all_to_all(gram, AXES, 0, 0, tiled=True)  25.4 us
    pallas_call x1, Pallas kernels, on_device(): call(iterate_body, (f32(K, CR, CC), f32(DEVICES * 3, 128), f32(16, 128),...  6.86 us
    ppermute x4, starting transfers between devices, neighbours(): lax.ppermute(value, axis, [(i, i + 1) for i in starts] + [(i + 1, i) for...  6.63 us
    pallas_call x1, Pallas kernels, on_device(): call(fields_body, (pltpu.VMEM((K, CR, CC), F32), pltpu.VMEM((K, CR, CC),...  4.63 us
    pallas_call x1, Pallas kernels, on_device(): call(direction_body, f32(K, CR, CC), scratch=[field], specs=[smem] + [vme...  4.63 us
    all_to_all x1, starting transfers between devices, on_device(): lax.all_to_all(message.reshape(DEVICES, 1, 384), AXES, 0, 0, tiled=True)  4.58 us
    all_to_all x1, waiting for transfers between devices, on_device(): lax.all_to_all(message.reshape(DEVICES, 1, 384), AXES, 0, 0, tiled=True)  4.33 us
    pallas_call x1, Pallas kernels, on_device(): call(front_body, (pltpu.VMEM((40, CC), F32), pltpu.VMEM((40, CC), F32), p...  2.77 us
  transfers between devices with their start and end apart: 5, of which 1 were waited for; matrix products, arithmetic and copies ran while one was open for 0% of the time, Pallas kernels for 14%

profile of v7, /device:TPU:1, one launch (start us, length us, event | category | flops | bytes accessed | tf_op | source)
XLA Modules:
  0.0 66.2 jit_solution(5598230938840058335)
XLA Ops:
  0.6 0.0 copy-start.2
  0.6 2.8 %shard_map.94 = (f32[40,256]{1,0:T(8,128)S(1)}, f32[40,256]{1,0:T(8,128)S(1)}, f32[128,128]{1,0:T(8,128)S(1)}, f32[16,128,256]{2,1,0:T(8,128)S(1)}, f32[16,128,2...) custom-call(f32[16,128,256]{2,1,0:T(8,128)} %x_ref.1, ...), custom_call_target="tpu_custom_call" | custom-call | bytes 8000000 | tf_op jit(solution)/shard_map/pallas_call | solution.py:444
  3.4 1.5 %collective-permute-start.3 = (f32[128,128]{1,0:T(8,128)S(1)}, f32[128,128]{1,0:T(8,128)S(1)}, u32[]{:S(2)}, u32[]{:S(2)}) collective-permute-start(f32[128,128]{1,0:T(8,128)S(1)} %get-tuple-element.36.cols_ref), channel_id=1, source_target_pairs={{0,1},{2,3},{4,5},{6,7},{1,0},{3,2},{5,4},{7,6},{8,9},{10,11},{12,... | collective-permute-start | bytes 196616 | tf_op jit(solution)/shard_map/ppermute | solution.py:434
  4.9 3.2 %collective-permute-start.1 = (f32[128,128]{1,0:T(8,128)S(1)}, f32[128,128]{1,0:T(8,128)S(1)}, u32[]{:S(2)}, u32[]{:S(2)}) collective-permute-start(f32[128,128]{1,0:T(8,128)S(1)} %get-tuple-element.36.cols_ref), channel_id=1, source_target_pairs={{1,2},{3,4},{5,6},{2,1},{4,3},{6,5},{9,10},{11,12},{13,14},{10,9},... | collective-permute-start | bytes 196616 | tf_op jit(solution)/shard_map/ppermute | solution.py:434
  8.1 1.3 %collective-permute-start.2 = (f32[40,256]{1,0:T(8,128)S(1)}, f32[40,256]{1,0:T(8,128)S(1)}, u32[]{:S(2)}, u32[]{:S(2)}) collective-permute-start(f32[40,256]{1,0:T(8,128)S(1)} %get-tuple-element.34.own_first_ref), channel_id=1, source_target_pairs={{0,8},{16,24},{32,40},{48,56},{64,72},{80,88},{96,104},{112,120},{... | collective-permute-start | bytes 122888 | tf_op jit(solution)/shard_map/ppermute | solution.py:434
  9.4 0.7 collective-permute-start
  10.1 0.0 copy-done.2
  10.1 4.6 %shard_map.95 = (f32[16,128,256]{2,1,0:T(8,128)S(1)}, f32[16,128,256]{2,1,0:T(8,128)S(1)}) custom-call(s32[16]{0:T(128)S(1)} %copy-done.2, f32[16,128,256]{2,1,0:T(8,128)S(1)} %get-tuple-element.27.x_ref, f32[16,128,256]{2,1,0:T(8,128)S(1)} %get-tuple-element.26.d_ref, f32[128,256]{1,0:T(8,128)S(1)} %get-tuple-element.28.ee_s, ...), custom_call_target="tpu_custom_call" | custom-call | bytes 12000000 | tf_op jit(solution)/shard_map/pallas_call | solution.py:476
  14.7 0.0 collective-permute-done.2.far_first_ref
  14.7 0.0 collective-permute-done.far_second_ref
  14.7 0.0 collective-permute-done.3.cols_first_ref
  14.7 0.0 collective-permute-done.1.cols_second_ref
  14.8 2.8 %shard_map.96 = (f32[1024,128]{1,0:T(8,128)S(1)}, f32[32,256]{1,0:T(8,128)S(1)}, f32[32,256]{1,0:T(8,128)S(1)}, f32[128,128]{1,0:T(8,128)S(1)}) custom-call(f32[16,128,256]{2,1,0:T(8,128)S(1)} %get-tuple-element.26.d_ref, f32[16,128,256]{2,1,0:T(8,128)S(1)} %get-tuple-element.32.q_ref, f32[16,128,256]{2,1,0:T(8,128)S(1)} %get-tuple-element.33.r_ref, ...), custom_call_target="tpu_custom_call" | custom-call | bytes 20000000 | tf_op jit(solution)/shard_map/pallas_call | solution.py:484
  17.5 25.4 %all_to_all.16 = f32[128,8,128]{2,1,0:T(8,128)S(1)} all-to-all(f32[128,8,128]{2,1,0:T(8,128)S(1)} %bitcast.6), channel_id=1, replica_groups=mesh['row'=16,'col'=8] {'row','col'}, dimensions={0} | all-to-all | bytes 1048576 | tf_op jit(solution)/shard_map/all_to_all | solution.py:494
  42.9 0.0 copy-start
  42.9 6.9 %shard_map.97 = (f32[16,128,256]{2,1,0:T(8,128)}, f32[384,128]{1,0:T(8,128)}, f32[16,128]{1,0:T(8,128)S(1)}, f32[16,256]{1,0:T(8,128)S(1)}, f32[16,256]{1,0:T(8,128)S(1)}, /*index=5*/f32[128,128]{1,0:T(8,128)S(1)}) custom-call(f32[1024,128]{1,0:T(8,128)S(1)} %bitcast.4, f32[16,128,256]{2,1,0:T(8,128)S(1)} %get-tuple-element.27.x_ref, ...), custom_call_target="tpu_custom_call" | custom-call | bytes 20000000 | tf_op jit(solution)/shard_map/pallas_call | solution.py:496
  49.8 4.6 %all-to-all-start.1 = ((f32[128,1,384]{2,1,0:T(1,128)}), f32[128,1,384]{2,1,0:T(1,128)S(1)}, u32[]{:S(2)}, u32[]{:S(2)}) async-start(f32[128,1,384]{2,1,0:T(1,128)} %bitcast.2), calls=%async_computation.1 | async-start | bytes 393216 | tf_op jit(solution)/shard_map/all_to_all | solution.py:509
  54.4 0.0 copy-done
  54.4 0.0 copy-start.1
  54.4 1.6 %copy-done.1 = f32[16,128,256]{2,1,0:T(8,128)S(1)} copy-done((f32[16,128,256]{2,1,0:T(8,128)S(1)}, f32[16,128,256]{2,1,0:T(8,128)}, u32[]{:S(2)}) %copy-start.1) | copy-done | bytes 2097176
  56.0 4.6 %shard_map.98 = f32[16,128,256]{2,1,0:T(8,128)} custom-call(s32[16]{0:T(128)S(1)} %copy-done.2, f32[16,128,256]{2,1,0:T(8,128)S(1)} %copy-done.1, f32[16,128,256]{2,1,0:T(8,128)S(1)} %copy-done, f32[128,256]{1,0:T(8,128)S(1)} %get-tuple-element.28.ee_s, f32[128,256]{1,0:T(8,128)S(1)} %get-tuple-element.29.es_s, f32[128,256]{1,0:T(8,128)S(1)} %get-tuple-element.30.leak_s, ...), custom_call_target="tpu_custom_call" | custom-call | bytes 20000000 | tf_op jit(solution)/shard_map/pallas_call | solution.py:510
  60.6 4.3 %all-to-all-done.1 = f32[128,1,384]{2,1,0:T(1,128)S(1)} async-done(((f32[128,1,384]{2,1,0:T(1,128)}), f32[128,1,384]{2,1,0:T(1,128)S(1)}, u32[]{:S(2)}, u32[]{:S(2)}) %all-to-all-start.1) | async-done | bytes 196640 | tf_op jit(solution)/shard_map/all_to_all | solution.py:509
  64.9 1.2 %shard_map.99 = f32[16,512]{1,0:T(8,128)} custom-call(f32[384,128]{1,0:T(8,128)S(1)} %bitcast.5), custom_call_target="tpu_custom_call" | custom-call | bytes 1000000 | tf_op jit(solution)/shard_map/pallas_call | solution.py:517
Async XLA Ops:
  0.6 9.4 %copy-start.2 = (s32[16]{0:T(128)S(1)}, s32[16]{0:T(128)}, u32[]{:S(2)}) copy-start(s32[16]{0:T(128)} %src_ref.3) | copy-start | bytes 196
  3.4 11.3 %collective-permute-start.3 = (f32[128,128]{1,0:T(8,128)S(1)}, f32[128,128]{1,0:T(8,128)S(1)}, u32[]{:S(2)}, u32[]{:S(2)}) collective-permute-start(f32[128,128]{1,0:T(8,128)S(1)} %get-tuple-element.36.cols_ref), channel_id=1, source_target_pairs={{0,1},{2,3},{4,5},{6,7},{1,0},{3,2},{5,4},{7,6},{8,9},{10,11},{12,... | collective-permute-start | bytes 196616 | tf_op jit(solution)/shard_map/ppermute | solution.py:434
  4.9 9.8 %collective-permute-start.1 = (f32[128,128]{1,0:T(8,128)S(1)}, f32[128,128]{1,0:T(8,128)S(1)}, u32[]{:S(2)}, u32[]{:S(2)}) collective-permute-start(f32[128,128]{1,0:T(8,128)S(1)} %get-tuple-element.36.cols_ref), channel_id=1, source_target_pairs={{1,2},{3,4},{5,6},{2,1},{4,3},{6,5},{9,10},{11,12},{13,14},{10,9},... | collective-permute-start | bytes 196616 | tf_op jit(solution)/shard_map/ppermute | solution.py:434
  8.1 6.6 %collective-permute-start.2 = (f32[40,256]{1,0:T(8,128)S(1)}, f32[40,256]{1,0:T(8,128)S(1)}, u32[]{:S(2)}, u32[]{:S(2)}) collective-permute-start(f32[40,256]{1,0:T(8,128)S(1)} %get-tuple-element.34.own_first_ref), channel_id=1, source_target_pairs={{0,8},{16,24},{32,40},{48,56},{64,72},{80,88},{96,104},{112,120},{... | collective-permute-start | bytes 122888 | tf_op jit(solution)/shard_map/ppermute | solution.py:434
  9.4 5.3 %collective-permute-start = (f32[40,256]{1,0:T(8,128)S(1)}, f32[40,256]{1,0:T(8,128)S(1)}, u32[]{:S(2)}, u32[]{:S(2)}) collective-permute-start(f32[40,256]{1,0:T(8,128)S(1)} %get-tuple-element.35.own_second_ref), channel_id=1, source_target_pairs={{8,16},{24,32},{40,48},{56,64},{72,80},{88,96},{104,112},{16,8},{3... | collective-permute-start | bytes 122888 | tf_op jit(solution)/shard_map/ppermute | solution.py:434
  42.9 11.5 %copy-start = (f32[16,128,256]{2,1,0:T(8,128)S(1)}, f32[16,128,256]{2,1,0:T(8,128)}, u32[]{:S(2)}) copy-start(f32[16,128,256]{2,1,0:T(8,128)} %d_ref.3) | copy-start | bytes 6291460
  49.8 15.1 %all-to-all-start.1 = ((f32[128,1,384]{2,1,0:T(1,128)}), f32[128,1,384]{2,1,0:T(1,128)S(1)}, u32[]{:S(2)}, u32[]{:S(2)}) async-start(f32[128,1,384]{2,1,0:T(1,128)} %bitcast.2), calls=%async_computation.1 | async-start | bytes 393216 | tf_op jit(solution)/shard_map/all_to_all | solution.py:509
  54.4 1.6 %copy-start.1 = (f32[16,128,256]{2,1,0:T(8,128)S(1)}, f32[16,128,256]{2,1,0:T(8,128)}, u32[]{:S(2)}) copy-start(f32[16,128,256]{2,1,0:T(8,128)} %get-tuple-element.23.xn_ref) | copy-start | bytes 6291460

commit v8 on v7

--- a/solution.py
+++ b/solution.py
@@ -246,7 +246,8 @@
         ll = stack2(dl, ql)
         gh = stack2(qh, rh)
         gl = stack2(ql, rl)
-        acc = acc + (dot(lh, gh, 1, 1) + (dot(lh, gl, 1, 1) + dot(ll, gh, 1, 1)))
+        left = jnp.concatenate([lh, lh, ll], axis=1)
+        acc = acc + dot(left, jnp.concatenate([gh, gl, gh], axis=1), 1, 1)
     i = iota((256, 256), 0)
     j = iota((256, 256), 1)
     kept = jnp.where((i & 7) == (j & 7), acc, 0.0)

time: 66.4 us -> 66.4 us (level)
  no operation moved by 1% of the time
where the time goes in v8:
time: 66.4 us; the launch traced here: 66.2 us
  blocking collectives  25.4 us (38%)
  Pallas kernels  22.9 us (34%)
  starting transfers between devices  11.2 us (17%)
  waiting for transfers between devices  4.34 us (7%)
  local copies, waits for them, and re-layouts  1.59 us (2%)
  between operations  0.75 us (1%)
    all_to_all x1, blocking collectives, on_device(): gram = lax.all_to_all(gram, AXES, 0, 0, tiled=True)  25.4 us
    pallas_call x1, Pallas kernels, on_device(): call(iterate_body, (f32(K, CR, CC), f32(DEVICES * 3, 128), f32(16, 128),...  6.86 us
    ppermute x4, starting transfers between devices, neighbours(): lax.ppermute(value, axis, [(i, i + 1) for i in starts] + [(i + 1, i) for...  6.63 us
    pallas_call x1, Pallas kernels, on_device(): call(fields_body, (pltpu.VMEM((K, CR, CC), F32), pltpu.VMEM((K, CR, CC),...  4.63 us
    pallas_call x1, Pallas kernels, on_device(): call(direction_body, f32(K, CR, CC), scratch=[field], specs=[smem] + [vme...  4.63 us
    all_to_all x1, starting transfers between devices, on_device(): lax.all_to_all(message.reshape(DEVICES, 1, 384), AXES, 0, 0, tiled=True)  4.58 us
    all_to_all x1, waiting for transfers between devices, on_device(): lax.all_to_all(message.reshape(DEVICES, 1, 384), AXES, 0, 0, tiled=True)  4.33 us
    pallas_call x1, Pallas kernels, on_device(): call(products_body, (f32(8 * DEVICES, 128), f32(32, CC), f32(32, CC), f32...  2.79 us
  transfers between devices with their start and end apart: 5, of which 1 were waited for; matrix products, arithmetic and copies ran while one was open for 0% of the time, Pallas kernels for 14%

profile of v8, /device:TPU:1, one launch (start us, length us, event | category | flops | bytes accessed | tf_op | source)
XLA Modules:
  0.0 66.2 jit_solution(17513506214328225677)
XLA Ops:
  0.6 0.0 copy-start.2
  0.6 2.8 %shard_map.94 = (f32[40,256]{1,0:T(8,128)S(1)}, f32[40,256]{1,0:T(8,128)S(1)}, f32[128,128]{1,0:T(8,128)S(1)}, f32[16,128,256]{2,1,0:T(8,128)S(1)}, f32[16,128,2...) custom-call(f32[16,128,256]{2,1,0:T(8,128)} %x_ref.1, ...), custom_call_target="tpu_custom_call" | custom-call | bytes 8000000 | tf_op jit(solution)/shard_map/pallas_call | solution.py:445
  3.4 1.5 %collective-permute-start.3 = (f32[128,128]{1,0:T(8,128)S(1)}, f32[128,128]{1,0:T(8,128)S(1)}, u32[]{:S(2)}, u32[]{:S(2)}) collective-permute-start(f32[128,128]{1,0:T(8,128)S(1)} %get-tuple-element.36.cols_ref), channel_id=1, source_target_pairs={{0,1},{2,3},{4,5},{6,7},{1,0},{3,2},{5,4},{7,6},{8,9},{10,11},{12,... | collective-permute-start | bytes 196616 | tf_op jit(solution)/shard_map/ppermute | solution.py:435
  4.9 3.2 %collective-permute-start.1 = (f32[128,128]{1,0:T(8,128)S(1)}, f32[128,128]{1,0:T(8,128)S(1)}, u32[]{:S(2)}, u32[]{:S(2)}) collective-permute-start(f32[128,128]{1,0:T(8,128)S(1)} %get-tuple-element.36.cols_ref), channel_id=1, source_target_pairs={{1,2},{3,4},{5,6},{2,1},{4,3},{6,5},{9,10},{11,12},{13,14},{10,9},... | collective-permute-start | bytes 196616 | tf_op jit(solution)/shard_map/ppermute | solution.py:435
  8.1 1.3 %collective-permute-start.2 = (f32[40,256]{1,0:T(8,128)S(1)}, f32[40,256]{1,0:T(8,128)S(1)}, u32[]{:S(2)}, u32[]{:S(2)}) collective-permute-start(f32[40,256]{1,0:T(8,128)S(1)} %get-tuple-element.34.own_first_ref), channel_id=1, source_target_pairs={{0,8},{16,24},{32,40},{48,56},{64,72},{80,88},{96,104},{112,120},{... | collective-permute-start | bytes 122888 | tf_op jit(solution)/shard_map/ppermute | solution.py:435
  9.4 0.7 collective-permute-start
  10.1 0.0 copy-done.2
  10.1 4.6 %shard_map.95 = (f32[16,128,256]{2,1,0:T(8,128)S(1)}, f32[16,128,256]{2,1,0:T(8,128)S(1)}) custom-call(s32[16]{0:T(128)S(1)} %copy-done.2, f32[16,128,256]{2,1,0:T(8,128)S(1)} %get-tuple-element.27.x_ref, f32[16,128,256]{2,1,0:T(8,128)S(1)} %get-tuple-element.26.d_ref, f32[128,256]{1,0:T(8,128)S(1)} %get-tuple-element.28.ee_s, ...), custom_call_target="tpu_custom_call" | custom-call | bytes 12000000 | tf_op jit(solution)/shard_map/pallas_call | solution.py:477
  14.7 0.0 collective-permute-done.2.far_first_ref
  14.7 0.0 collective-permute-done.far_second_ref
  14.7 0.0 collective-permute-done.3.cols_first_ref
  14.7 0.0 collective-permute-done.1.cols_second_ref
  14.8 2.8 %shard_map.96 = (f32[1024,128]{1,0:T(8,128)S(1)}, f32[32,256]{1,0:T(8,128)S(1)}, f32[32,256]{1,0:T(8,128)S(1)}, f32[128,128]{1,0:T(8,128)S(1)}) custom-call(f32[16,128,256]{2,1,0:T(8,128)S(1)} %get-tuple-element.26.d_ref, f32[16,128,256]{2,1,0:T(8,128)S(1)} %get-tuple-element.32.q_ref, f32[16,128,256]{2,1,0:T(8,128)S(1)} %get-tuple-element.33.r_ref, ...), custom_call_target="tpu_custom_call" | custom-call | bytes 20000000 | tf_op jit(solution)/shard_map/pallas_call | solution.py:485
  17.5 25.4 %all_to_all.16 = f32[128,8,128]{2,1,0:T(8,128)S(1)} all-to-all(f32[128,8,128]{2,1,0:T(8,128)S(1)} %bitcast.6), channel_id=1, replica_groups=mesh['row'=16,'col'=8] {'row','col'}, dimensions={0} | all-to-all | bytes 1048576 | tf_op jit(solution)/shard_map/all_to_all | solution.py:495
  43.0 0.0 copy-start
  43.0 6.9 %shard_map.97 = (f32[16,128,256]{2,1,0:T(8,128)}, f32[384,128]{1,0:T(8,128)}, f32[16,128]{1,0:T(8,128)S(1)}, f32[16,256]{1,0:T(8,128)S(1)}, f32[16,256]{1,0:T(8,128)S(1)}, /*index=5*/f32[128,128]{1,0:T(8,128)S(1)}) custom-call(f32[1024,128]{1,0:T(8,128)S(1)} %bitcast.4, f32[16,128,256]{2,1,0:T(8,128)S(1)} %get-tuple-element.27.x_ref, ...), custom_call_target="tpu_custom_call" | custom-call | bytes 20000000 | tf_op jit(solution)/shard_map/pallas_call | solution.py:497
  49.8 4.6 %all-to-all-start.1 = ((f32[128,1,384]{2,1,0:T(1,128)}), f32[128,1,384]{2,1,0:T(1,128)S(1)}, u32[]{:S(2)}, u32[]{:S(2)}) async-start(f32[128,1,384]{2,1,0:T(1,128)} %bitcast.2), calls=%async_computation.1 | async-start | bytes 393216 | tf_op jit(solution)/shard_map/all_to_all | solution.py:510
  54.4 0.0 copy-done
  54.4 0.0 copy-start.1
  54.4 1.6 %copy-done.1 = f32[16,128,256]{2,1,0:T(8,128)S(1)} copy-done((f32[16,128,256]{2,1,0:T(8,128)S(1)}, f32[16,128,256]{2,1,0:T(8,128)}, u32[]{:S(2)}) %copy-start.1) | copy-done | bytes 2097176
  56.0 4.6 %shard_map.98 = f32[16,128,256]{2,1,0:T(8,128)} custom-call(s32[16]{0:T(128)S(1)} %copy-done.2, f32[16,128,256]{2,1,0:T(8,128)S(1)} %copy-done.1, f32[16,128,256]{2,1,0:T(8,128)S(1)} %copy-done, f32[128,256]{1,0:T(8,128)S(1)} %get-tuple-element.28.ee_s, f32[128,256]{1,0:T(8,128)S(1)} %get-tuple-element.29.es_s, f32[128,256]{1,0:T(8,128)S(1)} %get-tuple-element.30.leak_s, ...), custom_call_target="tpu_custom_call" | custom-call | bytes 20000000 | tf_op jit(solution)/shard_map/pallas_call | solution.py:511
  60.6 4.3 %all-to-all-done.1 = f32[128,1,384]{2,1,0:T(1,128)S(1)} async-done(((f32[128,1,384]{2,1,0:T(1,128)}), f32[128,1,384]{2,1,0:T(1,128)S(1)}, u32[]{:S(2)}, u32[]{:S(2)}) %all-to-all-start.1) | async-done | bytes 196640 | tf_op jit(solution)/shard_map/all_to_all | solution.py:510
  65.0 1.2 %shard_map.99 = f32[16,512]{1,0:T(8,128)} custom-call(f32[384,128]{1,0:T(8,128)S(1)} %bitcast.5), custom_call_target="tpu_custom_call" | custom-call | bytes 1000000 | tf_op jit(solution)/shard_map/pallas_call | solution.py:518
Async XLA Ops:
  0.6 9.4 %copy-start.2 = (s32[16]{0:T(128)S(1)}, s32[16]{0:T(128)}, u32[]{:S(2)}) copy-start(s32[16]{0:T(128)} %src_ref.3) | copy-start | bytes 196
  3.4 11.3 %collective-permute-start.3 = (f32[128,128]{1,0:T(8,128)S(1)}, f32[128,128]{1,0:T(8,128)S(1)}, u32[]{:S(2)}, u32[]{:S(2)}) collective-permute-start(f32[128,128]{1,0:T(8,128)S(1)} %get-tuple-element.36.cols_ref), channel_id=1, source_target_pairs={{0,1},{2,3},{4,5},{6,7},{1,0},{3,2},{5,4},{7,6},{8,9},{10,11},{12,... | collective-permute-start | bytes 196616 | tf_op jit(solution)/shard_map/ppermute | solution.py:435
  4.9 9.8 %collective-permute-start.1 = (f32[128,128]{1,0:T(8,128)S(1)}, f32[128,128]{1,0:T(8,128)S(1)}, u32[]{:S(2)}, u32[]{:S(2)}) collective-permute-start(f32[128,128]{1,0:T(8,128)S(1)} %get-tuple-element.36.cols_ref), channel_id=1, source_target_pairs={{1,2},{3,4},{5,6},{2,1},{4,3},{6,5},{9,10},{11,12},{13,14},{10,9},... | collective-permute-start | bytes 196616 | tf_op jit(solution)/shard_map/ppermute | solution.py:435
  8.1 6.6 %collective-permute-start.2 = (f32[40,256]{1,0:T(8,128)S(1)}, f32[40,256]{1,0:T(8,128)S(1)}, u32[]{:S(2)}, u32[]{:S(2)}) collective-permute-start(f32[40,256]{1,0:T(8,128)S(1)} %get-tuple-element.34.own_first_ref), channel_id=1, source_target_pairs={{0,8},{16,24},{32,40},{48,56},{64,72},{80,88},{96,104},{112,120},{... | collective-permute-start | bytes 122888 | tf_op jit(solution)/shard_map/ppermute | solution.py:435
  9.4 5.3 %collective-permute-start = (f32[40,256]{1,0:T(8,128)S(1)}, f32[40,256]{1,0:T(8,128)S(1)}, u32[]{:S(2)}, u32[]{:S(2)}) collective-permute-start(f32[40,256]{1,0:T(8,128)S(1)} %get-tuple-element.35.own_second_ref), channel_id=1, source_target_pairs={{8,16},{24,32},{40,48},{56,64},{72,80},{88,96},{104,112},{16,8},{3... | collective-permute-start | bytes 122888 | tf_op jit(solution)/shard_map/ppermute | solution.py:435
  43.0 11.5 %copy-start = (f32[16,128,256]{2,1,0:T(8,128)S(1)}, f32[16,128,256]{2,1,0:T(8,128)}, u32[]{:S(2)}) copy-start(f32[16,128,256]{2,1,0:T(8,128)} %d_ref.3) | copy-start | bytes 6291460
  49.8 15.1 %all-to-all-start.1 = ((f32[128,1,384]{2,1,0:T(1,128)}), f32[128,1,384]{2,1,0:T(1,128)S(1)}, u32[]{:S(2)}, u32[]{:S(2)}) async-start(f32[128,1,384]{2,1,0:T(1,128)} %bitcast.2), calls=%async_computation.1 | async-start | bytes 393216 | tf_op jit(solution)/shard_map/all_to_all | solution.py:510
  54.4 1.6 %copy-start.1 = (f32[16,128,256]{2,1,0:T(8,128)S(1)}, f32[16,128,256]{2,1,0:T(8,128)}, u32[]{:S(2)}) copy-start(f32[16,128,256]{2,1,0:T(8,128)} %get-tuple-element.23.xn_ref) | copy-start | bytes 6291460
